TPU v7x, 128 devices: a whole 4x4x4 slice. The times are simulated.
128 devices in a mesh: sec: 4 (over y_lo, core), xy: 32 (over y_hi, z, x).
Axes of the slice: x: 4, y: 4 (y_hi: 2, y_lo: 2; y = y_hi * 2 + y_lo), z: 4, core: 2. Of those that a mesh axis runs over, the one named last changes fastest.
Arguments:
- raw_pieces: bfloat16 [16, 3072, 4096], P('sec', 'xy'), may hold values from -6 to 6
- piece_owner: int32 [16, 3072, 1], P('sec', 'xy'), may hold values from 0 to 31; in each aligned block of 96 rows (0 to 95, 96 to 191, ..., all dimensions but the last counted through in order) at most 6 rows name the same one
- piece_slot: int32 [16, 3072], P('sec', 'xy'), may hold values from 0 to 63
- blend: float32 [16, 3072], P('sec', 'xy'), may hold values from 0.5 to 2
Outputs:
- relaxed_mesh: float32 [15, 2, 64, 32], P(None, None, 'xy', 'sec')
Inputs may be any that keep to these rules, and one draw needn't show every extreme that they name: `piece_owner`: among the pieces of one section held by one index of xy (an aligned block of 96), no block is named more than 6 times.
All inputs are finite; a program needn't handle non-finite values.
Results may differ from a plain program's by a relative error of at most 0.0023.
Values may be sent and summed in bfloat16 or wider, within the bound.
No kernel may reach another device: no remote copies, remote signals or barrier semaphores. Data moves between devices by JAX's collectives and lax.ppermute only.
A program may use at most 128 MiB of HBM per device.

v0:
```python
import math

import jax
import jax.numpy as jnp
from jax import lax
from jax.sharding import PartitionSpec as P

PS = 64
PX_DEV = 2
PY_DEV = 8
ITERS = 8


HIGH = lax.Precision.HIGHEST


def padded_2(block, sides, width):
    for axis, dim in sides:
        count = lax.axis_size(axis)
        forward = [(i, i + 1) for i in range(count - 1)]
        backward = [(target, source) for source, target in forward]
        low = lax.ppermute(
            lax.slice_in_dim(block, block.shape[dim] - width, None, axis=dim), axis, forward
        )
        high = lax.ppermute(lax.slice_in_dim(block, 0, width, axis=dim), axis, backward)
        block = jnp.concatenate([low, block, high], axis=dim)
    return block


def normalize(patch):
    mean = jnp.mean(patch, axis=(-2, -1), keepdims=True)
    centred = patch - mean
    var = jnp.mean(centred * centred, axis=(-2, -1), keepdims=True)
    return centred / jnp.sqrt(var + 1e-05)


def right_mul(data, table):
    return jnp.einsum(
        "sxyjk,kl->sxyjl", data, table, precision=HIGH, preferred_element_type=jnp.float32
    )


def left_mul(table, data):
    return jnp.einsum(
        "jk,sxykl->sxyjl", table, data, precision=HIGH, preferred_element_type=jnp.float32
    )


def relax_step(mesh, target, inside):
    centre = mesh[:, :, 1:-1, 1:-1]
    lap = (
        mesh[:, :, 2:, 1:-1]
        + mesh[:, :, :-2, 1:-1]
        + mesh[:, :, 1:-1, 2:]
        + mesh[:, :, 1:-1, :-2]
        - 4.0 * centre
    )
    return (centre + 0.2 * (target - centre + lap)) * inside


def pair_flow(patches):
    grid_index = jnp.arange(PS, dtype=jnp.int32)
    product = grid_index[:, None] * grid_index[None, :] % PS
    angle = product.astype(jnp.float32) * (2.0 * math.pi / PS)
    cos_table = jnp.cos(angle)
    sin_table = -jnp.sin(angle)
    half_real = right_mul(patches, cos_table)
    half_imag = right_mul(patches, sin_table)
    spec_real = left_mul(cos_table, half_real) - left_mul(sin_table, half_imag)
    spec_imag = left_mul(cos_table, half_imag) + left_mul(sin_table, half_real)
    cross_real = spec_real[:-1] * spec_real[1:] + spec_imag[:-1] * spec_imag[1:]
    cross_imag = spec_real[:-1] * spec_imag[1:] - spec_imag[:-1] * spec_real[1:]
    back_real = right_mul(cross_real, cos_table) + right_mul(cross_imag, sin_table)
    back_imag = right_mul(cross_imag, cos_table) - right_mul(cross_real, sin_table)
    corr = (left_mul(cos_table, back_real) + left_mul(sin_table, back_imag)) / float(
        PS * PS * PS * PS
    )
    shifts = ((jnp.arange(PS) + PS // 2) % PS - PS // 2).astype(jnp.float32)
    power = corr * corr
    total = jnp.maximum(jnp.sum(power, axis=(-2, -1)), 0.5)
    along_x = jnp.sum(power * shifts[:, None], axis=(-2, -1)) / total
    along_y = jnp.sum(power * shifts[None, :], axis=(-2, -1)) / total
    return jnp.stack([along_x, along_y], axis=1)


def local(raw_pieces, piece_owner, piece_slot, blend):
    sec_dev, pieces, flat = raw_pieces.shape
    n_xy = lax.axis_size("xy")
    n_sec = lax.axis_size("sec")
    cap = max(2, (2 * pieces + n_xy - 1) // n_xy)
    block = PX_DEV * PY_DEV * n_sec
    warped = (raw_pieces.astype(jnp.float32) * blend[:, :, None]).astype(jnp.bfloat16)
    owner = piece_owner[:, :, 0]
    onehot = (owner[:, :, None] == jnp.arange(n_xy, dtype=jnp.int32)[None, None, :]).astype(
        jnp.int32
    )
    before = jnp.cumsum(onehot, axis=1) - onehot
    rank = jnp.sum(onehot * before, axis=-1)
    target_row = owner * cap + rank
    select = target_row[:, None, :] == jnp.arange(n_xy * cap, dtype=jnp.int32)[None, :, None]
    outgoing = jnp.einsum(
        "sqp,spk->sqk", select.astype(jnp.bfloat16), warped, preferred_element_type=jnp.float32
    ).astype(jnp.bfloat16)
    sent_slot = jnp.sum(jnp.where(select, piece_slot[:, None, :] + 1, 0), axis=-1) - 1
    arrived_list = []
    slot_list = []
    for index in range(sec_dev):
        got, got_slot = (
            lax.all_to_all(
                outgoing[index : index + 1], "xy", split_axis=1, concat_axis=1, tiled=True
            ),
            lax.all_to_all(
                sent_slot[index : index + 1], "xy", split_axis=1, concat_axis=1, tiled=True
            ),
        )
        arrived_list.append(got)
        slot_list.append(got_slot)
    arrived = jnp.concatenate(arrived_list, axis=0)
    arrived_slot = jnp.concatenate(slot_list, axis=0)
    placing = arrived_slot[:, None, :] == jnp.arange(block, dtype=jnp.int32)[None, :, None]
    stitched = jnp.einsum(
        "srq,sqk->srk", placing.astype(jnp.bfloat16), arrived, preferred_element_type=jnp.float32
    ).astype(jnp.bfloat16)
    arranged = stitched.reshape(sec_dev, PX_DEV, n_sec, PY_DEV, flat)
    all_sections = sec_dev * n_sec
    columns = lax.all_to_all(arranged, "sec", split_axis=2, concat_axis=0, tiled=True)
    patches = normalize(columns.reshape(all_sections, PX_DEV, PY_DEV, PS, PS).astype(jnp.float32))
    flow = pair_flow(patches)
    mesh = flow
    ones_grid = jnp.ones_like(flow)
    for step in range(ITERS):
        padded = padded_2(mesh, (("sec", 3), ("xy", 2)), 1)
        mesh = relax_step(padded, flow, ones_grid)
    return mesh


def solution(mesh):
    in_specs = (P("sec", "xy", None), P("sec", "xy", None), P("sec", "xy"), P("sec", "xy"))
    out_specs = P(None, None, "xy", "sec")
    return jax.shard_map(local, mesh=mesh, in_specs=in_specs, out_specs=out_specs, check_vma=False)
```

profile of v0, /device:TPU:17, one launch (start us, length us, event | category | flops | bytes accessed | tf_op | source)
XLA Modules:
  0.0 652.7 jit_solution(3736369986173872862)
XLA Ops:
  3.6 10.3 %all-to-all-start = ((s32[1,32,6]{2,0,1:T(1,128)}), s32[1,32,6]{2,0,1:T(1,128)S(1)}, u32[]{:S(2)}, u32[]{:S(2)}) async-start(s32[1,32,6]{2,0,1:T(1,128)} %bitcast.1), calls=%async_computation | async-start | bytes 32768 | tf_op jit(solution)/shard_map/all_to_all | solution.py:112
  45.9 9.5 %all-to-all-start.3 = ((s32[1,32,6]{2,0,1:T(1,128)}), s32[1,32,6]{2,0,1:T(1,128)S(1)}, u32[]{:S(2)}, u32[]{:S(2)}) async-start(s32[1,32,6]{2,0,1:T(1,128)} %bitcast.4), calls=%async_computation.3 | async-start | bytes 32768 | tf_op jit(solution)/shard_map/all_to_all | solution.py:112
  64.6 11.7 %reduce.37 = bf16[192,4096]{1,0:T(8,128)(2,1)} reduce(bf16[192,1,4096]{2,1,0:T(2,128)(2,1)S(1)} %bitcast.101, bf16[]{:T(256)} %broadcast.240), dimensions={1}, to_apply=%bitcast.98.reduce_sub_computation | reduce | bytes 3145730
  80.9 9.3 %all-to-all-start.4 = ((bf16[32,2,12288]{2,1,0:T(2,128)(2,1)}), bf16[32,2,12288]{2,1,0:T(2,128)(2,1)}, u32[]{:S(2)}, u32[]{:S(2)}) async-start(bf16[32,2,12288]{2,1,0:T(2,128)(2,1)} %reshape.185), calls=%async_computation.4 | async-start | bytes 3145728 | tf_op jit(solution)/shard_map/all_to_all | solution.py:109
  95.2 11.5 %reduce.36 = bf16[192,4096]{1,0:T(8,128)(2,1)} reduce(bf16[192,1,4096]{2,1,0:T(2,128)(2,1)S(1)} %bitcast.103, bf16[]{:T(256)} %broadcast.240), dimensions={1}, to_apply=%bitcast.97.reduce_sub_computation | reduce | bytes 3145730
  111.3 9.3 %all-to-all-start.5 = ((bf16[32,2,12288]{2,1,0:T(2,128)(2,1)}), bf16[32,2,12288]{2,1,0:T(2,128)(2,1)}, u32[]{:S(2)}, u32[]{:S(2)}) async-start(bf16[32,2,12288]{2,1,0:T(2,128)(2,1)} %reshape.183), calls=%async_computation.5 | async-start | bytes 3145728 | tf_op jit(solution)/shard_map/all_to_all | solution.py:109
  125.7 11.8 %reduce.35 = bf16[192,4096]{1,0:T(8,128)(2,1)} reduce(bf16[192,1,4096]{2,1,0:T(2,128)(2,1)S(1)} %bitcast.104, bf16[]{:T(256)} %broadcast.240), dimensions={1}, to_apply=%bitcast.96.reduce_sub_computation | reduce | bytes 3145730
  142.0 9.3 %all-to-all-start.6 = ((bf16[32,2,12288]{2,1,0:T(2,128)(2,1)}), bf16[32,2,12288]{2,1,0:T(2,128)(2,1)}, u32[]{:S(2)}, u32[]{:S(2)}) async-start(bf16[32,2,12288]{2,1,0:T(2,128)(2,1)} %reshape.181), calls=%async_computation.6 | async-start | bytes 3145728 | tf_op jit(solution)/shard_map/all_to_all | solution.py:109
  156.4 11.5 %reduce.34 = bf16[192,4096]{1,0:T(8,128)(2,1)} reduce(bf16[192,1,4096]{2,1,0:T(2,128)(2,1)S(1)} %bitcast.102, bf16[]{:T(256)} %broadcast.240), dimensions={1}, to_apply=%bitcast.95.reduce_sub_computation | reduce | bytes 3145730
  172.4 9.3 %all-to-all-start.7 = ((bf16[32,2,12288]{2,1,0:T(2,128)(2,1)}), bf16[32,2,12288]{2,1,0:T(2,128)(2,1)}, u32[]{:S(2)}, u32[]{:S(2)}) async-start(bf16[32,2,12288]{2,1,0:T(2,128)(2,1)} %reshape.179), calls=%async_computation.7 | async-start | bytes 3145728 | tf_op jit(solution)/shard_map/all_to_all | solution.py:109
  233.3 10.2 %all-to-all-start.8 = ((bf16[4,2,4,8,4096]{4,3,1,0,2:T(8,128)(2,1)}), bf16[4,2,4,8,4096]{4,3,1,0,2:T(8,128)(2,1)S(1)}, u32[]{:S(2)}, u32[]{:S(2)}) async-start(bf16[4,2,4,8,4096]{4,3,1,0,2:T(8,128)(2,1)} %copy.31), calls=%async_computation.8 | async-start | bytes 4194304 | tf_op jit(solution)/shard_map/all_to_all | solution.py:126
  243.4 24.8 %all-to-all-done.8 = bf16[4,2,4,8,4096]{4,3,1,0,2:T(8,128)(2,1)S(1)} async-done(((bf16[4,2,4,8,4096]{4,3,1,0,2:T(8,128)(2,1)}), bf16[4,2,4,8,4096]{4,3,1,0,2:T(8,128)(2,1)S(1)}, u32[]{:S(2)}, u32[]{:S(2)}) %all-to-all-start.8) | async-done | bytes 2097184 | tf_op jit(solution)/shard_map/all_to_all | solution.py:126
  279.7 27.7 %fusion.19 = f32[16,2,8,64,64]{3,4,2,1,0:T(8,128)S(1)} fusion(f32[16,2,8,64,64]{4,3,2,1,0:T(8,128)} %reshape.124, f32[16,2,8]{2,1,0:T(2,128)S(1)} %bitcast.115, f32[16,2,8]{2,1,0:T(2,128)S(1)} %bitcast.110), kind=kOutput, calls=%fused_computation.30 | convolution fusion | flops 807460864 | bytes 8390656 | tf_op jit(solution)/shard_map/sxyjk,kl->sxyjl/dot_general | solution.py:38
  307.4 24.6 %fusion.18 = f32[16,2,8,64,64]{3,4,2,1,0:T(8,128)S(1)} fusion(f32[16,2,8,64,64]{4,3,2,1,0:T(8,128)S(1)} %copy-done.1, f32[16,2,8]{2,1,0:T(2,128)S(1)} %bitcast.116, f32[16,2,8]{2,1,0:T(2,128)S(1)} %bitcast.111), kind=kOutput, calls=%fused_computation.29 | convolution fusion | flops 807464960 | bytes 8390656 | tf_op jit(solution)/shard_map/sxyjk,kl->sxyjl/dot_general | solution.py:38
  341.1 10.3 %fusion.42 = f32[16,2,8,64,64]{4,3,2,1,0:T(8,128)S(1)} fusion(f32[16,2,8,64,64]{3,4,2,1,0:T(8,128)S(1)} %fusion.18), kind=kOutput, calls=%fused_computation.59 | convolution fusion | flops 805363712 | bytes 8388608 | tf_op jit(solution)/shard_map/jk,sxykl->sxyjl/dot_general | solution.py:44
  351.4 11.5 %subtract_bitcast_fusion = f32[16,2,8,64,64]{3,4,2,1,0:T(8,128)} fusion(f32[16,2,8,64,64]{4,3,2,1,0:T(8,128)} %fusion.44, f32[16,2,8,64,64]{3,4,2,1,0:T(8,128)S(1)} %fusion.18), kind=kOutput, calls=%fused_computation.1 | convolution fusion | flops 806416384 | bytes 12582912 | tf_op jit(solution)/shard_map/jk,sxykl->sxyjl/dot_general | solution.py:44
  362.9 9.2 %add_bitcast_fusion = f32[16,2,8,64,64]{3,4,2,1,0:T(8,128)} fusion(f32[16,2,8,64,64]{4,3,2,1,0:T(8,128)S(1)} %fusion.42, f32[16,2,8,64,64]{3,4,2,1,0:T(8,128)S(1)} %fusion.19), kind=kOutput, calls=%fused_computation | convolution fusion | flops 806416384 | bytes 12582912 | tf_op jit(solution)/shard_map/jk,sxykl->sxyjl/dot_general | solution.py:44
  372.1 15.8 %multiply_add_fusion = (f32[15,2,8,64,64]{3,4,2,1,0:T(8,128)S(1)}, f32[15,2,8,64,64]{3,4,2,1,0:T(8,128)}) fusion(f32[16,2,8,64,64]{3,4,2,1,0:T(8,128)} %add_bitcast_fusion, f32[16,2,8,64,64]{3,4,2,1,0:T(8,128)} %subtract_bitcast_fusion), kind=kLoop, calls=%fused_computation.14 | loop fusion | flops 5898240 | bytes 23592960 | tf_op jit(solution)/shard_map/add | solution.py:71
  387.8 15.4 %fusion.37 = f32[15,2,8,64,64]{4,3,2,1,0:T(8,128)S(1)} fusion(f32[15,2,8,64,64]{3,4,2,1,0:T(8,128)} %get-tuple-element.13), kind=kOutput, calls=%fused_computation.54 | convolution fusion | flops 755032064 | bytes 7864320 | tf_op jit(solution)/shard_map/sxyjk,kl->sxyjl/dot_general | solution.py:38
  403.3 13.4 %fusion.32 = f32[15,2,8,64,64]{4,3,2,1,0:T(8,128)S(1)} fusion(f32[15,2,8,64,64]{3,4,2,1,0:T(8,128)S(1)} %bitcast.100), kind=kOutput, calls=%fused_computation.49 | convolution fusion | flops 755036160 | bytes 7864320 | tf_op jit(solution)/shard_map/sxyjk,kl->sxyjl/dot_general | solution.py:38
  416.7 14.9 %fusion.30 = f32[15,2,8,64,64]{4,3,2,1,0:T(8,128)} fusion(f32[15,2,8,64,64]{3,4,2,1,0:T(8,128)S(1)} %get-tuple-element.12), kind=kOutput, calls=%fused_computation.47 | convolution fusion | flops 755036160 | bytes 7864320 | tf_op jit(solution)/shard_map/sxyjk,kl->sxyjl/dot_general | solution.py:38
  431.6 15.1 %fusion.40 = f32[15,2,8,64,64]{4,3,2,1,0:T(8,128)} fusion(f32[15,2,8,64,64]{3,4,2,1,0:T(8,128)S(1)} %get-tuple-element.12), kind=kOutput, calls=%fused_computation.57 | convolution fusion | flops 755032064 | bytes 7864320 | tf_op jit(solution)/shard_map/sxyjk,kl->sxyjl/dot_general | solution.py:38
  446.7 15.6 %fusion.2 = f32[15,2,8,64,64]{4,3,2,1,0:T(8,128)S(1)} fusion(f32[15,2,8,64,64]{4,3,2,1,0:T(8,128)S(1)} %fusion.37, f32[15,2,8,64,64]{4,3,2,1,0:T(8,128)} %fusion.30), kind=kOutput, calls=%fused_computation.9 | convolution fusion | flops 756019200 | bytes 11796480 | tf_op jit(solution)/shard_map/jk,sxykl->sxyjl/dot_general | solution.py:44
  462.4 15.9 %fusion = (f32[15,2,8]{2,1,0:T(2,128)S(1)}, f32[15,2,8]{2,1,0:T(2,128)S(1)}, f32[15,2,8]{2,1,0:T(2,128)S(1)}) fusion(f32[64]{0:T(128)S(1)} %fusion.100, f32[15,2,8,64,64]{4,3,2,1,0:T(8,128)S(1)} %fusion.2, f32[15,2,8,64,64]{4,3,2,1,0:T(8,128)S(1)} %copy-done, f32[15,2,8,64,64]{4,3,2,1,0:T(8,128)S(1)} %fusion.32), kind=kOutput, calls=%fused_computation.6 | convolution fusion | flops 763878720 | bytes 11799616 | tf_op jit(solution)/shard_map/jk,sxykl->sxyjl/dot_general | solution.py:44
  (167 shorter events, 323.6 us)
Async XLA Ops:
  3.6 16.5 %all-to-all-start = ((s32[1,32,6]{2,0,1:T(1,128)}), s32[1,32,6]{2,0,1:T(1,128)S(1)}, u32[]{:S(2)}, u32[]{:S(2)}) async-start(s32[1,32,6]{2,0,1:T(1,128)} %bitcast.1), calls=%async_computation | async-start | bytes 32768 | tf_op jit(solution)/shard_map/all_to_all | solution.py:112
  20.1 12.4 %all-to-all-start.1 = ((s32[1,32,6]{2,0,1:T(1,128)}), s32[1,32,6]{2,0,1:T(1,128)S(1)}, u32[]{:S(2)}, u32[]{:S(2)}) async-start(s32[1,32,6]{2,0,1:T(1,128)} %bitcast.2), calls=%async_computation.1 | async-start | bytes 32768 | tf_op jit(solution)/shard_map/all_to_all | solution.py:112
  32.5 13.3 %all-to-all-start.2 = ((s32[1,32,6]{2,0,1:T(1,128)}), s32[1,32,6]{2,0,1:T(1,128)S(1)}, u32[]{:S(2)}, u32[]{:S(2)}) async-start(s32[1,32,6]{2,0,1:T(1,128)} %bitcast.3), calls=%async_computation.2 | async-start | bytes 32768 | tf_op jit(solution)/shard_map/all_to_all | solution.py:112
  45.9 35.0 %all-to-all-start.3 = ((s32[1,32,6]{2,0,1:T(1,128)}), s32[1,32,6]{2,0,1:T(1,128)S(1)}, u32[]{:S(2)}, u32[]{:S(2)}) async-start(s32[1,32,6]{2,0,1:T(1,128)} %bitcast.4), calls=%async_computation.3 | async-start | bytes 32768 | tf_op jit(solution)/shard_map/all_to_all | solution.py:112
  80.9 30.4 %all-to-all-start.4 = ((bf16[32,2,12288]{2,1,0:T(2,128)(2,1)}), bf16[32,2,12288]{2,1,0:T(2,128)(2,1)}, u32[]{:S(2)}, u32[]{:S(2)}) async-start(bf16[32,2,12288]{2,1,0:T(2,128)(2,1)} %reshape.185), calls=%async_computation.4 | async-start | bytes 3145728 | tf_op jit(solution)/shard_map/all_to_all | solution.py:109
  111.3 30.7 %all-to-all-start.5 = ((bf16[32,2,12288]{2,1,0:T(2,128)(2,1)}), bf16[32,2,12288]{2,1,0:T(2,128)(2,1)}, u32[]{:S(2)}, u32[]{:S(2)}) async-start(bf16[32,2,12288]{2,1,0:T(2,128)(2,1)} %reshape.183), calls=%async_computation.5 | async-start | bytes 3145728 | tf_op jit(solution)/shard_map/all_to_all | solution.py:109
  142.0 30.4 %all-to-all-start.6 = ((bf16[32,2,12288]{2,1,0:T(2,128)(2,1)}), bf16[32,2,12288]{2,1,0:T(2,128)(2,1)}, u32[]{:S(2)}, u32[]{:S(2)}) async-start(bf16[32,2,12288]{2,1,0:T(2,128)(2,1)} %reshape.181), calls=%async_computation.6 | async-start | bytes 3145728 | tf_op jit(solution)/shard_map/all_to_all | solution.py:109
  172.4 46.3 %all-to-all-start.7 = ((bf16[32,2,12288]{2,1,0:T(2,128)(2,1)}), bf16[32,2,12288]{2,1,0:T(2,128)(2,1)}, u32[]{:S(2)}, u32[]{:S(2)}) async-start(bf16[32,2,12288]{2,1,0:T(2,128)(2,1)} %reshape.179), calls=%async_computation.7 | async-start | bytes 3145728 | tf_op jit(solution)/shard_map/all_to_all | solution.py:109
  233.3 35.0 %all-to-all-start.8 = ((bf16[4,2,4,8,4096]{4,3,1,0,2:T(8,128)(2,1)}), bf16[4,2,4,8,4096]{4,3,1,0,2:T(8,128)(2,1)S(1)}, u32[]{:S(2)}, u32[]{:S(2)}) async-start(bf16[4,2,4,8,4096]{4,3,1,0,2:T(8,128)(2,1)} %copy.31), calls=%async_computation.8 | async-start | bytes 4194304 | tf_op jit(solution)/shard_map/all_to_all | solution.py:126
  486.6 8.3 %collective-permute-start.2 = (f32[15,2,1,10]{3,2,0,1:T(1,128)S(1)}, f32[15,2,1,10]{3,2,0,1:T(1,128)S(1)}, u32[]{:S(2)}, u32[]{:S(2)}) collective-permute-start(f32[15,2,1,10]{3,2,0,1:T(1,128)S(1)} %get-tuple-element.46), channel_id=1, source_target_pairs={{1,0},{2,1},{3,2},{4,3},{5,4},{6,5},{7,6},{8,7},{9,8},{10,9},{11,1... | collective-permute-start | bytes 3608 | tf_op jit(solution)/shard_map/ppermute | solution.py:25
  493.0 10.2 %collective-permute-start.3 = (f32[15,2,1,10]{3,2,0,1:T(1,128)S(1)}, f32[15,2,1,10]{3,2,0,1:T(1,128)S(1)}, u32[]{:S(2)}, u32[]{:S(2)}) collective-permute-start(f32[15,2,1,10]{3,2,0,1:T(1,128)S(1)} %get-tuple-element.47), channel_id=1, source_target_pairs={{0,1},{1,2},{2,3},{3,4},{4,5},{5,6},{6,7},{7,8},{8,9},{9,10},{10,1... | collective-permute-start | bytes 3608 | tf_op jit(solution)/shard_map/ppermute | solution.py:22
  503.6 5.9 collective-permute-start.4
  513.0 5.3 collective-permute-start.6
  514.9 10.2 %collective-permute-start.7 = (f32[15,2,1,10]{3,2,0,1:T(1,128)S(1)}, f32[15,2,1,10]{3,2,0,1:T(1,128)S(1)}, u32[]{:S(2)}, u32[]{:S(2)}) collective-permute-start(f32[15,2,1,10]{3,2,0,1:T(1,128)S(1)} %get-tuple-element.43), channel_id=1, source_target_pairs={{0,1},{1,2},{2,3},{3,4},{4,5},{5,6},{6,7},{7,8},{8,9},{9,10},{10,1... | collective-permute-start | bytes 3608 | tf_op jit(solution)/shard_map/ppermute | solution.py:22
  534.0 5.3 collective-permute-start.10
  536.0 10.2 %collective-permute-start.11 = (f32[15,2,1,10]{3,2,0,1:T(1,128)S(1)}, f32[15,2,1,10]{3,2,0,1:T(1,128)S(1)}, u32[]{:S(2)}, u32[]{:S(2)}) collective-permute-start(f32[15,2,1,10]{3,2,0,1:T(1,128)S(1)} %get-tuple-element.39), channel_id=1, source_target_pairs={{0,1},{1,2},{2,3},{3,4},{4,5},{5,6},{6,7},{7,8},{8,9},{9,10},{10,1... | collective-permute-start | bytes 3608 | tf_op jit(solution)/shard_map/ppermute | solution.py:22
  555.1 5.3 collective-permute-start.14
  557.0 10.2 %collective-permute-start.15 = (f32[15,2,1,10]{3,2,0,1:T(1,128)S(1)}, f32[15,2,1,10]{3,2,0,1:T(1,128)S(1)}, u32[]{:S(2)}, u32[]{:S(2)}) collective-permute-start(f32[15,2,1,10]{3,2,0,1:T(1,128)S(1)} %get-tuple-element.35), channel_id=1, source_target_pairs={{0,1},{1,2},{2,3},{3,4},{4,5},{5,6},{6,7},{7,8},{8,9},{9,10},{10,1... | collective-permute-start | bytes 3608 | tf_op jit(solution)/shard_map/ppermute | solution.py:22
  576.1 5.3 collective-permute-start.18
  578.0 10.2 %collective-permute-start.19 = (f32[15,2,1,10]{3,2,0,1:T(1,128)S(1)}, f32[15,2,1,10]{3,2,0,1:T(1,128)S(1)}, u32[]{:S(2)}, u32[]{:S(2)}) collective-permute-start(f32[15,2,1,10]{3,2,0,1:T(1,128)S(1)} %get-tuple-element.31), channel_id=1, source_target_pairs={{0,1},{1,2},{2,3},{3,4},{4,5},{5,6},{6,7},{7,8},{8,9},{9,10},{10,1... | collective-permute-start | bytes 3608 | tf_op jit(solution)/shard_map/ppermute | solution.py:22
  597.1 5.3 collective-permute-start.22
  599.1 10.2 %collective-permute-start.23 = (f32[15,2,1,10]{3,2,0,1:T(1,128)S(1)}, f32[15,2,1,10]{3,2,0,1:T(1,128)S(1)}, u32[]{:S(2)}, u32[]{:S(2)}) collective-permute-start(f32[15,2,1,10]{3,2,0,1:T(1,128)S(1)} %get-tuple-element.27), channel_id=1, source_target_pairs={{0,1},{1,2},{2,3},{3,4},{4,5},{5,6},{6,7},{7,8},{8,9},{9,10},{10,1... | collective-permute-start | bytes 3608 | tf_op jit(solution)/shard_map/ppermute | solution.py:22
  620.1 10.2 %collective-permute-start.27 = (f32[15,2,1,10]{3,2,0,1:T(1,128)S(1)}, f32[15,2,1,10]{3,2,0,1:T(1,128)S(1)}, u32[]{:S(2)}, u32[]{:S(2)}) collective-permute-start(f32[15,2,1,10]{3,2,0,1:T(1,128)S(1)} %get-tuple-element.23), channel_id=1, source_target_pairs={{0,1},{1,2},{2,3},{3,4},{4,5},{5,6},{6,7},{7,8},{8,9},{9,10},{10,1... | collective-permute-start | bytes 3608 | tf_op jit(solution)/shard_map/ppermute | solution.py:22
  641.2 10.2 %collective-permute-start.31 = (f32[15,2,1,10]{3,2,0,1:T(1,128)S(1)}, f32[15,2,1,10]{3,2,0,1:T(1,128)S(1)}, u32[]{:S(2)}, u32[]{:S(2)}) collective-permute-start(f32[15,2,1,10]{3,2,0,1:T(1,128)S(1)} %get-tuple-element.19), channel_id=1, source_target_pairs={{0,1},{1,2},{2,3},{3,4},{4,5},{5,6},{6,7},{7,8},{8,9},{9,10},{10,1... | collective-permute-start | bytes 3608 | tf_op jit(solution)/shard_map/ppermute | solution.py:22
  (21 other events, 161.2 us)
where the time goes:
time: 659 us; the launch traced here: 653 us
  matrix products  192 us (29%)
  starting transfers between devices  165 us (25%)
  waiting for transfers between devices  118 us (18%)
  local copies, waits for them, and re-layouts  100 us (15%)
  other arithmetic  75.5 us (11%)
    dot_general x6, matrix products, right_mul(): jnp.einsum('sxyjk,kl->sxyjl', data, table, precision=HIGH, preferred_elem...  111 us
    dot_general x6, matrix products, left_mul(): jnp.einsum('jk,sxykl->sxyjl', table, data, precision=HIGH, preferred_elem...  71.6 us
    ppermute x16, waiting for transfers between devices, padded_2(): lax.ppermute(lax.slice_in_dim(block, block.shape[dim] - width, None, axis...  56 us
    unnamed x17, local copies, waits for them, and re-layouts  51.7 us
    ppermute x16, starting transfers between devices, padded_2(): lax.ppermute(lax.slice_in_dim(block, block.shape[dim] - width, None, axis...  50.5 us
    unnamed x5, other arithmetic  46.5 us
    all_to_all x4, starting transfers between devices, local(): lax.all_to_all(outgoing[index:index + 1], 'xy', split_axis=1, concat_axis...  37.3 us
    ppermute x16, starting transfers between devices, padded_2(): lax.ppermute(lax.slice_in_dim(block, 0, width, axis=dim), axis, backward)  35.2 us
  transfers between devices with their start and end apart: 41, of which 19 were waited for; matrix products, arithmetic and copies ran while one was open for 20% of the time, Pallas kernels for 0%

commit v1 on v0

v1 whole, which is shorter than its diff:
```python
import functools
import math

import jax
import jax.numpy as jnp
import numpy as np
from jax import lax
from jax.experimental import pallas as pl
from jax.experimental.pallas import tpu as pltpu
from jax.sharding import PartitionSpec as P

PS = 64
FLAT = PS * PS
CAP = 6
N_SEC = 4
N_XY = 32
SEC_DEV = 4
PIECES = 96
BLOCK = 64
ITERS = 8
ROWS_IN = SEC_DEV * PIECES
CHUNK = SEC_DEV * CAP
ROWS_OUT = N_XY * CHUNK
SLOT_LANES = 128
WIDTH = FLAT + SLOT_LANES
PATCHES = SEC_DEV * BLOCK
TILE = 256
TILES = FLAT // TILE
GYW = 24
F32 = jnp.float32
BF16 = jnp.bfloat16
VMEM_LIMIT = 56 * 1024 * 1024

NT = (((1,), (1,)), ((), ()))
NN = (((1,), (0,)), ((), ()))


def real_basis(kind):
    pos = np.arange(PS)
    rows = {}
    for k in range(32):
        angle = 2.0 * math.pi * ((k * pos) % PS) / PS
        rows[k, 0] = np.cos(angle)
        rows[k, 1] = np.sin(angle) if k else np.cos(math.pi * pos)
    if kind == "forward":
        for (k, part), row in rows.items():
            rows[k, part] = row * (math.sqrt(2.0) if k else 1.0) / 8.0
    x_order = np.stack([rows[k, part] for part in range(2) for k in range(32)])
    y_order = np.stack([rows[k, part] for k in range(32) for part in range(2)])
    return x_order, y_order


def split_table(table):
    high = table.astype(jnp.bfloat16)
    low = (table - high.astype(np.float64)).astype(jnp.bfloat16)
    return np.concatenate([high, low], axis=0)


def tables():
    fwd_x, fwd_y = real_basis("forward")
    inv_x, inv_y = real_basis("inverse")
    eye = np.eye(4)
    first = np.einsum("ab,ky->kaby", eye, fwd_y).reshape(256, 256)
    second = np.einsum("ab,ktx->aktbx", eye, fwd_x.reshape(64, 16, 4)).reshape(256, 256)
    third = np.einsum("ab,kd->dabk", eye, inv_x).reshape(256, 256)
    fourth = np.einsum("ab,qkd->adqbk", eye, inv_y.reshape(16, 4, 64)).reshape(256, 256)
    return [split_table(t) for t in (first, second, third, fourth)]


def mm(a, b, dims=NN):
    return lax.dot_general(a, b, dims, preferred_element_type=F32)


def split(value):
    high = value.astype(BF16)
    return high, (value - high.astype(F32)).astype(BF16)


def mm3(table, high, low):
    both = mm(table, high)
    return both[:256] + both[256:] + mm(table[:256], low)


def send_kernel(meta_ref, raw_ref, out_ref, select, blend, warped):
    step = pl.program_id(0)

    @pl.when(step == 0)
    def _():
        key = meta_ref[0:1, :]
        column = jnp.broadcast_to(key, (128, ROWS_IN)).T
        column = jnp.concatenate([column] * 3, axis=1)
        before = lax.broadcasted_iota(jnp.int32, (ROWS_IN, ROWS_IN), 0) < lax.broadcasted_iota(
            jnp.int32, (ROWS_IN, ROWS_IN), 1
        )
        same = jnp.where((column == key) & before, 1.0, 0.0)
        rank = jnp.sum(same, axis=0, keepdims=True)
        target = (meta_ref[1:2, :] + rank).astype(jnp.int32)
        rows = lax.broadcasted_iota(jnp.int32, (ROWS_OUT, ROWS_IN), 0)
        select[...] = jnp.where(rows == target, 1.0, 0.0).astype(BF16)
        blend[...] = jnp.broadcast_to(meta_ref[2:3, :], (128, ROWS_IN)).T

    part = out_ref.shape[1]
    scale = blend[...]
    for lane in range(0, part, 128):
        warped[:, lane : lane + 128] = (
            raw_ref[:, lane : lane + 128].astype(F32) * scale
        ).astype(BF16)

    @pl.when(step == pl.num_programs(0) - 1)
    def _():
        slot = jnp.broadcast_to(meta_ref[3:4, :], (128, ROWS_IN)).T
        warped[:, part - 128 :] = slot.astype(BF16)

    out_ref[...] = mm(select[...], warped[...]).astype(BF16)


def send_rows(meta, raw):
    part = WIDTH // 3
    return pl.pallas_call(
        send_kernel,
        grid=(3,),
        out_shape=jax.ShapeDtypeStruct((ROWS_OUT, WIDTH), BF16),
        in_specs=[
            pl.BlockSpec((8, ROWS_IN), lambda i: (0, 0)),
            pl.BlockSpec((ROWS_IN, part), lambda i: (0, i)),
        ],
        out_specs=pl.BlockSpec((ROWS_OUT, part), lambda i: (0, i)),
        scratch_shapes=[
            pltpu.VMEM((ROWS_OUT, ROWS_IN), BF16),
            pltpu.VMEM((ROWS_IN, 128), F32),
            pltpu.VMEM((ROWS_IN, part), BF16),
        ],
        compiler_params=pltpu.CompilerParams(vmem_limit_bytes=VMEM_LIMIT),
    )(meta, raw)


def stitch_kernel(slot_ref, rows_ref, table_ref, first_ref, high_ref, low_ref, place):
    @pl.when(pl.program_id(0) == 0)
    def _():
        ids = slot_ref[...].astype(F32).T
        wanted = lax.broadcasted_iota(jnp.int32, (PATCHES, ROWS_OUT), 0).astype(F32) + 1.0
        place[...] = jnp.where(jnp.concatenate([ids, ids], axis=0) == wanted, 1.0, 0.0).astype(BF16)

    patches = mm(place[...], rows_ref[...]).astype(BF16)
    first_ref[...] = patches[:BLOCK]
    both = mm(table_ref[...], patches, NT)
    high, low = split(both[:256] + both[256:])
    high_ref[0] = high
    low_ref[0] = low


def stitch(rows, table):
    half = jax.ShapeDtypeStruct((TILES, 256, PATCHES), BF16)
    return pl.pallas_call(
        stitch_kernel,
        grid=(TILES,),
        out_shape=[jax.ShapeDtypeStruct((BLOCK, FLAT), BF16), half, half],
        in_specs=[
            pl.BlockSpec((ROWS_OUT, SLOT_LANES), lambda t: (0, FLAT // SLOT_LANES)),
            pl.BlockSpec((ROWS_OUT, TILE), lambda t: (0, t)),
            pl.BlockSpec((512, 256), lambda t: (0, 0)),
        ],
        out_specs=[
            pl.BlockSpec((BLOCK, TILE), lambda t: (0, t)),
            pl.BlockSpec((1, 256, PATCHES), lambda t: (t, 0, 0)),
            pl.BlockSpec((1, 256, PATCHES), lambda t: (t, 0, 0)),
        ],
        scratch_shapes=[pltpu.VMEM((PATCHES, ROWS_OUT), BF16)],
        compiler_params=pltpu.CompilerParams(vmem_limit_bytes=VMEM_LIMIT),
        cost_estimate=pl.CostEstimate(
            flops=2 * TILES * 256 * 256 * 5 * 256, bytes_accessed=12 << 20, transcendentals=0
        ),
    )(rows, rows, table)


def second_kernel(high_ref, low_ref, table_ref, out_ref):
    high = high_ref[...].reshape(256, PATCHES)
    low = low_ref[...].reshape(256, PATCHES)
    out_ref[0] = mm3(table_ref[...], high, low)


def second(high, low, table):
    return pl.pallas_call(
        second_kernel,
        grid=(TILES,),
        out_shape=jax.ShapeDtypeStruct((TILES, 256, PATCHES), F32),
        in_specs=[
            pl.BlockSpec((TILES, 16, PATCHES), lambda q: (0, q, 0)),
            pl.BlockSpec((TILES, 16, PATCHES), lambda q: (0, q, 0)),
            pl.BlockSpec((512, 256), lambda q: (0, 0)),
        ],
        out_specs=pl.BlockSpec((1, 256, PATCHES), lambda q: (q, 0, 0)),
        compiler_params=pltpu.CompilerParams(vmem_limit_bytes=VMEM_LIMIT),
        cost_estimate=pl.CostEstimate(
            flops=2 * TILES * 256 * 256 * 3 * 256, bytes_accessed=8 << 20, transcendentals=0
        ),
    )(high, low, table)


def sublane_sum(value):
    total = value[0:8]
    for row in range(8, value.shape[0], 8):
        total = total + value[row : row + 8]
    return total


def signed(index):
    return float((index + 32) % 64 - 32)


def cross(a, b, whole):
    def along_y(p, r):
        if whole:
            return a[p, 0] * b[r, 0], a[p, 1] * b[r, 1]
        return a[p, 0] * b[r, 0] + a[p, 1] * b[r, 1], a[p, 0] * b[r, 1] - a[p, 1] * b[r, 0]

    cc, cs, sc, ss = along_y(0, 0), along_y(0, 1), along_y(1, 0), along_y(1, 1)
    head = lax.broadcasted_iota(jnp.int32, cc[0].shape, 0) == 0
    out = {}
    for part in range(2):
        out[0, part] = cc[part] + jnp.where(head, 0.0, ss[part])
        out[1, part] = jnp.where(head, ss[part], cs[part] - sc[part])
    return out


def flow_kernel(
    spec_ref, next_ref, first_ref, second_ref, third_ref, fourth_ref, out_ref,
    next_high, next_low, back_high, back_low, square, next_square, sum_y, sum_x,
):
    lanes = PATCHES
    def next_first(t, carry):
        tile = next_ref[t]
        both = mm(first_ref[...], tile, NT)
        high, low = split(both[:256] + both[256:])
        next_high[t] = high
        next_low[t] = low
        return carry

    lax.fori_loop(0, TILES, next_first, 0)
    square[...] = jnp.zeros_like(square)
    next_square[...] = jnp.zeros_like(next_square)
    left = lax.broadcasted_iota(jnp.int32, (256, 128), 1) < BLOCK

    def per_q(q, carry):
        rows = pl.ds(pl.multiple_of(q * 16, 16), 16)
        follow = mm3(
            second_ref[...],
            next_high[:, rows, :].reshape(256, 128),
            next_low[:, rows, :].reshape(256, 128),
        )
        own = spec_ref[q]
        dc = (lax.broadcasted_iota(jnp.int32, (256, 1), 0) + q * 256) == 0
        own = jnp.where(dc, 0.0, own)
        follow = jnp.where(dc, 0.0, follow)
        low_half, high_half = own[:, :128], own[:, 128:]
        low_roll, high_roll = pltpu.roll(low_half, 64, 1), pltpu.roll(high_half, 64, 1)
        other = jnp.concatenate(
            [
                jnp.where(left, low_roll, high_roll),
                jnp.where(left, high_roll, pltpu.roll(follow, 64, 1)),
            ],
            axis=1,
        )
        square[...] += sublane_sum(own * own)
        next_square[...] += sublane_sum(other * other)
        def parts(value, base):
            return {
                (x, y): value[base + y * 64 + x * 32 : base + y * 64 + x * 32 + 32]
                for x in range(2)
                for y in range(2)
            }

        def emit(whole_first):
            pieces = []
            for yk in range(2):
                out = cross(
                    parts(own, yk * 128), parts(other, yk * 128), whole_first and yk == 0
                )
                pieces += [out[0, 0], out[1, 0], out[0, 1], out[1, 1]]
            high, low = split(jnp.concatenate(pieces, axis=0))
            high, low = split(mm3(third_ref[...], high, low))
            back_high[q] = high
            back_low[q] = low

        @pl.when(q == 0)
        def _():
            emit(True)

        @pl.when(q != 0)
        def _():
            emit(False)

        return carry

    lax.fori_loop(0, TILES, per_q, 0)
    sum_y[...] = jnp.zeros_like(sum_y)
    sum_x[...] = jnp.zeros_like(sum_x)

    def per_g(g, carry):
        rows = pl.ds(pl.multiple_of(g * 16, 16), 16)
        corr = mm3(
            fourth_ref[...],
            back_high[:, rows, :].reshape(256, lanes),
            back_low[:, rows, :].reshape(256, lanes),
        )
        power = corr * corr
        all_d0 = power[0:64]
        weighted = jnp.zeros((8, lanes), F32)
        for d in range(4):
            block = power[d * 64 : d * 64 + 64]
            if d:
                all_d0 = all_d0 + block
            index = g * 4 + d
            shift = jnp.where(index < 32, index, index - 64).astype(F32)
            weighted = weighted + sublane_sum(block) * shift
        sum_y[...] += all_d0
        sum_x[...] += weighted
        return carry

    lax.fori_loop(0, TILES, per_g, 0)

    def down(value):
        return jnp.sum(value, axis=0, keepdims=True)

    index = lax.broadcasted_iota(jnp.int32, (64, lanes), 0)
    shift = jnp.where(index < 32, index, index - 64).astype(F32)
    total = down(sum_y[...])
    along_x = down(sum_x[...])
    along_y = down(sum_y[...] * shift)
    norm = (down(square[...]) * (1.0 / FLAT) + 1e-05) * (
        down(next_square[...]) * (1.0 / FLAT) + 1e-05
    )
    factor = (1.0 / (float(FLAT) * float(FLAT))) / norm
    total = jnp.maximum(total * factor, 0.5)
    flow = jnp.concatenate([along_x * factor / total, along_y * factor / total], axis=0)
    tile_rows = []
    for half in range(2):
        value = flow[:, half * 128 : half * 128 + 128]
        tile_rows += [value, pltpu.roll(value, 64, 1)]
    grid = jnp.concatenate(tile_rows, axis=0)
    lane = lax.broadcasted_iota(jnp.int32, (8, 128), 1)
    for j in range(N_SEC):
        upper = pltpu.roll(grid, (8 - 8 * j) % 128, 1)
        lower = pltpu.roll(grid, (128 - 8 * j) % 128, 1)
        gy = jnp.where(lane < GYW, lane, lane - GYW) + (8 * j - 8)
        window = jnp.where(lane < GYW, upper, lower)
        window = jnp.where((lane < 2 * GYW) & (gy >= 0) & (gy < 32), window, 0.0)
        out_ref[j] = jnp.broadcast_to(window[None, :, : 2 * GYW], (N_XY, 8, 2 * GYW))


def flow_windows(spec, following, tabs):
    return pl.pallas_call(
        flow_kernel,
        out_shape=jax.ShapeDtypeStruct((N_SEC, N_XY, 8, 2 * GYW), F32),
        scratch_shapes=[
            pltpu.VMEM((TILES, 256, 128), BF16),
            pltpu.VMEM((TILES, 256, 128), BF16),
            pltpu.VMEM((TILES, 256, PATCHES), BF16),
            pltpu.VMEM((TILES, 256, PATCHES), BF16),
            pltpu.VMEM((8, PATCHES), F32),
            pltpu.VMEM((8, PATCHES), F32),
            pltpu.VMEM((64, PATCHES), F32),
            pltpu.VMEM((8, PATCHES), F32),
        ],
        compiler_params=pltpu.CompilerParams(vmem_limit_bytes=VMEM_LIMIT),
        cost_estimate=pl.CostEstimate(
            flops=2 * TILES * 256 * 256 * 8 * 256, bytes_accessed=8 << 20, transcendentals=0
        ),
    )(spec, following, *tabs)


def relax_kernel(place_ref, arrived_ref, out_ref):
    column, block = place_ref[0], place_ref[1]
    lane = lax.broadcasted_iota(jnp.int32, (8, 128), 1)
    top = lane < GYW
    gy = jnp.where(top, lane, lane - GYW) + (8 * column - 8)
    inside = (lane < 2 * GYW) & (gy >= 0) & (gy < 32)
    mask = {}
    for o in range(-4, 5):
        valid = (block + o >= 0) & (block + o < N_XY)
        mask[o] = jnp.where(inside & valid, 0.2, 0.0)
    for s in range(N_SEC):
        flow, mesh = {}, {}
        for o in range(-4, 5):
            at = jnp.clip(block + o, 0, N_XY - 1)
            value = arrived_ref[s, at]
            value = jnp.concatenate([value, jnp.zeros((8, 128 - 2 * GYW), F32)], axis=1)
            flow[o] = value * mask[o]
            mesh[o] = jnp.where(mask[o] > 0.0, value, 0.0)
        for step in range(ITERS):
            reach = (ITERS - step) // 2
            up = {o: pltpu.roll(mesh[o], 128 - GYW, 1) for o in mesh}
            down = {o: pltpu.roll(mesh[o], GYW, 1) for o in mesh}
            new = {}
            zero = jnp.zeros((8, 128), F32)
            for o in range(-reach, reach + 1):
                near = jnp.where(
                    top, up[o] + up.get(o - 1, zero), down[o] + down.get(o + 1, zero)
                )
                near = near + pltpu.roll(mesh[o], 1, 1) + pltpu.roll(mesh[o], 127, 1)
                new[o] = flow[o] + mask[o] * near
            mesh = new
        out_ref[s] = mesh[0]


def relax(place, arrived):
    return pl.pallas_call(
        relax_kernel,
        out_shape=jax.ShapeDtypeStruct((N_SEC, 8, 128), F32),
        in_specs=[
            pl.BlockSpec(memory_space=pltpu.SMEM),
            pl.BlockSpec(memory_space=pltpu.VMEM),
        ],
        out_specs=pl.BlockSpec(memory_space=pltpu.VMEM),
        compiler_params=pltpu.CompilerParams(vmem_limit_bytes=VMEM_LIMIT),
    )(place, arrived)


def local(raw_pieces, piece_owner, piece_slot, blend):
    tabs = [jnp.asarray(t) for t in tables()]
    owner = piece_owner[:, :, 0].astype(F32)
    section = jnp.arange(SEC_DEV, dtype=F32)[:, None]
    zero = jnp.zeros((SEC_DEV, PIECES), F32)
    meta = jnp.stack(
        [
            owner + N_XY * section,
            owner * CHUNK + section * CAP,
            blend,
            piece_slot.astype(F32) + (section * BLOCK + 1.0),
            zero, zero, zero, zero,
        ]
    ).reshape(8, ROWS_IN)
    outgoing = send_rows(meta, raw_pieces.reshape(ROWS_IN, FLAT))
    arrived = lax.all_to_all(outgoing, "xy", split_axis=0, concat_axis=0, tiled=True)
    first, high, low = stitch(arrived, tabs[0])
    back = [(i + 1, i) for i in range(N_SEC - 1)]
    following = lax.ppermute(first, "sec", back)
    spec = second(high, low, tabs[1])
    following = following.reshape(BLOCK, TILES, TILE).transpose(1, 0, 2)
    following = jnp.pad(following, ((0, 0), (0, 128 - BLOCK), (0, 0)))
    windows = flow_windows(spec, following, tabs)
    got = lax.all_to_all(
        windows.reshape(N_SEC * N_XY, 8, 2 * GYW), ("sec", "xy"), split_axis=0, concat_axis=0,
        tiled=True,
    )
    place = jnp.stack([lax.axis_index("sec"), lax.axis_index("xy")]).astype(jnp.int32)
    mesh = relax(place, got.reshape(N_SEC, N_XY, 8, 2 * GYW))
    mesh = mesh.reshape(N_SEC * 4, 2, 128)[:15, :, : 2 * GYW].reshape(15, 2, 2, GYW)
    return mesh[:, :, :, 8:16]


def solution(mesh):
    in_specs = (P("sec", "xy", None), P("sec", "xy", None), P("sec", "xy"), P("sec", "xy"))
    out_specs = P(None, None, "xy", "sec")
    return jax.shard_map(local, mesh=mesh, in_specs=in_specs, out_specs=out_specs, check_vma=False)
```

time: 659 us -> 180 us (0.27)
  the two profiles are of different devices: /device:TPU:17 before, /device:TPU:1 now
where the time goes in v1:
time: 180 us; the launch traced here: 179 us
  blocking collectives  87.2 us (48%)
  Pallas kernels  62.5 us (35%)
  waiting for transfers between devices  9.95 us (6%)
  local copies, waits for them, and re-layouts  8.16 us (5%)
  starting transfers between devices  7.84 us (4%)
  other arithmetic  3.25 us (2%)
    all_to_all x1, blocking collectives, local(): lax.all_to_all(outgoing, 'xy', split_axis=0, concat_axis=0, tiled=True)  87.2 us
    pallas_call x1, Pallas kernels, flow_windows(): pl.pallas_call(flow_kernel, out_shape=jax.ShapeDtypeStruct((N_SEC, N_XY,...  23.4 us
    pallas_call x1, Pallas kernels, stitch(): pl.pallas_call(stitch_kernel, grid=(TILES,), out_shape=[jax.ShapeDtypeStr...  15.5 us
    pallas_call x1, Pallas kernels, second(): pl.pallas_call(second_kernel, grid=(TILES,), out_shape=jax.ShapeDtypeStru...  12.3 us
    all_to_all x1, waiting for transfers between devices, local(): lax.all_to_all(windows.reshape(N_SEC * N_XY, 8, 2 * GYW), ('sec', 'xy'),...  9.95 us
    pallas_call x1, Pallas kernels, send_rows(): pl.pallas_call(send_kernel, grid=(3,), out_shape=jax.ShapeDtypeStruct((RO...  8.18 us
    ppermute x1, starting transfers between devices, local(): following = lax.ppermute(first, 'sec', back)  4.31 us
  transfers between devices with their start and end apart: 2, of which 1 were waited for; matrix products, arithmetic and copies ran while one was open for 0% of the time, Pallas kernels for 7%

profile of v1, /device:TPU:1, one launch (start us, length us, event | category | flops | bytes accessed | tf_op | source)
XLA Modules:
  0.0 179.0 jit_solution(2714406519541062975)
XLA Ops:
  0.3 0.1 add.58
  0.3 0.7 convert_reduce_fusion
  1.0 0.1 convert_element_type.25
  1.1 0.8 convert_add_fusion
  2.0 0.8 stack.26
  2.7 0.6 stack.29.meta_ref
  3.4 8.2 %shard_map.82 = bf16[768,4224]{1,0:T(8,128)(2,1)} custom-call(f32[8,384]{1,0:T(8,128)} %stack.29.meta_ref, bf16[384,4096]{1,0:T(8,128)(2,1)} %bitcast.23), custom_call_target="tpu_custom_call" | custom-call | tf_op jit(solution)/shard_map/pallas_call | solution.py:119
  11.6 87.2 %all_to_all.16 = bf16[32,24,4224]{2,1,0:T(8,128)(2,1)} all-to-all(bf16[32,24,4224]{2,1,0:T(8,128)(2,1)} %bitcast.22), channel_id=1, replica_groups=mesh['sec'=4,'xy'=32] {'xy'}, dimensions={0} | all-to-all | bytes 12976128 | tf_op jit(solution)/shard_map/all_to_all | solution.py:434
  98.8 15.5 %shard_map.83 = (bf16[64,4096]{1,0:T(8,128)(2,1)}, bf16[16,256,256]{2,1,0:T(8,128)(2,1)}, bf16[16,256,256]{2,1,0:T(8,128)(2,1)}) custom-call(bf16[768,4224]{1,0:T(8,128)(2,1)} %bitcast.20, bf16[768,4224]{1,0:T(8,128)(2,1)} %bitcast.21, bf16[512,256]{1,0:T(8,128)(2,1)} %constant.32.clone.table_ref.first_ref), custom_call_target="tpu_custom_call" | custom-call | flops 2684354560 | bytes 12582912 | tf_op jit(solution)/shard_map/pallas_call | solution.py:154
  114.3 4.3 %collective-permute-start = (bf16[64,4096]{1,0:T(8,128)(2,1)}, bf16[64,4096]{1,0:T(8,128)(2,1)S(1)}, u32[]{:S(2)}, u32[]{:S(2)}) collective-permute-start(bf16[64,4096]{1,0:T(8,128)(2,1)} %get-tuple-element.10), channel_id=1, source_target_pairs={{32,0},{64,32},{96,64},{33,1},{65,33},{97,65},{34,2},{66,34},{98,6... | collective-permute-start | bytes 1572872 | tf_op jit(solution)/shard_map/ppermute | solution.py:437
  118.6 12.3 %shard_map.84.spec_ref = f32[16,256,256]{2,1,0:T(8,128)} custom-call(bf16[16,256,256]{2,1,0:T(8,128)(2,1)} %get-tuple-element.8.high_ref, bf16[16,256,256]{2,1,0:T(8,128)(2,1)} %get-tuple-element.9.low_ref, bf16[512,256]{1,0:T(8,128)(2,1)} %constant.33.clone.table_ref.second_ref), custom_call_target="tpu_custom_call" | custom-call | flops 1610612736 | bytes 8388608 | tf_op jit(solution)/shard_map/pallas_call | solution.py:183
  131.0 1.1 pad.4.next_ref
  132.1 23.4 %shard_map.85 = f32[4,32,8,48]{3,2,1,0:T(8,128)} custom-call(f32[16,256,256]{2,1,0:T(8,128)} %shard_map.84.spec_ref, bf16[16,128,256]{2,1,0:T(8,128)(2,1)} %pad.4.next_ref, bf16[512,256]{1,0:T(8,128)(2,1)} %constant.32.clone.table_ref.first_ref, bf16[512,256]{1,0:T(8,128)(2,1)} %constant.33.clone.table_ref.second_ref, ...), custom_call_target="tpu_custom_call" | custom-call | flops 4294967296 | bytes 8388608 | tf_op jit(solution)/shard_map/pallas_call | solution.py:352
  155.4 2.2 %reshape.112 = f32[128,1,384]{2,1,0:T(1,128)} reshape(f32[128,8,48]{2,1,0:T(8,128)} %bitcast.27) | data formatting | bytes 393216
  157.6 3.5 %all-to-all-start.1 = ((f32[128,1,384]{2,1,0:T(1,128)}), f32[128,1,384]{2,1,0:T(1,128)S(1)}, u32[]{:S(2)}, u32[]{:S(2)}) async-start(f32[128,1,384]{2,1,0:T(1,128)} %reshape.112), calls=%async_computation.1 | async-start | bytes 393216 | tf_op jit(solution)/shard_map/all_to_all | solution.py:442
  161.2 0.7 pad_add_fusion.place_ref
  161.9 10.0 %all-to-all-done.1 = f32[128,1,384]{2,1,0:T(1,128)S(1)} async-done(((f32[128,1,384]{2,1,0:T(1,128)}), f32[128,1,384]{2,1,0:T(1,128)S(1)}, u32[]{:S(2)}, u32[]{:S(2)}) %all-to-all-start.1) | async-done | bytes 196640 | tf_op jit(solution)/shard_map/all_to_all | solution.py:442
  171.8 0.5 broadcast.64
  172.3 1.1 reduce.4
  173.4 1.0 reshape.113
  174.4 3.1 %shard_map.86 = f32[4,8,128]{2,1,0:T(8,128)} custom-call(s32[2]{0:T(128)} %pad_add_fusion.place_ref, f32[4,32,8,48]{3,2,1,0:T(8,128)} %bitcast.25), custom_call_target="tpu_custom_call" | custom-call | tf_op jit(solution)/shard_map/pallas_call | solution.py:407
  177.5 0.7 slice.8
  178.3 0.1 copy.11
  178.4 0.6 slice.9
  (11 shorter events, 0.4 us)
Async XLA Ops:
  114.3 16.7 %collective-permute-start = (bf16[64,4096]{1,0:T(8,128)(2,1)}, bf16[64,4096]{1,0:T(8,128)(2,1)S(1)}, u32[]{:S(2)}, u32[]{:S(2)}) collective-permute-start(bf16[64,4096]{1,0:T(8,128)(2,1)} %get-tuple-element.10), channel_id=1, source_target_pairs={{32,0},{64,32},{96,64},{33,1},{65,33},{97,65},{34,2},{66,34},{98,6... | collective-permute-start | bytes 1572872 | tf_op jit(solution)/shard_map/ppermute | solution.py:437
  157.6 14.2 %all-to-all-start.1 = ((f32[128,1,384]{2,1,0:T(1,128)}), f32[128,1,384]{2,1,0:T(1,128)S(1)}, u32[]{:S(2)}, u32[]{:S(2)}) async-start(f32[128,1,384]{2,1,0:T(1,128)} %reshape.112), calls=%async_computation.1 | async-start | bytes 393216 | tf_op jit(solution)/shard_map/all_to_all | solution.py:442

commit v2 on v1

v2 whole, which is shorter than its diff:
```python
import math

import jax
import jax.numpy as jnp
import numpy as np
from jax import lax
from jax.experimental import pallas as pl
from jax.experimental.pallas import tpu as pltpu
from jax.sharding import PartitionSpec as P

PS = 64
FLAT = PS * PS
CAP = 6
N_SEC = 4
N_XY = 32
SEC_DEV = 4
PIECES = 96
BLOCK = 64
ITERS = 8
KEYS = SEC_DEV * 128
CHUNK = SEC_DEV * CAP
ROWS_OUT = N_XY * CHUNK
SLOT_LANES = 128
WIDTH = FLAT + SLOT_LANES
PATCHES = SEC_DEV * BLOCK
TILE = 256
TILES = FLAT // TILE
GYW = 24
F32 = jnp.float32
BF16 = jnp.bfloat16
VMEM_LIMIT = 56 * 1024 * 1024

NT = (((1,), (1,)), ((), ()))
NN = (((1,), (0,)), ((), ()))


def real_basis(kind):
    pos = np.arange(PS)
    rows = {}
    for k in range(32):
        angle = 2.0 * math.pi * ((k * pos) % PS) / PS
        rows[k, 0] = np.cos(angle)
        rows[k, 1] = np.sin(angle) if k else np.cos(math.pi * pos)
    if kind == "forward":
        for (k, part), row in rows.items():
            rows[k, part] = row * (math.sqrt(2.0) if k else 1.0) / 8.0
    x_order = np.stack([rows[k, part] for part in range(2) for k in range(32)])
    y_order = np.stack([rows[k, part] for k in range(32) for part in range(2)])
    return x_order, y_order


def split_table(table):
    high = table.astype(jnp.bfloat16)
    low = (table - high.astype(np.float64)).astype(jnp.bfloat16)
    return np.concatenate([high, low], axis=0)


def tables():
    fwd_x, fwd_y = real_basis("forward")
    inv_x, inv_y = real_basis("inverse")
    eye = np.eye(4)
    first = np.einsum("ab,ky->kaby", eye, fwd_y).reshape(256, 256)
    second = np.einsum("ab,ktx->aktbx", eye, fwd_x.reshape(64, 16, 4)).reshape(256, 256)
    third = np.einsum("ab,kd->dabk", eye, inv_x).reshape(256, 256)
    fourth = np.einsum("ab,qkd->adqbk", eye, inv_y.reshape(16, 4, 64)).reshape(256, 256)
    return [split_table(t) for t in (first, second, third, fourth)]


def mm(a, b, dims=NN):
    return lax.dot_general(a, b, dims, preferred_element_type=F32)


def split(value):
    high = value.astype(BF16)
    return high, (value - high.astype(F32)).astype(BF16)


def mm3(table, high, low):
    both = mm(table, high)
    return both[:256] + both[256:] + mm(table[:256], low)


def lane_rows(scratch, ref):
    scratch[...] = jnp.zeros_like(scratch)
    scratch[0:SEC_DEV, 0:PIECES] = ref[...].astype(F32)
    return scratch[0:SEC_DEV, :]


def column(row):
    return jnp.broadcast_to(row, (128, 128)).T


def send_kernel(owner_ref, slot_ref, blend_ref, raw_ref, out_ref, lanes, select, blend, slots, warped):
    step = pl.program_id(0)

    @pl.when(step == 0)
    def _():
        warped[...] = jnp.zeros_like(warped)
        owners = lane_rows(lanes, owner_ref)
        slot_rows = lane_rows(lanes, slot_ref)
        blend_rows = lane_rows(lanes, blend_ref)
        line = lax.broadcasted_iota(jnp.int32, (128, 128), 0)
        lane = lax.broadcasted_iota(jnp.int32, (128, 128), 1)
        rows = lax.broadcasted_iota(jnp.int32, (ROWS_OUT, 128), 0)
        for s in range(SEC_DEV):
            owner = owners[s : s + 1]
            same = jnp.where((column(owner) == owner) & (line < lane), 1.0, 0.0)
            rank = jnp.sum(same, axis=0, keepdims=True)
            target = (owner * CHUNK + rank + float(s * CAP)).astype(jnp.int32)
            target = jnp.where(lane[0:1] < PIECES, target, -1)
            at = slice(128 * s, 128 * s + 128)
            select[:, at] = jnp.where(rows == target, 1.0, 0.0).astype(BF16)
            blend[at, :] = column(blend_rows[s : s + 1])
            slots[at, :] = (column(slot_rows[s : s + 1]) + float(s * BLOCK + 1)).astype(BF16)

    part = out_ref.shape[1]
    for s in range(SEC_DEV):
        at = slice(128 * s, 128 * s + PIECES)
        scale = blend[at, :]
        for lane in range(0, part, 128):
            warped[at, lane : lane + 128] = (
                raw_ref[s, :, lane : lane + 128].astype(F32) * scale
            ).astype(BF16)

    @pl.when(step == pl.num_programs(0) - 1)
    def _():
        for s in range(SEC_DEV):
            at = slice(128 * s, 128 * s + PIECES)
            warped[at, part - 128 :] = slots[at, :]

    out_ref[...] = mm(select[...], warped[...]).astype(BF16)


def send_rows(owner, slot, blend, raw):
    part = WIDTH // 3
    small = pl.BlockSpec((SEC_DEV, PIECES), lambda i: (0, 0))
    return pl.pallas_call(
        send_kernel,
        grid=(3,),
        out_shape=jax.ShapeDtypeStruct((ROWS_OUT, WIDTH), BF16),
        in_specs=[small, small, small, pl.BlockSpec((SEC_DEV, PIECES, part), lambda i: (0, 0, i))],
        out_specs=pl.BlockSpec((ROWS_OUT, part), lambda i: (0, i)),
        scratch_shapes=[
            pltpu.VMEM((8, 128), F32),
            pltpu.VMEM((ROWS_OUT, KEYS), BF16),
            pltpu.VMEM((KEYS, 128), F32),
            pltpu.VMEM((KEYS, 128), BF16),
            pltpu.VMEM((KEYS, part), BF16),
        ],
        compiler_params=pltpu.CompilerParams(vmem_limit_bytes=VMEM_LIMIT),
    )(owner, slot, blend, raw)


LANES_B = 1024


def stitch_kernel(slot_ref, rows_ref, first_ref, out_ref, place):
    @pl.when(pl.program_id(0) == 0)
    def _():
        ids = slot_ref[...].astype(F32).T
        wanted = lax.broadcasted_iota(jnp.int32, (PATCHES, ROWS_OUT), 0).astype(F32) + 1.0
        place[...] = jnp.where(jnp.concatenate([ids, ids], axis=0) == wanted, 1.0, 0.0).astype(BF16)

    patches = mm(place[...], rows_ref[...]).astype(BF16)
    first_ref[...] = patches[:BLOCK]
    out_ref[...] = patches


def stitch(rows):
    return pl.pallas_call(
        stitch_kernel,
        grid=(FLAT // LANES_B,),
        out_shape=[
            jax.ShapeDtypeStruct((BLOCK, FLAT), BF16),
            jax.ShapeDtypeStruct((PATCHES, FLAT), BF16),
        ],
        in_specs=[
            pl.BlockSpec((ROWS_OUT, SLOT_LANES), lambda t: (0, FLAT // SLOT_LANES)),
            pl.BlockSpec((ROWS_OUT, LANES_B), lambda t: (0, t)),
        ],
        out_specs=[
            pl.BlockSpec((BLOCK, LANES_B), lambda t: (0, t)),
            pl.BlockSpec((PATCHES, LANES_B), lambda t: (0, t)),
        ],
        scratch_shapes=[pltpu.VMEM((PATCHES, ROWS_OUT), BF16)],
        compiler_params=pltpu.CompilerParams(vmem_limit_bytes=VMEM_LIMIT),
    )(rows, rows)


GROUP = 4
GROUPS = TILES // GROUP


def spectrum_kernel(patch_ref, first_ref, second_ref, out_ref, high, low):
    @pl.when(pl.program_id(0) == 0)
    def _():
        for t in range(TILES):
            both = mm(first_ref[...], patch_ref[:, t * TILE : t * TILE + TILE], NT)
            high[t], low[t] = split(both[:256] + both[256:])

    for i in range(GROUP):
        at = pl.ds(pl.multiple_of(pl.program_id(0) * (16 * GROUP) + 16 * i, 16), 16)
        out_ref[i] = mm3(
            second_ref[...],
            high[:, at, :].reshape(256, PATCHES),
            low[:, at, :].reshape(256, PATCHES),
        )


def spectrum(patches, first, second):
    return pl.pallas_call(
        spectrum_kernel,
        grid=(GROUPS,),
        out_shape=jax.ShapeDtypeStruct((TILES, 256, PATCHES), F32),
        in_specs=[
            pl.BlockSpec((PATCHES, FLAT), lambda q: (0, 0)),
            pl.BlockSpec((512, 256), lambda q: (0, 0)),
            pl.BlockSpec((512, 256), lambda q: (0, 0)),
        ],
        out_specs=pl.BlockSpec((GROUP, 256, PATCHES), lambda q: (q, 0, 0)),
        scratch_shapes=[
            pltpu.VMEM((TILES, 256, PATCHES), BF16),
            pltpu.VMEM((TILES, 256, PATCHES), BF16),
        ],
        compiler_params=pltpu.CompilerParams(vmem_limit_bytes=VMEM_LIMIT),
        cost_estimate=pl.CostEstimate(
            flops=2 * TILES * 256 * 256 * 5 * 256, bytes_accessed=8 << 20, transcendentals=0
        ),
    )(patches, first, second)


def sublane_sum(value):
    total = value[0:8]
    for row in range(8, value.shape[0], 8):
        total = total + value[row : row + 8]
    return total


def next_spectrum(next_ref, first_ref, second_ref, high, low, follow):
    left = lax.broadcasted_iota(jnp.int32, (16, 128), 1) < BLOCK
    for tg in range(GROUPS):
        rows = jnp.concatenate(
            [
                next_ref[:, (GROUP * tg + i) * TILE : (GROUP * tg + i + 1) * TILE]
                for i in range(GROUP)
            ],
            axis=0,
        )
        both = mm(first_ref[...], rows, NT)
        value = both[:256] + both[256:]
        for half in range(2):
            lanes = value[:, half * 128 : half * 128 + 128]
            rolled = pltpu.roll(lanes, BLOCK, 1)
            for pair in range(TILES // 2):
                g, to = pair // 2, (pair % 2) * 128
                even = slice(32 * pair, 32 * pair + 16)
                odd = slice(32 * pair + 16, 32 * pair + 32)
                for i in range(2):
                    t = GROUP * tg + 2 * half + i
                    if i == 0:
                        packed = jnp.where(left, lanes[even], rolled[odd])
                    else:
                        packed = jnp.where(left, rolled[even], lanes[odd])
                    at = slice(16 * t, 16 * t + 16)
                    up, down = split(packed)
                    high[g, at, to : to + 128] = up
                    low[g, at, to : to + 128] = down
    for g in range(GROUPS):
        follow[g] = mm3(second_ref[...], high[g], low[g])


def cross(a, b, first_step):
    def along_y(p, r):
        b_sine, b_cosine = b[r, 1], b[r, 0]
        if first_step is not None:
            b_sine, b_cosine = (
                jnp.where(first_step, 0.0, b_sine),
                jnp.where(first_step, -b_sine, b_cosine),
            )
        return a[p, 0] * b[r, 0] + a[p, 1] * b_sine, a[p, 0] * b_sine - a[p, 1] * b_cosine

    cc, cs, sc, ss = along_y(0, 0), along_y(0, 1), along_y(1, 0), along_y(1, 1)
    head = lax.broadcasted_iota(jnp.int32, cc[0].shape, 0) == 0
    out = {}
    for part in range(2):
        out[0, part] = cc[part] + jnp.where(head, 0.0, ss[part])
        out[1, part] = jnp.where(head, ss[part], cs[part] - sc[part])
    return out


def flow_kernel(
    spec_ref, next_ref, first_ref, second_ref, third_ref, fourth_ref, out_ref,
    next_high, next_low, follow, back_high, back_low, square, next_square, sum_y, sum_x,
):
    lanes = PATCHES
    step = pl.program_id(0)

    @pl.when(step == 0)
    def _():
        next_spectrum(next_ref, first_ref, second_ref, next_high, next_low, follow)
        square[...] = jnp.zeros_like(square)
        next_square[...] = jnp.zeros_like(next_square)

    left = lax.broadcasted_iota(jnp.int32, (256, 128), 1) < BLOCK
    top = lax.broadcasted_iota(jnp.int32, (256, 1), 0) == 0
    own_total = jnp.zeros((8, lanes), F32)
    other_total = jnp.zeros((8, lanes), F32)
    for i in range(GROUP):
        own = spec_ref[i]
        after = follow[step, :, (i // 2) * 128 : (i // 2) * 128 + 128]
        if i == 0:
            zero = top & (step == 0)
            own = jnp.where(zero, 0.0, own)
            after = jnp.where(zero, 0.0, after)
        if i % 2 == 0:
            after = pltpu.roll(after, BLOCK, 1)
        low_roll = pltpu.roll(own[:, :128], BLOCK, 1)
        high_roll = pltpu.roll(own[:, 128:], BLOCK, 1)
        other = jnp.concatenate(
            [jnp.where(left, low_roll, high_roll), jnp.where(left, high_roll, after)], axis=1
        )
        own_total = own_total + sublane_sum(own * own)
        other_total = other_total + sublane_sum(other * other)
        pieces = []
        for yk in range(2):
            a, b = (
                {
                    (x, y): value[yk * 128 + y * 64 + x * 32 : yk * 128 + y * 64 + x * 32 + 32]
                    for x in range(2)
                    for y in range(2)
                }
                for value in (own, other)
            )
            out = cross(a, b, step == 0 if i == 0 and yk == 0 else None)
            pieces += [out[0, 0], out[1, 0], out[0, 1], out[1, 1]]
        high, low = split(jnp.concatenate(pieces, axis=0))
        high, low = split(mm3(third_ref[...], high, low))
        back_high[step * GROUP + i] = high
        back_low[step * GROUP + i] = low
    square[...] += own_total
    next_square[...] += other_total

    @pl.when(step == GROUPS - 1)
    def _():
        finish(fourth_ref, out_ref, back_high, back_low, square, next_square, sum_y, sum_x)


def finish(fourth_ref, out_ref, back_high, back_low, square, next_square, sum_y, sum_x):
    lanes = PATCHES
    sum_y[...] = jnp.zeros_like(sum_y)
    sum_x[...] = jnp.zeros_like(sum_x)

    def per_group(group, carry):
        all_d0 = jnp.zeros((64, lanes), F32)
        weighted = jnp.zeros((8, lanes), F32)
        for i in range(GROUP):
            g = group * GROUP + i
            rows = pl.ds(pl.multiple_of(g * 16, 16), 16)
            corr = mm3(
                fourth_ref[...],
                back_high[:, rows, :].reshape(256, lanes),
                back_low[:, rows, :].reshape(256, lanes),
            )
            power = corr * corr
            for d in range(4):
                block = power[d * 64 : d * 64 + 64]
                all_d0 = all_d0 + block
                index = g * 4 + d
                shift = jnp.where(index < 32, index, index - 64).astype(F32)
                weighted = weighted + sublane_sum(block) * shift
        sum_y[...] += all_d0
        sum_x[...] += weighted
        return carry

    lax.fori_loop(0, GROUPS, per_group, 0)

    def down(value):
        return jnp.sum(value, axis=0, keepdims=True)

    index = lax.broadcasted_iota(jnp.int32, (64, lanes), 0)
    shift = jnp.where(index < 32, index, index - 64).astype(F32)
    total = down(sum_y[...])
    along_x = down(sum_x[...])
    along_y = down(sum_y[...] * shift)
    norm = (down(square[...]) * (1.0 / FLAT) + 1e-05) * (
        down(next_square[...]) * (1.0 / FLAT) + 1e-05
    )
    factor = (1.0 / (float(FLAT) * float(FLAT))) / norm
    total = jnp.maximum(total * factor, 0.5)
    tile_rows = []
    for value in (along_x * factor / total, along_y * factor / total):
        for half in range(2):
            lane_tile = value[:, half * 128 : half * 128 + 128]
            tile_rows += [lane_tile, pltpu.roll(lane_tile, 64, 1)]
    grid = jnp.concatenate(tile_rows, axis=0)
    lane = lax.broadcasted_iota(jnp.int32, (8, 128), 1)
    for j in range(N_SEC):
        upper = pltpu.roll(grid, (8 - 8 * j) % 128, 1)
        lower = pltpu.roll(grid, (128 - 8 * j) % 128, 1)
        gy = jnp.where(lane < GYW, lane, lane - GYW) + (8 * j - 8)
        window = jnp.where(lane < GYW, upper, lower)
        window = jnp.where((lane < 2 * GYW) & (gy >= 0) & (gy < 32), window, 0.0)
        for b in range(N_XY):
            out_ref[(j * N_XY + b) * 8 : (j * N_XY + b) * 8 + 8, :] = window


def flow_windows(spec, following, tabs):
    table = pl.BlockSpec((512, 256), lambda q: (0, 0))
    return pl.pallas_call(
        flow_kernel,
        grid=(GROUPS,),
        out_shape=jax.ShapeDtypeStruct((N_SEC * N_XY * 8, 128), F32),
        in_specs=[
            pl.BlockSpec((GROUP, 256, PATCHES), lambda q: (q, 0, 0)),
            pl.BlockSpec((BLOCK, FLAT), lambda q: (0, 0)),
            table, table, table, table,
        ],
        out_specs=pl.BlockSpec((N_SEC * N_XY * 8, 128), lambda q: (0, 0)),
        scratch_shapes=[
            pltpu.VMEM((GROUPS, 256, 256), BF16),
            pltpu.VMEM((GROUPS, 256, 256), BF16),
            pltpu.VMEM((GROUPS, 256, 256), F32),
            pltpu.VMEM((TILES, 256, PATCHES), BF16),
            pltpu.VMEM((TILES, 256, PATCHES), BF16),
            pltpu.VMEM((8, PATCHES), F32),
            pltpu.VMEM((8, PATCHES), F32),
            pltpu.VMEM((64, PATCHES), F32),
            pltpu.VMEM((8, PATCHES), F32),
        ],
        compiler_params=pltpu.CompilerParams(vmem_limit_bytes=VMEM_LIMIT),
        cost_estimate=pl.CostEstimate(
            flops=2 * TILES * 256 * 256 * 8 * 256, bytes_accessed=8 << 20, transcendentals=0
        ),
    )(spec, following, *tabs)


def relax_kernel(place_ref, arrived_ref, out_ref):
    column, block = place_ref[0], place_ref[1]
    lane = lax.broadcasted_iota(jnp.int32, (8, 128), 1)
    top = lane < GYW
    gy = jnp.where(top, lane, lane - GYW) + (8 * column - 8)
    inside = (lane < 2 * GYW) & (gy >= 0) & (gy < 32)
    mask = {}
    for o in range(-4, 5):
        valid = (block + o >= 0) & (block + o < N_XY)
        mask[o] = jnp.where(inside & valid, 0.2, 0.0)
    zero = jnp.zeros((8, 128), F32)
    result = []
    for s in range(N_SEC):
        flow, mesh = {}, {}
        for o in range(-4, 5):
            at = s * N_XY + jnp.clip(block + o, 0, N_XY - 1)
            value = arrived_ref[pl.ds(pl.multiple_of(at * 8, 8), 8), :]
            flow[o] = value * mask[o]
            mesh[o] = jnp.where(mask[o] > 0.0, value, 0.0)
        for step in range(ITERS):
            reach = (ITERS - step) // 2
            up = {o: pltpu.roll(mesh[o], 128 - GYW, 1) for o in mesh}
            down = {o: pltpu.roll(mesh[o], GYW, 1) for o in mesh}
            new = {}
            for o in range(-reach, reach + 1):
                near = jnp.where(
                    top, up[o] + up.get(o - 1, zero), down[o] + down.get(o + 1, zero)
                )
                near = near + pltpu.roll(mesh[o], 1, 1) + pltpu.roll(mesh[o], 127, 1)
                new[o] = flow[o] + mask[o] * near
            mesh = new
        result.append(mesh[0])
    for c in range(2):
        rows = [value[4 * c : 4 * c + 4] for value in result]
        turned = jnp.concatenate(rows + [jnp.zeros((112, 128), F32)], axis=0).T
        for i in range(2):
            out_ref[c, i] = turned[GYW * i + 8 : GYW * i + 16, :15]


def relax(place, arrived):
    return pl.pallas_call(
        relax_kernel,
        out_shape=jax.ShapeDtypeStruct((2, 2, 8, 15), F32),
        in_specs=[
            pl.BlockSpec(memory_space=pltpu.SMEM),
            pl.BlockSpec(memory_space=pltpu.VMEM),
        ],
        out_specs=pl.BlockSpec(memory_space=pltpu.VMEM),
        compiler_params=pltpu.CompilerParams(vmem_limit_bytes=VMEM_LIMIT),
    )(place, arrived)


def local(raw_pieces, piece_owner, piece_slot, blend):
    tabs = [jnp.asarray(t) for t in tables()]
    outgoing = send_rows(piece_owner[:, :, 0], piece_slot, blend, raw_pieces)
    arrived = lax.all_to_all(outgoing, "xy", split_axis=0, concat_axis=0, tiled=True)
    first, patches = stitch(arrived)
    back = [(i + 1, i) for i in range(N_SEC - 1)]
    following = lax.ppermute(first, "sec", back)
    spec = spectrum(patches, tabs[0], tabs[1])
    windows = flow_windows(spec, following, tabs)
    got = lax.all_to_all(windows, ("sec", "xy"), split_axis=0, concat_axis=0, tiled=True)
    place = jnp.stack([lax.axis_index("sec"), lax.axis_index("xy")]).astype(jnp.int32)
    return relax(place, got).transpose(3, 0, 1, 2)


def solution(mesh):
    in_specs = (P("sec", "xy", None), P("sec", "xy", None), P("sec", "xy"), P("sec", "xy"))
    out_specs = P(None, None, "xy", "sec")
    return jax.shard_map(local, mesh=mesh, in_specs=in_specs, out_specs=out_specs, check_vma=False)
```

time: 180 us -> 147 us (0.82)
  Pallas kernels: 62.5 us -> 34.9 us
  local copies, waits for them, and re-layouts: 8.16 us -> 1.59 us
  waiting for transfers between devices: 9.95 us -> 13.7 us
  other arithmetic: 3.25 us -> 0.65 us
    pallas_call x4, Pallas kernels: 54.3 us -> 26.5 us  [the longest x1 10.5 us: flow_windows(): pl.pallas_call(flow_kernel, grid=(GROUPS,), out_shape=jax.ShapeDtypeStruc...]
    all_to_all x1, waiting for transfers between devices: 9.95 us -> 13.1 us  [local(): lax.all_to_all(windows, ('sec', 'xy'), split_axis=0, concat_axis=0, tiled...]
  transfers between devices with their start and end apart: 2 -> 2, of which waited for: 1 -> 2; matrix products, arithmetic and copies ran while one was open for 0% -> 0% of each run, Pallas kernels for 7% -> 5%
where the time goes in v2:
time: 147 us; the launch traced here: 146 us
  blocking collectives  87.2 us (59%)
  Pallas kernels  34.9 us (24%)
  waiting for transfers between devices  13.7 us (9%)
  starting transfers between devices  8.21 us (6%)
  local copies, waits for them, and re-layouts  1.59 us (1%)
    all_to_all x1, blocking collectives, local(): lax.all_to_all(outgoing, 'xy', split_axis=0, concat_axis=0, tiled=True)  87.2 us
    all_to_all x1, waiting for transfers between devices, local(): lax.all_to_all(windows, ('sec', 'xy'), split_axis=0, concat_axis=0, tiled...  13.1 us
    pallas_call x1, Pallas kernels, flow_windows(): pl.pallas_call(flow_kernel, grid=(GROUPS,), out_shape=jax.ShapeDtypeStruc...  10.5 us
    pallas_call x1, Pallas kernels, send_rows(): pl.pallas_call(send_kernel, grid=(3,), out_shape=jax.ShapeDtypeStruct((RO...  8.4 us
    pallas_call x1, Pallas kernels, spectrum(): pl.pallas_call(spectrum_kernel, grid=(GROUPS,), out_shape=jax.ShapeDtypeS...  6.76 us
    pallas_call x1, Pallas kernels, stitch(): pl.pallas_call(stitch_kernel, grid=(FLAT // LANES_B,), out_shape=[jax.Sha...  6.02 us
    ppermute x1, starting transfers between devices, local(): following = lax.ppermute(first, 'sec', back)  4.31 us
    all_to_all x1, starting transfers between devices, local(): lax.all_to_all(windows, ('sec', 'xy'), split_axis=0, concat_axis=0, tiled...  3.9 us
  transfers between devices with their start and end apart: 2, of which 2 were waited for; matrix products, arithmetic and copies ran while one was open for 0% of the time, Pallas kernels for 5%

profile of v2, /device:TPU:1, one launch (start us, length us, event | category | flops | bytes accessed | tf_op | source)
XLA Modules:
  0.0 146.2 jit_solution(6357755188842979652)
XLA Ops:
  0.0 8.4 %shard_map.82 = bf16[768,4224]{1,0:T(8,128)(2,1)} custom-call(s32[4,96]{1,0:T(4,128)} %bitcast.13, s32[4,96]{1,0:T(4,128)} %slot_ref.1, f32[4,96]{1,0:T(4,128)} %blend_ref.1, bf16[4,96,4096]{2,1,0:T(8,128)(2,1)} %raw_ref.1), custom_call_target="tpu_custom_call" | custom-call | tf_op jit(solution)/shard_map/pallas_call | solution.py:137
  8.4 87.2 %all_to_all.22 = bf16[32,24,4224]{2,1,0:T(8,128)(2,1)} all-to-all(bf16[32,24,4224]{2,1,0:T(8,128)(2,1)} %bitcast.10), channel_id=1, replica_groups=mesh['sec'=4,'xy'=32] {'xy'}, dimensions={0} | all-to-all | bytes 12976128 | tf_op jit(solution)/shard_map/all_to_all | solution.py:492
  95.6 6.0 %shard_map.83 = (bf16[64,4096]{1,0:T(8,128)(2,1)}, bf16[256,4096]{1,0:T(8,128)(2,1)}) custom-call(bf16[768,4224]{1,0:T(8,128)(2,1)} %bitcast.8, bf16[768,4224]{1,0:T(8,128)(2,1)} %bitcast.9), custom_call_target="tpu_custom_call" | custom-call | tf_op jit(solution)/shard_map/pallas_call | solution.py:170
  101.6 4.3 %collective-permute-start = (bf16[64,4096]{1,0:T(8,128)(2,1)}, bf16[64,4096]{1,0:T(8,128)(2,1)S(1)}, u32[]{:S(2)}, u32[]{:S(2)}) collective-permute-start(bf16[64,4096]{1,0:T(8,128)(2,1)} %get-tuple-element.8), channel_id=1, source_target_pairs={{32,0},{64,32},{96,64},{33,1},{65,33},{97,65},{34,2},{66,34},{98,6... | collective-permute-start | bytes 1572872 | tf_op jit(solution)/shard_map/ppermute | solution.py:495
  106.0 6.8 %shard_map.84.spec_ref = f32[16,256,256]{2,1,0:T(8,128)} custom-call(bf16[256,4096]{1,0:T(8,128)(2,1)} %get-tuple-element.7.patch_ref, bf16[512,256]{1,0:T(8,128)(2,1)} %constant.17.clone.first_ref, bf16[512,256]{1,0:T(8,128)(2,1)} %constant.18.clone.second_ref), custom_call_target="tpu_custom_call" | custom-call | flops 2684354560 | bytes 8388608 | tf_op jit(solution)/shard_map/pallas_call | solution.py:211
  112.7 0.6 collective-permute-done.next_ref
  113.3 0.0 copy-start.1
  113.3 0.8 copy-done.1
  114.1 10.5 %shard_map.85 = f32[1024,128]{1,0:T(8,128)} custom-call(f32[16,256,256]{2,1,0:T(8,128)} %shard_map.84.spec_ref, bf16[64,4096]{1,0:T(8,128)(2,1)} %copy-done.1, bf16[512,256]{1,0:T(8,128)(2,1)} %constant.17.clone.first_ref, bf16[512,256]{1,0:T(8,128)(2,1)} %constant.18.clone.second_ref, bf16[512,256]{1,0:T(8,128)(2,1)} %constant.19.clone.third_ref, ...), custom_call_target="tpu_custom_call" | custom-call | flops 4294967296 | bytes 8388608 | tf_op jit(solution)/shard_map/pallas_call | solution.py:409
  124.6 3.9 %all-to-all-start.1 = ((f32[128,8,128]{2,1,0:T(8,128)}), f32[128,8,128]{2,1,0:T(8,128)S(1)}, u32[]{:S(2)}, u32[]{:S(2)}) async-start(f32[128,8,128]{2,1,0:T(8,128)} %bitcast.12), calls=%async_computation.1 | async-start | bytes 1048576 | tf_op jit(solution)/shard_map/all_to_all | solution.py:498
  128.5 0.7 pad_add_fusion.place_ref
  129.2 13.1 %all-to-all-done.1 = f32[128,8,128]{2,1,0:T(8,128)S(1)} async-done(((f32[128,8,128]{2,1,0:T(8,128)}), f32[128,8,128]{2,1,0:T(8,128)S(1)}, u32[]{:S(2)}, u32[]{:S(2)}) %all-to-all-start.1) | async-done | bytes 524320 | tf_op jit(solution)/shard_map/all_to_all | solution.py:498
  142.2 0.0 copy-start
  142.3 0.8 copy-done
  143.0 3.2 %shard_map.86 = f32[2,2,8,15]{3,2,1,0:T(8,128)} custom-call(s32[2]{0:T(128)} %pad_add_fusion.place_ref, f32[1024,128]{1,0:T(8,128)} %bitcast.11), custom_call_target="tpu_custom_call" | custom-call | tf_op jit(solution)/shard_map/pallas_call | solution.py:477
Async XLA Ops:
  101.6 11.7 %collective-permute-start = (bf16[64,4096]{1,0:T(8,128)(2,1)}, bf16[64,4096]{1,0:T(8,128)(2,1)S(1)}, u32[]{:S(2)}, u32[]{:S(2)}) collective-permute-start(bf16[64,4096]{1,0:T(8,128)(2,1)} %get-tuple-element.8), channel_id=1, source_target_pairs={{32,0},{64,32},{96,64},{33,1},{65,33},{97,65},{34,2},{66,34},{98,6... | collective-permute-start | bytes 1572872 | tf_op jit(solution)/shard_map/ppermute | solution.py:495
  113.3 0.8 copy-start.1
  124.6 17.6 %all-to-all-start.1 = ((f32[128,8,128]{2,1,0:T(8,128)}), f32[128,8,128]{2,1,0:T(8,128)S(1)}, u32[]{:S(2)}, u32[]{:S(2)}) async-start(f32[128,8,128]{2,1,0:T(8,128)} %bitcast.12), calls=%async_computation.1 | async-start | bytes 1048576 | tf_op jit(solution)/shard_map/all_to_all | solution.py:498
  142.2 0.8 copy-start

commit v3 on v2

v3 whole, which is shorter than its diff:
```python
import math

import jax
import jax.numpy as jnp
import numpy as np
from jax import lax
from jax.experimental import pallas as pl
from jax.experimental.pallas import tpu as pltpu
from jax.sharding import PartitionSpec as P

PS = 64
FLAT = PS * PS
CAP = 6
N_SEC = 4
N_XY = 32
SEC_DEV = 4
PIECES = 96
BLOCK = 64
ITERS = 8
KEYS = SEC_DEV * 128
CHUNK = SEC_DEV * CAP
LANE_TILES = FLAT // 128
PARTS = CHUNK // 8
TILES_OUT = PARTS * LANE_TILES + 1
PATCHES = SEC_DEV * BLOCK
TILE = 256
TILES = FLAT // TILE
GYW = 24
F32 = jnp.float32
BF16 = jnp.bfloat16
MIB = 1024 * 1024

VMEM_SPEC = pl.BlockSpec(memory_space=pltpu.VMEM)
NT = (((1,), (1,)), ((), ()))
NN = (((1,), (0,)), ((), ()))


def real_basis(kind):
    pos = np.arange(PS)
    rows = {}
    for k in range(32):
        angle = 2.0 * math.pi * ((k * pos) % PS) / PS
        rows[k, 0] = np.cos(angle)
        rows[k, 1] = np.sin(angle) if k else np.cos(math.pi * pos)
    if kind == "forward":
        for (k, part), row in rows.items():
            rows[k, part] = row * (math.sqrt(2.0) if k else 1.0) / 8.0
    x_order = np.stack([rows[k, part] for part in range(2) for k in range(32)])
    y_order = np.stack([rows[k, part] for k in range(32) for part in range(2)])
    return x_order, y_order


def split_table(table):
    high = table.astype(jnp.bfloat16)
    low = (table - high.astype(np.float64)).astype(jnp.bfloat16)
    return np.concatenate([high, low], axis=0)


def tables():
    fwd_x, fwd_y = real_basis("forward")
    inv_x, inv_y = real_basis("inverse")
    eye = np.eye(4)
    first = np.einsum("ab,ky->kaby", eye, fwd_y).reshape(256, 256)
    second = np.einsum("ab,ktx->aktbx", eye, fwd_x.reshape(64, 16, 4)).reshape(256, 256)
    third = np.einsum("ab,kd->dabk", eye, inv_x).reshape(256, 256)
    fourth = np.einsum("ab,qkd->adqbk", eye, inv_y.reshape(16, 4, 64)).reshape(256, 256)
    return [split_table(t) for t in (first, second, third, fourth)]


def mm(a, b, dims=NN):
    return lax.dot_general(a, b, dims, preferred_element_type=F32)


def split(value):
    high = value.astype(BF16)
    return high, (value - high.astype(F32)).astype(BF16)


def mm3(table, high, low):
    both = mm(table, high)
    return both[:256] + both[256:] + mm(table[:256], low)


def lane_rows(scratch, ref):
    scratch[...] = jnp.zeros_like(scratch)
    scratch[0:SEC_DEV, 0:PIECES] = ref[...].astype(F32)
    return scratch[0:SEC_DEV, :]


def column(row):
    return jnp.broadcast_to(row, (128, 128)).T


SEND_LANES = 1024
SENDS = FLAT // SEND_LANES


def send_kernel(
    owner_hbm, slot_hbm, blend_hbm, raw_hbm, out_hbm,
    owner_ref, slot_ref, blend_ref, raw_ref, lanes, select, blend, slots, warped, out_ref,
    sems, raw_sems, out_sems,
):
    small = [
        pltpu.make_async_copy(source, target, sems.at[i])
        for i, (source, target) in enumerate(
            [(owner_hbm, owner_ref), (slot_hbm, slot_ref), (blend_hbm, blend_ref)]
        )
    ]
    for copy in small:
        copy.start()
    large = [
        pltpu.make_async_copy(
            raw_hbm.at[:, :, pl.ds(i * SEND_LANES, SEND_LANES)], raw_ref.at[i], raw_sems.at[i]
        )
        for i in range(SENDS)
    ]
    for copy in large:
        copy.start()
    for s in range(SEC_DEV):
        for i in range(SENDS):
            warped[i, 128 * s + PIECES : 128 * s + 128, :] = jnp.zeros((32, SEND_LANES), BF16)
    line = lax.broadcasted_iota(jnp.int32, (128, 128), 0)
    lane = lax.broadcasted_iota(jnp.int32, (128, 128), 1)
    rows = lax.broadcasted_iota(jnp.int32, (8 * N_XY, 128), 0)
    rows = (rows // 8) * CHUNK + rows % 8
    for copy in small:
        copy.wait()
    owners = lane_rows(lanes, owner_ref)
    slot_rows = lane_rows(lanes, slot_ref)
    blend_rows = lane_rows(lanes, blend_ref)
    for s in range(SEC_DEV):
        owner = owners[s : s + 1]
        same = jnp.where((column(owner) == owner) & (line < lane), 1.0, 0.0)
        rank = jnp.sum(same, axis=0, keepdims=True)
        target = (owner * CHUNK + rank + float(s * CAP)).astype(jnp.int32)
        target = jnp.where(lane[0:1] < PIECES, target, -1)
        for j in range(PARTS):
            if s - j in (0, 1):
                at = slice(128 * (s - j), 128 * (s - j) + 128)
                select[j, :, at] = jnp.where(rows + 8 * j == target, 1.0, 0.0).astype(BF16)
        at = slice(128 * s, 128 * s + 128)
        blend[at, :] = column(blend_rows[s : s + 1])
        slots[at, :] = (column(slot_rows[s : s + 1]) + float(s * BLOCK + 1)).astype(BF16)

    copies = []

    def send_tiles(first, count):
        at = pl.ds(first, count)
        copies.append(
            pltpu.make_async_copy(out_ref.at[:, at], out_hbm.at[:, at], out_sems.at[len(copies)])
        )
        copies[-1].start()

    for i in range(SENDS):
        large[i].wait()
        for s in range(SEC_DEV):
            at = slice(128 * s, 128 * s + PIECES)
            scale = blend[at, :]
            for lane_at in range(0, SEND_LANES, 128):
                to = slice(lane_at, lane_at + 128)
                warped[i, at, to] = (raw_ref[i, s, :, to].astype(F32) * scale).astype(BF16)
        for j in range(PARTS):
            value = mm(select[j], warped[i, 128 * j : 128 * j + 256, :])
            first = LANE_TILES * j + i * (SEND_LANES // 128)
            for tile in range(SEND_LANES // 128):
                piece = value[:, tile * 128 : tile * 128 + 128].reshape(N_XY, 8, 128)
                out_ref[:, first + tile] = piece.astype(BF16)
            send_tiles(first, SEND_LANES // 128)
    ids = [mm(select[j], slots[128 * j : 128 * j + 256, :]) for j in range(PARTS)]
    lane = lax.broadcasted_iota(jnp.int32, (8 * N_XY, 128), 1)
    ids = jnp.where(lane == 0, ids[0], jnp.where(lane == 1, ids[1], ids[2]))
    out_ref[:, TILES_OUT - 1] = ids.reshape(N_XY, 8, 128).astype(BF16)
    send_tiles(TILES_OUT - 1, 1)
    for copy in copies:
        copy.wait()


def send_rows(owner, slot, blend, raw):
    hbm = pl.BlockSpec(memory_space=pltpu.HBM)
    return pl.pallas_call(
        send_kernel,
        out_shape=jax.ShapeDtypeStruct((N_XY, TILES_OUT, 8, 128), BF16),
        in_specs=[hbm, hbm, hbm, hbm],
        out_specs=hbm,
        scratch_shapes=[
            pltpu.VMEM((SEC_DEV, PIECES), jnp.int32),
            pltpu.VMEM((SEC_DEV, PIECES), jnp.int32),
            pltpu.VMEM((SEC_DEV, PIECES), F32),
            pltpu.VMEM((SENDS, SEC_DEV, PIECES, SEND_LANES), BF16),
            pltpu.VMEM((8, 128), F32),
            pltpu.VMEM((PARTS, 8 * N_XY, 256), BF16),
            pltpu.VMEM((KEYS, 128), F32),
            pltpu.VMEM((KEYS, 128), BF16),
            pltpu.VMEM((SENDS, KEYS, SEND_LANES), BF16),
            pltpu.VMEM((N_XY, TILES_OUT, 8, 128), BF16),
            pltpu.SemaphoreType.DMA((3,)),
            pltpu.SemaphoreType.DMA((SENDS,)),
            pltpu.SemaphoreType.DMA((SENDS * PARTS + 1,)),
        ],
        compiler_params=pltpu.CompilerParams(vmem_limit_bytes=60 * MIB),
    )(owner, slot, blend, raw)


def places(ids, part, count):
    wanted = lax.broadcasted_iota(jnp.int32, (count, 8 * N_XY), 0).astype(F32)
    match = ids[part : part + 1] == wanted + float(part * BLOCK + 1)
    return jnp.where(match, 1.0, 0.0).astype(BF16)


def row_ids(rows_ref):
    return rows_ref[:, TILES_OUT - 1].astype(F32).reshape(8 * N_XY, 128).T


def row_tiles(rows_ref, part, lane, size):
    first = LANE_TILES * part + lane // 128
    return jnp.concatenate(
        [rows_ref[:, first + tile].reshape(8 * N_XY, 128) for tile in range(size // 128)], axis=1
    )


def first_kernel(rows_ref, out_ref, place):
    place[...] = places(row_ids(rows_ref), 0, BLOCK)
    for at in range(0, FLAT, 1024):
        out_ref[:, at : at + 1024] = mm(place[...], row_tiles(rows_ref, 0, at, 1024)).astype(BF16)


def first_section(rows):
    return pl.pallas_call(
        first_kernel,
        out_shape=jax.ShapeDtypeStruct((BLOCK, FLAT), BF16),
        in_specs=[VMEM_SPEC],
        out_specs=VMEM_SPEC,
        scratch_shapes=[pltpu.VMEM((BLOCK, 8 * N_XY), BF16)],
        compiler_params=pltpu.CompilerParams(vmem_limit_bytes=8 * MIB),
        cost_estimate=pl.CostEstimate(flops=1 << 28, bytes_accessed=3 << 20, transcendentals=0),
    )(rows)


GROUP = 4
GROUPS = TILES // GROUP


def spectrum_kernel(rows_ref, first_ref, second_ref, out_ref, place, high, low):
    ids = row_ids(rows_ref)
    for j in range(PARTS):
        place[j] = places(ids, j, 2 * BLOCK)
    wide = 2 * TILE
    for at in range(0, FLAT, wide):
        pieces, before = [], None
        for j in range(PARTS):
            value = mm(place[j], row_tiles(rows_ref, j, at, wide))
            pieces.append(value[:BLOCK] if before is None else before + value[:BLOCK])
            before = value[BLOCK:]
        patches = jnp.concatenate(pieces + [before], axis=0).astype(BF16)
        for i in range(2):
            both = mm(first_ref[...], patches[:, i * TILE : (i + 1) * TILE], NT)
            t = at // TILE + i
            high[t], low[t] = split(both[:256] + both[256:])

    def per_group(group, carry):
        for i in range(GROUP):
            q = group * GROUP + i
            at = pl.ds(pl.multiple_of(16 * q, 16), 16)
            out_ref[q] = mm3(
                second_ref[...],
                high[:, at, :].reshape(256, PATCHES),
                low[:, at, :].reshape(256, PATCHES),
            )
        return carry

    lax.fori_loop(0, GROUPS, per_group, 0)
    out_ref[0, 0:1, :] = jnp.zeros((1, PATCHES), F32)


def spectrum(rows, first, second):
    return pl.pallas_call(
        spectrum_kernel,
        out_shape=jax.ShapeDtypeStruct((TILES, 256, PATCHES), F32),
        in_specs=[VMEM_SPEC] * 3,
        out_specs=VMEM_SPEC,
        scratch_shapes=[
            pltpu.VMEM((PARTS, 2 * BLOCK, 8 * N_XY), BF16),
            pltpu.VMEM((TILES, 256, PATCHES), BF16),
            pltpu.VMEM((TILES, 256, PATCHES), BF16),
        ],
        compiler_params=pltpu.CompilerParams(vmem_limit_bytes=16 * MIB),
        cost_estimate=pl.CostEstimate(
            flops=2 * TILES * 256 * 256 * 8 * 256, bytes_accessed=12 << 20, transcendentals=0
        ),
    )(rows, first, second)


def sublane_sum(value):
    total = value[0:8]
    for row in range(8, value.shape[0], 8):
        total = total + value[row : row + 8]
    return total


def next_spectrum(next_ref, first_ref, second_ref, high, low, follow):
    left = lax.broadcasted_iota(jnp.int32, (16, 128), 1) < BLOCK
    for tg in range(GROUPS):
        rows = jnp.concatenate(
            [
                next_ref[:, (GROUP * tg + i) * TILE : (GROUP * tg + i + 1) * TILE]
                for i in range(GROUP)
            ],
            axis=0,
        )
        both = mm(first_ref[...], rows, NT)
        value = both[:256] + both[256:]
        for half in range(2):
            lanes = value[:, half * 128 : half * 128 + 128]
            rolled = pltpu.roll(lanes, BLOCK, 1)
            for pair in range(TILES // 2):
                g, to = pair // 2, (pair % 2) * 128
                even = slice(32 * pair, 32 * pair + 16)
                odd = slice(32 * pair + 16, 32 * pair + 32)
                for i in range(2):
                    t = GROUP * tg + 2 * half + i
                    if i == 0:
                        packed = jnp.where(left, lanes[even], rolled[odd])
                    else:
                        packed = jnp.where(left, rolled[even], lanes[odd])
                    at = slice(16 * t, 16 * t + 16)
                    up, down = split(packed)
                    high[g, at, to : to + 128] = up
                    low[g, at, to : to + 128] = down
    for g in range(GROUPS):
        follow[g] = mm3(second_ref[...], high[g], low[g])
    follow[0, 0:1, 0:BLOCK] = jnp.zeros((1, BLOCK), F32)


def cross(a, b, first_step):
    def along_y(p, r):
        b_sine, b_cosine = b[r, 1], b[r, 0]
        if first_step is not None:
            b_sine, b_cosine = (
                jnp.where(first_step, 0.0, b_sine),
                jnp.where(first_step, -b_sine, b_cosine),
            )
        return a[p, 0] * b[r, 0] + a[p, 1] * b_sine, a[p, 0] * b_sine - a[p, 1] * b_cosine

    cc, cs, sc, ss = along_y(0, 0), along_y(0, 1), along_y(1, 0), along_y(1, 1)
    head = lax.broadcasted_iota(jnp.int32, cc[0].shape, 0) == 0
    out = {}
    for part in range(2):
        out[0, part] = cc[part] + jnp.where(head, 0.0, ss[part])
        out[1, part] = jnp.where(head, ss[part], cs[part] - sc[part])
    return out


def flow_kernel(
    spec_ref, next_ref, first_ref, second_ref, third_ref, fourth_ref, out_ref,
    next_high, next_low, follow, back_high, back_low, square, next_square, sum_y, sum_x,
):
    lanes = PATCHES
    next_spectrum(next_ref, first_ref, second_ref, next_high, next_low, follow)
    square[...] = jnp.zeros_like(square)
    left = lax.broadcasted_iota(jnp.int32, (256, 128), 1) < BLOCK

    def per_group(step, carry):
        own_total = jnp.zeros((8, lanes), F32)
        for i in range(GROUP):
            own = spec_ref[step * GROUP + i]
            after = follow[step, :, (i // 2) * 128 : (i // 2) * 128 + 128]
            if i % 2 == 0:
                after = pltpu.roll(after, BLOCK, 1)
            low_roll = pltpu.roll(own[:, :128], BLOCK, 1)
            high_roll = pltpu.roll(own[:, 128:], BLOCK, 1)
            other = jnp.concatenate(
                [jnp.where(left, low_roll, high_roll), jnp.where(left, high_roll, after)], axis=1
            )
            own_total = own_total + sublane_sum(own * own)
            pieces = []
            for yk in range(2):
                a, b = (
                    {
                        (x, y): value[yk * 128 + y * 64 + x * 32 : yk * 128 + y * 64 + x * 32 + 32]
                        for x in range(2)
                        for y in range(2)
                    }
                    for value in (own, other)
                )
                out = cross(a, b, step == 0 if i == 0 and yk == 0 else None)
                pieces += [out[0, 0], out[1, 0], out[0, 1], out[1, 1]]
            high, low = split(jnp.concatenate(pieces, axis=0))
            high, low = split(mm3(third_ref[...], high, low))
            back_high[step * GROUP + i] = high
            back_low[step * GROUP + i] = low
        square[...] += own_total
        return carry

    lax.fori_loop(0, GROUPS, per_group, 0)
    after = jnp.zeros((8, lanes), F32)
    for g in range(GROUPS):
        after = after + sublane_sum(follow[g] * follow[g])
    after = after[:, :128] + after[:, 128:]
    after = after + pltpu.roll(after, BLOCK, 1)
    own = square[...]
    low_roll, high_roll = (pltpu.roll(own[:, i : i + 128], BLOCK, 1) for i in (0, 128))
    left = lax.broadcasted_iota(jnp.int32, (8, 128), 1) < BLOCK
    next_square[...] = jnp.concatenate(
        [jnp.where(left, low_roll, high_roll), jnp.where(left, high_roll, after)], axis=1
    )
    finish(fourth_ref, out_ref, back_high, back_low, square, next_square, sum_y, sum_x)


def finish(fourth_ref, out_ref, back_high, back_low, square, next_square, sum_y, sum_x):
    lanes = PATCHES
    sum_y[...] = jnp.zeros_like(sum_y)
    sum_x[...] = jnp.zeros_like(sum_x)

    def per_group(group, carry):
        all_d0 = jnp.zeros((64, lanes), F32)
        weighted = jnp.zeros((8, lanes), F32)
        for i in range(GROUP):
            g = group * GROUP + i
            rows = pl.ds(pl.multiple_of(g * 16, 16), 16)
            corr = mm3(
                fourth_ref[...],
                back_high[:, rows, :].reshape(256, lanes),
                back_low[:, rows, :].reshape(256, lanes),
            )
            power = corr * corr
            for d in range(4):
                block = power[d * 64 : d * 64 + 64]
                all_d0 = all_d0 + block
                index = g * 4 + d
                shift = jnp.where(index < 32, index, index - 64).astype(F32)
                weighted = weighted + sublane_sum(block) * shift
        sum_y[...] += all_d0
        sum_x[...] += weighted
        return carry

    lax.fori_loop(0, GROUPS, per_group, 0)

    def down(value):
        return jnp.sum(value, axis=0, keepdims=True)

    index = lax.broadcasted_iota(jnp.int32, (64, lanes), 0)
    shift = jnp.where(index < 32, index, index - 64).astype(F32)
    total = down(sum_y[...])
    along_x = down(sum_x[...])
    along_y = down(sum_y[...] * shift)
    norm = (down(square[...]) * (1.0 / FLAT) + 1e-05) * (
        down(next_square[...]) * (1.0 / FLAT) + 1e-05
    )
    factor = (1.0 / (float(FLAT) * float(FLAT))) / norm
    total = jnp.maximum(total * factor, 0.5)
    tile_rows = []
    for value in (along_x * factor / total, along_y * factor / total):
        for half in range(2):
            lane_tile = value[:, half * 128 : half * 128 + 128]
            tile_rows += [lane_tile, pltpu.roll(lane_tile, 64, 1)]
    grid = jnp.concatenate(tile_rows, axis=0)
    lane = lax.broadcasted_iota(jnp.int32, (8, 128), 1)
    for j in range(N_SEC):
        upper = pltpu.roll(grid, (8 - 8 * j) % 128, 1)
        lower = pltpu.roll(grid, (128 - 8 * j) % 128, 1)
        gy = jnp.where(lane < GYW, lane, lane - GYW) + (8 * j - 8)
        window = jnp.where(lane < GYW, upper, lower)
        window = jnp.where((lane < 2 * GYW) & (gy >= 0) & (gy < 32), window, 0.0)
        packed = window[0:4] + pltpu.roll(window, 64, 1)[4:8]
        for b in range(N_XY):
            out_ref[j * N_XY + b] = packed


def flow_windows(spec, following, tabs):
    return pl.pallas_call(
        flow_kernel,
        out_shape=jax.ShapeDtypeStruct((N_SEC * N_XY, 4, 128), F32),
        in_specs=[VMEM_SPEC] * 6,
        out_specs=VMEM_SPEC,
        scratch_shapes=[
            pltpu.VMEM((GROUPS, 256, 256), BF16),
            pltpu.VMEM((GROUPS, 256, 256), BF16),
            pltpu.VMEM((GROUPS, 256, 256), F32),
            pltpu.VMEM((TILES, 256, PATCHES), BF16),
            pltpu.VMEM((TILES, 256, PATCHES), BF16),
            pltpu.VMEM((8, PATCHES), F32),
            pltpu.VMEM((8, PATCHES), F32),
            pltpu.VMEM((64, PATCHES), F32),
            pltpu.VMEM((8, PATCHES), F32),
        ],
        compiler_params=pltpu.CompilerParams(vmem_limit_bytes=24 * MIB),
        cost_estimate=pl.CostEstimate(
            flops=2 * TILES * 256 * 256 * 8 * 256, bytes_accessed=8 << 20, transcendentals=0
        ),
    )(spec, following, *tabs)


def relax_kernel(place_ref, arrived_ref, out_ref):
    column, block = place_ref[0], place_ref[1]
    lane = lax.broadcasted_iota(jnp.int32, (8, 128), 1)
    lane = jnp.where(lane < 64, lane, lane - 64)
    top = lane < GYW
    gy = jnp.where(top, lane, lane - GYW) + (8 * column - 8)
    inside = (lane < 2 * GYW) & (gy >= 0) & (gy < 32)
    mask = {}
    for o in range(-4, 5):
        valid = (block + o >= 0) & (block + o < N_XY)
        mask[o] = jnp.where(inside & valid, 0.2, 0.0)
    zero = jnp.zeros((8, 128), F32)
    result = []
    for s in range(0, N_SEC, 2):
        flow, mesh = {}, {}
        for o in range(-4, 5):
            at = jnp.clip(block + o, 0, N_XY - 1)
            value = jnp.concatenate(
                [arrived_ref[s * N_XY + at], arrived_ref[(s + 1) * N_XY + at]], axis=0
            )
            flow[o] = value * mask[o]
            mesh[o] = jnp.where(mask[o] > 0.0, value, 0.0)
        for step in range(ITERS):
            reach = (ITERS - step) // 2
            up = {o: pltpu.roll(mesh[o], 128 - GYW, 1) for o in mesh}
            down = {o: pltpu.roll(mesh[o], GYW, 1) for o in mesh}
            new = {}
            for o in range(-reach, reach + 1):
                near = jnp.where(
                    top, up[o] + up.get(o - 1, zero), down[o] + down.get(o + 1, zero)
                )
                near = near + pltpu.roll(mesh[o], 1, 1) + pltpu.roll(mesh[o], 127, 1)
                new[o] = flow[o] + mask[o] * near
            mesh = new
        result.append(mesh[0])
    turned = jnp.concatenate(result + [jnp.zeros((112, 128), F32)], axis=0).T
    for c in range(2):
        for i in range(2):
            at = 64 * c + GYW * i + 8
            out_ref[c, i] = turned[at : at + 8, :15]


def relax(place, arrived):
    return pl.pallas_call(
        relax_kernel,
        out_shape=jax.ShapeDtypeStruct((2, 2, 8, 15), F32),
        in_specs=[
            pl.BlockSpec(memory_space=pltpu.SMEM),
            pl.BlockSpec(memory_space=pltpu.VMEM),
        ],
        out_specs=pl.BlockSpec(memory_space=pltpu.VMEM),
        compiler_params=pltpu.CompilerParams(vmem_limit_bytes=8 * MIB),
    )(place, arrived)


def local(raw_pieces, piece_owner, piece_slot, blend):
    tabs = [jnp.asarray(t) for t in tables()]
    outgoing = send_rows(piece_owner[:, :, 0], piece_slot, blend, raw_pieces)
    arrived = lax.all_to_all(outgoing, "xy", split_axis=0, concat_axis=0, tiled=True)
    first = first_section(arrived)
    back = [(i + 1, i) for i in range(N_SEC - 1)]
    following = lax.ppermute(first, "sec", back)
    spec = spectrum(arrived, tabs[0], tabs[1])
    windows = flow_windows(spec, following, tabs)
    got = lax.all_to_all(windows, ("sec", "xy"), split_axis=0, concat_axis=0, tiled=True)
    place = jnp.stack([lax.axis_index("sec"), lax.axis_index("xy")]).astype(jnp.int32)
    return relax(place, got).transpose(3, 0, 1, 2)


def solution(mesh):
    in_specs = (P("sec", "xy", None), P("sec", "xy", None), P("sec", "xy"), P("sec", "xy"))
    out_specs = P(None, None, "xy", "sec")
    return jax.shard_map(local, mesh=mesh, in_specs=in_specs, out_specs=out_specs, check_vma=False)
```

time: 147 us -> 129 us (0.88)
  Pallas kernels: 34.9 us -> 21.9 us
  local copies, waits for them, and re-layouts: 1.59 us -> 0.02 us
    pallas_call x4, Pallas kernels: 31.7 us -> 19.8 us  [the longest x1 8.21 us: flow_windows(): pl.pallas_call(flow_kernel, out_shape=jax.ShapeDtypeStruct((N_SEC * N_XY,...]
    all_to_all x1, waiting for transfers between devices: 13.1 us -> 11.2 us  [local(): lax.all_to_all(windows, ('sec', 'xy'), split_axis=0, concat_axis=0, tiled...]
    unnamed x4 -> x8, local copies, waits for them, and re-layouts: 1.59 us -> 0.02 us
  transfers between devices with their start and end apart: 2 -> 2, of which waited for: 2 -> 2; matrix products, arithmetic and copies ran while one was open for 0% -> 0% of each run, Pallas kernels for 5% -> 4%
where the time goes in v3:
time: 129 us
  blocking collectives  86.3 us (67%)
  Pallas kernels  21.9 us (17%)
  waiting for transfers between devices  12.8 us (10%)
  starting transfers between devices  7.83 us (6%)
    all_to_all x1, blocking collectives, local(): lax.all_to_all(outgoing, 'xy', split_axis=0, concat_axis=0, tiled=True)  86.3 us
    all_to_all x1, waiting for transfers between devices, local(): lax.all_to_all(windows, ('sec', 'xy'), split_axis=0, concat_axis=0, tiled...  11.2 us
    pallas_call x1, Pallas kernels, flow_windows(): pl.pallas_call(flow_kernel, out_shape=jax.ShapeDtypeStruct((N_SEC * N_XY,...  8.21 us
    pallas_call x1, Pallas kernels, send_rows(): pl.pallas_call(send_kernel, out_shape=jax.ShapeDtypeStruct((N_XY, TILES_O...  5.55 us
    pallas_call x1, Pallas kernels, spectrum(): pl.pallas_call(spectrum_kernel, out_shape=jax.ShapeDtypeStruct((TILES, 25...  5.52 us
    ppermute x1, starting transfers between devices, local(): following = lax.ppermute(first, 'sec', back)  4.24 us
    all_to_all x1, starting transfers between devices, local(): lax.all_to_all(windows, ('sec', 'xy'), split_axis=0, concat_axis=0, tiled...  3.59 us
  transfers between devices with their start and end apart: 2, of which 2 were waited for; matrix products, arithmetic and copies ran while one was open for 0% of the time, Pallas kernels for 4%

profile of v3, /device:TPU:1, one launch (start us, length us, event | category | flops | bytes accessed | tf_op | source)
XLA Modules:
  0.0 128.9 jit_solution(11564654447385986248)
XLA Ops:
  0.0 5.5 %shard_map.82 = bf16[32,97,8,128]{3,2,1,0:T(8,128)(2,1)} custom-call(s32[4,96]{1,0:T(4,128)} %bitcast.4, s32[4,96]{1,0:T(4,128)} %slot_hbm.1, f32[4,96]{1,0:T(4,128)} %blend_hbm.1, bf16[4,96,4096]{2,1,0:T(8,128)(2,1)} %raw_hbm.1), custom_call_target="tpu_custom_call" | custom-call | tf_op jit(solution)/shard_map/pallas_call | solution.py:180
  5.6 86.3 %all_to_all.10.rows_ref = bf16[32,97,8,128]{3,2,1,0:T(8,128)(2,1)S(1)} all-to-all(bf16[32,97,8,128]{3,2,1,0:T(8,128)(2,1)} %shard_map.82), channel_id=1, replica_groups=mesh['sec'=4,'xy'=32] {'xy'}, dimensions={0} | all-to-all | bytes 12713984 | tf_op jit(solution)/shard_map/all_to_all | solution.py:551
  91.8 0.0 copy-start
  91.8 0.0 copy-start.1
  91.8 0.5 shard_map.84
  92.4 0.0 copy-start.2
  92.4 0.0 copy-start.3
  92.4 4.2 %collective-permute-start = (bf16[64,4096]{1,0:T(8,128)(2,1)S(1)}, bf16[64,4096]{1,0:T(8,128)(2,1)S(1)}, u32[]{:S(2)}, u32[]{:S(2)}) collective-permute-start(bf16[64,4096]{1,0:T(8,128)(2,1)S(1)} %shard_map.84), channel_id=1, source_target_pairs={{32,0},{64,32},{96,64},{33,1},{65,33},{97,65},{34,2},{66,34},{98,6... | collective-permute-start | bytes 1572872 | tf_op jit(solution)/shard_map/ppermute | solution.py:554
  96.7 0.0 copy-done
  96.7 0.0 copy-done.1
  96.7 5.5 %shard_map.83.spec_ref = f32[16,256,256]{2,1,0:T(8,128)S(1)} custom-call(bf16[32,97,8,128]{3,2,1,0:T(8,128)(2,1)S(1)} %all_to_all.10.rows_ref, bf16[512,256]{1,0:T(8,128)(2,1)S(1)} %copy-done, bf16[512,256]{1,0:T(8,128)(2,1)S(1)} %copy-done.1), custom_call_target="tpu_custom_call" | custom-call | flops 4294967296 | bytes 12582912 | tf_op jit(solution)/shard_map/pallas_call | solution.py:276
  102.2 1.6 %collective-permute-done.next_ref = bf16[64,4096]{1,0:T(8,128)(2,1)S(1)} collective-permute-done((bf16[64,4096]{1,0:T(8,128)(2,1)S(1)}, bf16[64,4096]{1,0:T(8,128)(2,1)S(1)}, u32[]{:S(2)}, u32[]{:S(2)}) %collective-permute-start) | collective-permute-done | bytes 524320 | tf_op jit(solution)/shard_map/ppermute | solution.py:554
  103.8 0.0 copy-done.2
  103.8 0.0 copy-done.3
  103.8 8.2 %shard_map.85 = f32[128,4,128]{2,1,0:T(4,128)} custom-call(f32[16,256,256]{2,1,0:T(8,128)S(1)} %shard_map.83.spec_ref, bf16[64,4096]{1,0:T(8,128)(2,1)S(1)} %collective-permute-done.next_ref, bf16[512,256]{1,0:T(8,128)(2,1)S(1)} %copy-done, bf16[512,256]{1,0:T(8,128)(2,1)S(1)} %copy-done.1, bf16[512,256]{1,0:T(8,128)(2,1)S(1)} %copy-done.2, ...), custom_call_target="tpu_custom_call" | custom-call | flops 4294967296 | bytes 8388608 | tf_op jit(solution)/shard_map/pallas_call | solution.py:470
  112.0 3.6 %all-to-all-start.1 = ((f32[128,4,128]{2,1,0:T(4,128)}), f32[128,4,128]{2,1,0:T(4,128)S(1)}, u32[]{:S(2)}, u32[]{:S(2)}) async-start(f32[128,4,128]{2,1,0:T(4,128)} %shard_map.85), calls=%async_computation.1 | async-start | bytes 524288 | tf_op jit(solution)/shard_map/all_to_all | solution.py:557
  115.6 0.1 pad_add_fusion.place_ref
  115.7 11.2 %all-to-all-done.1.arrived_ref = f32[128,4,128]{2,1,0:T(4,128)S(1)} async-done(((f32[128,4,128]{2,1,0:T(4,128)}), f32[128,4,128]{2,1,0:T(4,128)S(1)}, u32[]{:S(2)}, u32[]{:S(2)}) %all-to-all-start.1) | async-done | bytes 262176 | tf_op jit(solution)/shard_map/all_to_all | solution.py:557
  126.9 2.1 %shard_map.86 = f32[2,2,8,15]{3,2,1,0:T(8,128)} custom-call(s32[2]{0:T(128)S(1)} %pad_add_fusion.place_ref, f32[128,4,128]{2,1,0:T(4,128)S(1)} %all-to-all-done.1.arrived_ref), custom_call_target="tpu_custom_call" | custom-call | tf_op jit(solution)/shard_map/pallas_call | solution.py:536
Async XLA Ops:
  91.8 4.8 %copy-start = (bf16[512,256]{1,0:T(8,128)(2,1)S(1)}, bf16[512,256]{1,0:T(8,128)(2,1)}, u32[]{:S(2)}) copy-start(bf16[512,256]{1,0:T(8,128)(2,1)} %constant.17.clone.first_ref) | copy-start | bytes 786436
  91.8 4.8 %copy-start.1 = (bf16[512,256]{1,0:T(8,128)(2,1)S(1)}, bf16[512,256]{1,0:T(8,128)(2,1)}, u32[]{:S(2)}) copy-start(bf16[512,256]{1,0:T(8,128)(2,1)} %constant.18.clone.second_ref) | copy-start | bytes 786436
  92.4 11.4 %copy-start.2 = (bf16[512,256]{1,0:T(8,128)(2,1)S(1)}, bf16[512,256]{1,0:T(8,128)(2,1)}, u32[]{:S(2)}) copy-start(bf16[512,256]{1,0:T(8,128)(2,1)} %constant.19.clone.third_ref) | copy-start | bytes 786436
  92.4 11.4 %copy-start.3 = (bf16[512,256]{1,0:T(8,128)(2,1)S(1)}, bf16[512,256]{1,0:T(8,128)(2,1)}, u32[]{:S(2)}) copy-start(bf16[512,256]{1,0:T(8,128)(2,1)} %constant.20.clone.fourth_ref) | copy-start | bytes 786436
  92.4 11.4 %collective-permute-start = (bf16[64,4096]{1,0:T(8,128)(2,1)S(1)}, bf16[64,4096]{1,0:T(8,128)(2,1)S(1)}, u32[]{:S(2)}, u32[]{:S(2)}) collective-permute-start(bf16[64,4096]{1,0:T(8,128)(2,1)S(1)} %shard_map.84), channel_id=1, source_target_pairs={{32,0},{64,32},{96,64},{33,1},{65,33},{97,65},{34,2},{66,34},{98,6... | collective-permute-start | bytes 1572872 | tf_op jit(solution)/shard_map/ppermute | solution.py:554
  112.0 14.9 %all-to-all-start.1 = ((f32[128,4,128]{2,1,0:T(4,128)}), f32[128,4,128]{2,1,0:T(4,128)S(1)}, u32[]{:S(2)}, u32[]{:S(2)}) async-start(f32[128,4,128]{2,1,0:T(4,128)} %shard_map.85), calls=%async_computation.1 | async-start | bytes 524288 | tf_op jit(solution)/shard_map/all_to_all | solution.py:557

commit v4 on v3

--- a/solution.py
+++ b/solution.py
@@ -240,7 +240,93 @@
 GROUPS = TILES // GROUP
 
 
-def spectrum_kernel(rows_ref, first_ref, second_ref, out_ref, place, high, low):
+def sublane_sum(value):
+    total = value[0:8]
+    for row in range(8, value.shape[0], 8):
+        total = total + value[row : row + 8]
+    return total
+
+
+def cross(a, b, first_step):
+    def along_y(p, r):
+        b_sine, b_cosine = b[r, 1], b[r, 0]
+        if first_step is not None:
+            b_sine, b_cosine = (
+                jnp.zeros_like(b_sine) if first_step else b_sine,
+                -b_sine if first_step else b_cosine,
+            )
+        return a[p, 0] * b[r, 0] + a[p, 1] * b_sine, a[p, 0] * b_sine - a[p, 1] * b_cosine
+
+    cc, cs, sc, ss = along_y(0, 0), along_y(0, 1), along_y(1, 0), along_y(1, 1)
+    head = lax.broadcasted_iota(jnp.int32, cc[0].shape, 0) == 0
+    out = {}
+    for part in range(2):
+        out[0, part] = cc[part] + jnp.where(head, 0.0, ss[part])
+        out[1, part] = jnp.where(head, ss[part], cs[part] - sc[part])
+    return out
+
+
+def cross_rows(own, other, first_step):
+    pieces = []
+    for yk in range(2):
+        a, b = (
+            {
+                (x, y): value[yk * 128 + y * 64 + x * 32 : yk * 128 + y * 64 + x * 32 + 32]
+                for x in range(2)
+                for y in range(2)
+            }
+            for value in (own, other)
+        )
+        out = cross(a, b, first_step if yk == 0 else None)
+        pieces += [out[0, 0], out[1, 0], out[0, 1], out[1, 1]]
+    return split(jnp.concatenate(pieces, axis=0))
+
+
+def signed(index):
+    return float((index + 32) % 64 - 32)
+
+
+def down(value):
+    return jnp.sum(value, axis=0, keepdims=True)
+
+
+def flow_sums(operands, third_ref, fourth_ref, back_high, back_low, sums_ref):
+    lanes = 128
+    for q in range(0, TILES, 2):
+        rows = [cross_rows(*operands(q + i), q + i == 0) for i in range(2)]
+        high, low = (jnp.concatenate([rows[0][i], rows[1][i]], axis=1) for i in range(2))
+        high, low = split(mm3(third_ref[...], high, low))
+        for i in range(2):
+            back_high[q + i] = high[:, i * lanes : (i + 1) * lanes]
+            back_low[q + i] = low[:, i * lanes : (i + 1) * lanes]
+    all_d0 = jnp.zeros((64, lanes), F32)
+    weighted = jnp.zeros((8, lanes), F32)
+    for g in range(0, TILES, 2):
+        high, low = (
+            jnp.concatenate(
+                [ref[:, 16 * (g + i) : 16 * (g + i) + 16, :].reshape(256, lanes) for i in range(2)],
+                axis=1,
+            )
+            for ref in (back_high, back_low)
+        )
+        corr = mm3(fourth_ref[...], high, low)
+        power = corr * corr
+        for i in range(2):
+            for d in range(4):
+                block = power[d * 64 : d * 64 + 64, i * lanes : (i + 1) * lanes]
+                all_d0 = all_d0 + block
+                weighted = weighted + sublane_sum(block) * signed((g + i) * 4 + d)
+    index = lax.broadcasted_iota(jnp.int32, (64, lanes), 0)
+    shift = jnp.where(index < 32, index, index - 64).astype(F32)
+    sums_ref[0:1, :] = down(all_d0)
+    sums_ref[1:2, :] = down(weighted)
+    sums_ref[2:3, :] = down(all_d0 * shift)
+
+
+def spectrum_kernel(
+    rows_ref, first_ref, second_ref, third_ref, fourth_ref, own_ref, square_ref, sums_ref,
+    place, high, low, own_first, back_high, back_low,
+):
     ids = row_ids(rows_ref)
     for j in range(PARTS):
         place[j] = places(ids, j, 2 * BLOCK)
@@ -257,44 +343,52 @@
             t = at // TILE + i
             high[t], low[t] = split(both[:256] + both[256:])
 
-    def per_group(group, carry):
-        for i in range(GROUP):
-            q = group * GROUP + i
-            at = pl.ds(pl.multiple_of(16 * q, 16), 16)
-            out_ref[q] = mm3(
-                second_ref[...],
-                high[:, at, :].reshape(256, PATCHES),
-                low[:, at, :].reshape(256, PATCHES),
-            )
-        return carry
-
-    lax.fori_loop(0, GROUPS, per_group, 0)
-    out_ref[0, 0:1, :] = jnp.zeros((1, PATCHES), F32)
-
-
-def spectrum(rows, first, second):
+    square = jnp.zeros((8, PATCHES), F32)
+    for q in range(TILES):
+        at = slice(16 * q, 16 * q + 16)
+        own = mm3(
+            second_ref[...],
+            high[:, at, :].reshape(256, PATCHES),
+            low[:, at, :].reshape(256, PATCHES),
+        )
+        if q == 0:
+            own = jnp.where(lax.broadcasted_iota(jnp.int32, (256, 1), 0) == 0, 0.0, own)
+        square = square + sublane_sum(own * own)
+        own_first[q] = own[:, :128]
+        own_ref[q] = own[:, 128:]
+    square_ref[...] = square
+    left = lax.broadcasted_iota(jnp.int32, (256, 128), 1) < BLOCK
+
+    def operands(q):
+        own, after = own_first[q], own_ref[q]
+        return own, jnp.where(left, pltpu.roll(own, BLOCK, 1), pltpu.roll(after, BLOCK, 1))
+
+    flow_sums(operands, third_ref, fourth_ref, back_high, back_low, sums_ref)
+
+
+def spectrum(rows, tabs):
     return pl.pallas_call(
         spectrum_kernel,
-        out_shape=jax.ShapeDtypeStruct((TILES, 256, PATCHES), F32),
-        in_specs=[VMEM_SPEC] * 3,
-        out_specs=VMEM_SPEC,
+        out_shape=[
+            jax.ShapeDtypeStruct((TILES, 256, 128), F32),
+            jax.ShapeDtypeStruct((8, PATCHES), F32),
+            jax.ShapeDtypeStruct((8, 128), F32),
+        ],
+        in_specs=[VMEM_SPEC] * 5,
+        out_specs=[VMEM_SPEC] * 3,
         scratch_shapes=[
             pltpu.VMEM((PARTS, 2 * BLOCK, 8 * N_XY), BF16),
             pltpu.VMEM((TILES, 256, PATCHES), BF16),
             pltpu.VMEM((TILES, 256, PATCHES), BF16),
+            pltpu.VMEM((TILES, 256, 128), F32),
+            pltpu.VMEM((TILES, 256, 128), BF16),
+            pltpu.VMEM((TILES, 256, 128), BF16),
         ],
-        compiler_params=pltpu.CompilerParams(vmem_limit_bytes=16 * MIB),
+        compiler_params=pltpu.CompilerParams(vmem_limit_bytes=20 * MIB),
         cost_estimate=pl.CostEstimate(
-            flops=2 * TILES * 256 * 256 * 8 * 256, bytes_accessed=12 << 20, transcendentals=0
+            flops=2 * TILES * 256 * 256 * 11 * 256, bytes_accessed=12 << 20, transcendentals=0
         ),
-    )(rows, first, second)
-
-
-def sublane_sum(value):
-    total = value[0:8]
-    for row in range(8, value.shape[0], 8):
-        total = total + value[row : row + 8]
-    return total
+    )(rows, *tabs)
 
 
 def next_spectrum(next_ref, first_ref, second_ref, high, low, follow):
@@ -331,121 +425,37 @@
     follow[0, 0:1, 0:BLOCK] = jnp.zeros((1, BLOCK), F32)
 
 
-def cross(a, b, first_step):
-    def along_y(p, r):
-        b_sine, b_cosine = b[r, 1], b[r, 0]
-        if first_step is not None:
-            b_sine, b_cosine = (
-                jnp.where(first_step, 0.0, b_sine),
-                jnp.where(first_step, -b_sine, b_cosine),
-            )
-        return a[p, 0] * b[r, 0] + a[p, 1] * b_sine, a[p, 0] * b_sine - a[p, 1] * b_cosine
-
-    cc, cs, sc, ss = along_y(0, 0), along_y(0, 1), along_y(1, 0), along_y(1, 1)
-    head = lax.broadcasted_iota(jnp.int32, cc[0].shape, 0) == 0
-    out = {}
-    for part in range(2):
-        out[0, part] = cc[part] + jnp.where(head, 0.0, ss[part])
-        out[1, part] = jnp.where(head, ss[part], cs[part] - sc[part])
-    return out
-
-
 def flow_kernel(
-    spec_ref, next_ref, first_ref, second_ref, third_ref, fourth_ref, out_ref,
-    next_high, next_low, follow, back_high, back_low, square, next_square, sum_y, sum_x,
+    own_ref, square_ref, early_ref, next_ref, first_ref, second_ref, third_ref, fourth_ref, out_ref,
+    next_high, next_low, follow, back_high, back_low, late,
 ):
-    lanes = PATCHES
     next_spectrum(next_ref, first_ref, second_ref, next_high, next_low, follow)
-    square[...] = jnp.zeros_like(square)
     left = lax.broadcasted_iota(jnp.int32, (256, 128), 1) < BLOCK
 
-    def per_group(step, carry):
-        own_total = jnp.zeros((8, lanes), F32)
-        for i in range(GROUP):
-            own = spec_ref[step * GROUP + i]
-            after = follow[step, :, (i // 2) * 128 : (i // 2) * 128 + 128]
-            if i % 2 == 0:
-                after = pltpu.roll(after, BLOCK, 1)
-            low_roll = pltpu.roll(own[:, :128], BLOCK, 1)
-            high_roll = pltpu.roll(own[:, 128:], BLOCK, 1)
-            other = jnp.concatenate(
-                [jnp.where(left, low_roll, high_roll), jnp.where(left, high_roll, after)], axis=1
-            )
-            own_total = own_total + sublane_sum(own * own)
-            pieces = []
-            for yk in range(2):
-                a, b = (
-                    {
-                        (x, y): value[yk * 128 + y * 64 + x * 32 : yk * 128 + y * 64 + x * 32 + 32]
-                        for x in range(2)
-                        for y in range(2)
-                    }
-                    for value in (own, other)
-                )
-                out = cross(a, b, step == 0 if i == 0 and yk == 0 else None)
-                pieces += [out[0, 0], out[1, 0], out[0, 1], out[1, 1]]
-            high, low = split(jnp.concatenate(pieces, axis=0))
-            high, low = split(mm3(third_ref[...], high, low))
-            back_high[step * GROUP + i] = high
-            back_low[step * GROUP + i] = low
-        square[...] += own_total
-        return carry
-
-    lax.fori_loop(0, GROUPS, per_group, 0)
-    after = jnp.zeros((8, lanes), F32)
+    def operands(q):
+        i = q % GROUP
+        own = own_ref[q]
+        after = follow[q // GROUP, :, (i // 2) * 128 : (i // 2) * 128 + 128]
+        if i % 2 == 0:
+            after = pltpu.roll(after, BLOCK, 1)
+        return own, jnp.where(left, pltpu.roll(own, BLOCK, 1), after)
+
+    flow_sums(operands, third_ref, fourth_ref, back_high, back_low, late)
+    after = jnp.zeros((8, 256), F32)
     for g in range(GROUPS):
         after = after + sublane_sum(follow[g] * follow[g])
     after = after[:, :128] + after[:, 128:]
     after = after + pltpu.roll(after, BLOCK, 1)
-    own = square[...]
+    own = square_ref[...]
     low_roll, high_roll = (pltpu.roll(own[:, i : i + 128], BLOCK, 1) for i in (0, 128))
     left = lax.broadcasted_iota(jnp.int32, (8, 128), 1) < BLOCK
-    next_square[...] = jnp.concatenate(
+    other = jnp.concatenate(
         [jnp.where(left, low_roll, high_roll), jnp.where(left, high_roll, after)], axis=1
     )
-    finish(fourth_ref, out_ref, back_high, back_low, square, next_square, sum_y, sum_x)
-
-
-def finish(fourth_ref, out_ref, back_high, back_low, square, next_square, sum_y, sum_x):
-    lanes = PATCHES
-    sum_y[...] = jnp.zeros_like(sum_y)
-    sum_x[...] = jnp.zeros_like(sum_x)
-
-    def per_group(group, carry):
-        all_d0 = jnp.zeros((64, lanes), F32)
-        weighted = jnp.zeros((8, lanes), F32)
-        for i in range(GROUP):
-            g = group * GROUP + i
-            rows = pl.ds(pl.multiple_of(g * 16, 16), 16)
-            corr = mm3(
-                fourth_ref[...],
-                back_high[:, rows, :].reshape(256, lanes),
-                back_low[:, rows, :].reshape(256, lanes),
-            )
-            power = corr * corr
-            for d in range(4):
-                block = power[d * 64 : d * 64 + 64]
-                all_d0 = all_d0 + block
-                index = g * 4 + d
-                shift = jnp.where(index < 32, index, index - 64).astype(F32)
-                weighted = weighted + sublane_sum(block) * shift
-        sum_y[...] += all_d0
-        sum_x[...] += weighted
-        return carry
-
-    lax.fori_loop(0, GROUPS, per_group, 0)
-
-    def down(value):
-        return jnp.sum(value, axis=0, keepdims=True)
-
-    index = lax.broadcasted_iota(jnp.int32, (64, lanes), 0)
-    shift = jnp.where(index < 32, index, index - 64).astype(F32)
-    total = down(sum_y[...])
-    along_x = down(sum_x[...])
-    along_y = down(sum_y[...] * shift)
-    norm = (down(square[...]) * (1.0 / FLAT) + 1e-05) * (
-        down(next_square[...]) * (1.0 / FLAT) + 1e-05
+    total, along_x, along_y = (
+        jnp.concatenate([early_ref[i : i + 1, :], late[i : i + 1, :]], axis=1) for i in range(3)
     )
+    norm = (down(own) * (1.0 / FLAT) + 1e-05) * (down(other) * (1.0 / FLAT) + 1e-05)
     factor = (1.0 / (float(FLAT) * float(FLAT))) / norm
     total = jnp.maximum(total * factor, 0.5)
     tile_rows = []
@@ -466,28 +476,25 @@
             out_ref[j * N_XY + b] = packed
 
 
-def flow_windows(spec, following, tabs):
+def flow_windows(own, square, early, following, tabs):
     return pl.pallas_call(
         flow_kernel,
         out_shape=jax.ShapeDtypeStruct((N_SEC * N_XY, 4, 128), F32),
-        in_specs=[VMEM_SPEC] * 6,
+        in_specs=[VMEM_SPEC] * 8,
         out_specs=VMEM_SPEC,
         scratch_shapes=[
             pltpu.VMEM((GROUPS, 256, 256), BF16),
             pltpu.VMEM((GROUPS, 256, 256), BF16),
             pltpu.VMEM((GROUPS, 256, 256), F32),
-            pltpu.VMEM((TILES, 256, PATCHES), BF16),
-            pltpu.VMEM((TILES, 256, PATCHES), BF16),
-            pltpu.VMEM((8, PATCHES), F32),
-            pltpu.VMEM((8, PATCHES), F32),
-            pltpu.VMEM((64, PATCHES), F32),
-            pltpu.VMEM((8, PATCHES), F32),
+            pltpu.VMEM((TILES, 256, 128), BF16),
+            pltpu.VMEM((TILES, 256, 128), BF16),
+            pltpu.VMEM((8, 128), F32),
         ],
         compiler_params=pltpu.CompilerParams(vmem_limit_bytes=24 * MIB),
         cost_estimate=pl.CostEstimate(
             flops=2 * TILES * 256 * 256 * 8 * 256, bytes_accessed=8 << 20, transcendentals=0
         ),
-    )(spec, following, *tabs)
+    )(own, square, early, following, *tabs)
 
 
 def relax_kernel(place_ref, arrived_ref, out_ref):
@@ -552,8 +559,8 @@
     first = first_section(arrived)
     back = [(i + 1, i) for i in range(N_SEC - 1)]
     following = lax.ppermute(first, "sec", back)
-    spec = spectrum(arrived, tabs[0], tabs[1])
-    windows = flow_windows(spec, following, tabs)
+    own, square, early = spectrum(arrived, tabs)
+    windows = flow_windows(own, square, early, following, tabs)
     got = lax.all_to_all(windows, ("sec", "xy"), split_axis=0, concat_axis=0, tiled=True)
     place = jnp.stack([lax.axis_index("sec"), lax.axis_index("xy")]).astype(jnp.int32)
     return relax(place, got).transpose(3, 0, 1, 2)

time: 129 us -> 125 us (0.969)
  Pallas kernels: 21.9 us -> 19.2 us
  waiting for transfers between devices: 12.8 us -> 11.3 us
    pallas_call x1, Pallas kernels: 8.21 us -> 4.35 us  [flow_windows(): pl.pallas_call(flow_kernel, out_shape=jax.ShapeDtypeStruct((N_SEC * N_XY,...]
    ppermute x1, waiting for transfers between devices: 1.58 us -> 0.07 us  [local(): following = lax.ppermute(first, 'sec', back)]
    pallas_call x1, Pallas kernels: 5.52 us -> 6.83 us  [spectrum(): pl.pallas_call(spectrum_kernel, out_shape=[jax.ShapeDtypeStruct((TILES, 2...]
  transfers between devices with their start and end apart: 2 -> 2, of which waited for: 2 -> 2; matrix products, arithmetic and copies ran while one was open for 0% -> 0% of each run, Pallas kernels for 4% -> 5%
where the time goes in v4:
time: 125 us
  blocking collectives  86.3 us (69%)
  Pallas kernels  19.2 us (15%)
  waiting for transfers between devices  11.3 us (9%)
  starting transfers between devices  7.88 us (6%)
    all_to_all x1, blocking collectives, local(): lax.all_to_all(outgoing, 'xy', split_axis=0, concat_axis=0, tiled=True)  86.3 us
    all_to_all x1, waiting for transfers between devices, local(): lax.all_to_all(windows, ('sec', 'xy'), split_axis=0, concat_axis=0, tiled...  11.2 us
    pallas_call x1, Pallas kernels, spectrum(): pl.pallas_call(spectrum_kernel, out_shape=[jax.ShapeDtypeStruct((TILES, 2...  6.83 us
    pallas_call x1, Pallas kernels, send_rows(): pl.pallas_call(send_kernel, out_shape=jax.ShapeDtypeStruct((N_XY, TILES_O...  5.47 us
    pallas_call x1, Pallas kernels, flow_windows(): pl.pallas_call(flow_kernel, out_shape=jax.ShapeDtypeStruct((N_SEC * N_XY,...  4.35 us
    ppermute x1, starting transfers between devices, local(): following = lax.ppermute(first, 'sec', back)  4.29 us
    all_to_all x1, starting transfers between devices, local(): lax.all_to_all(windows, ('sec', 'xy'), split_axis=0, concat_axis=0, tiled...  3.59 us
  transfers between devices with their start and end apart: 2, of which 2 were waited for; matrix products, arithmetic and copies ran while one was open for 0% of the time, Pallas kernels for 5%

profile of v4, /device:TPU:1, one launch (start us, length us, event | category | flops | bytes accessed | tf_op | source)
XLA Modules:
  0.0 124.8 jit_solution(8680179490396774239)
XLA Ops:
  0.0 5.5 %shard_map.82 = bf16[32,97,8,128]{3,2,1,0:T(8,128)(2,1)} custom-call(s32[4,96]{1,0:T(4,128)} %bitcast.4, s32[4,96]{1,0:T(4,128)} %slot_hbm.1, f32[4,96]{1,0:T(4,128)} %blend_hbm.1, bf16[4,96,4096]{2,1,0:T(8,128)(2,1)} %raw_hbm.1), custom_call_target="tpu_custom_call" | custom-call | tf_op jit(solution)/shard_map/pallas_call | solution.py:180
  5.5 86.3 %all_to_all.10.rows_ref = bf16[32,97,8,128]{3,2,1,0:T(8,128)(2,1)S(1)} all-to-all(bf16[32,97,8,128]{3,2,1,0:T(8,128)(2,1)} %shard_map.82), channel_id=1, replica_groups=mesh['sec'=4,'xy'=32] {'xy'}, dimensions={0} | all-to-all | bytes 12713984 | tf_op jit(solution)/shard_map/all_to_all | solution.py:558
  91.8 0.0 copy-start
  91.8 0.0 copy-start.1
  91.8 0.0 copy-start.2
  91.8 0.0 copy-start.3
  91.8 0.5 shard_map.84
  92.3 4.3 %collective-permute-start = (bf16[64,4096]{1,0:T(8,128)(2,1)S(1)}, bf16[64,4096]{1,0:T(8,128)(2,1)S(1)}, u32[]{:S(2)}, u32[]{:S(2)}) collective-permute-start(bf16[64,4096]{1,0:T(8,128)(2,1)S(1)} %shard_map.84), channel_id=1, source_target_pairs={{32,0},{64,32},{96,64},{33,1},{65,33},{97,65},{34,2},{66,34},{98,6... | collective-permute-start | bytes 1572872 | tf_op jit(solution)/shard_map/ppermute | solution.py:561
  96.6 0.0 copy-done
  96.6 0.0 copy-done.1
  96.6 0.0 copy-done.2
  96.6 0.0 copy-done.3
  96.6 6.8 %shard_map.83 = (f32[16,256,128]{2,1,0:T(8,128)S(1)}, f32[8,256]{1,0:T(8,128)S(1)}, f32[8,128]{1,0:T(8,128)S(1)}) custom-call(bf16[32,97,8,128]{3,2,1,0:T(8,128)(2,1)S(1)} %all_to_all.10.rows_ref, bf16[512,256]{1,0:T(8,128)(2,1)S(1)} %copy-done, bf16[512,256]{1,0:T(8,128)(2,1)S(1)} %copy-done.1, bf16[512,256]{1,0:T(8,128)(2,1)S(1)} %copy-done.2, ...), custom_call_target="tpu_custom_call" | custom-call | flops 5905580032 | bytes 12582912 | tf_op jit(solution)/shard_map/pallas_call | solution.py:370
  103.5 0.1 collective-permute-done.next_ref
  103.6 4.3 %shard_map.85 = f32[128,4,128]{2,1,0:T(4,128)} custom-call(f32[16,256,128]{2,1,0:T(8,128)S(1)} %get-tuple-element.8.own_ref, f32[8,256]{1,0:T(8,128)S(1)} %get-tuple-element.9.square_ref, f32[8,128]{1,0:T(8,128)S(1)} %get-tuple-element.10.early_ref, bf16[64,4096]{1,0:T(8,128)(2,1)S(1)} %collective-permute-done.next_ref, bf16[512,256]{1,0:T(8,128)(2,1)S(1)} %copy-done, ...), custom_call_target="tpu_custom_call" | custom-call | flops 4294967296 | bytes 8388608 | tf_op jit(solution)/shard_map/pallas_call | solution.py:480
  107.9 3.6 %all-to-all-start.1 = ((f32[128,4,128]{2,1,0:T(4,128)}), f32[128,4,128]{2,1,0:T(4,128)S(1)}, u32[]{:S(2)}, u32[]{:S(2)}) async-start(f32[128,4,128]{2,1,0:T(4,128)} %shard_map.85), calls=%async_computation.1 | async-start | bytes 524288 | tf_op jit(solution)/shard_map/all_to_all | solution.py:564
  111.5 0.1 pad_add_fusion.place_ref
  111.6 11.2 %all-to-all-done.1.arrived_ref = f32[128,4,128]{2,1,0:T(4,128)S(1)} async-done(((f32[128,4,128]{2,1,0:T(4,128)}), f32[128,4,128]{2,1,0:T(4,128)S(1)}, u32[]{:S(2)}, u32[]{:S(2)}) %all-to-all-start.1) | async-done | bytes 262176 | tf_op jit(solution)/shard_map/all_to_all | solution.py:564
  122.8 2.1 %shard_map.86 = f32[2,2,8,15]{3,2,1,0:T(8,128)} custom-call(s32[2]{0:T(128)S(1)} %pad_add_fusion.place_ref, f32[128,4,128]{2,1,0:T(4,128)S(1)} %all-to-all-done.1.arrived_ref), custom_call_target="tpu_custom_call" | custom-call | tf_op jit(solution)/shard_map/pallas_call | solution.py:543
Async XLA Ops:
  91.8 4.8 %copy-start = (bf16[512,256]{1,0:T(8,128)(2,1)S(1)}, bf16[512,256]{1,0:T(8,128)(2,1)}, u32[]{:S(2)}) copy-start(bf16[512,256]{1,0:T(8,128)(2,1)} %constant.17.clone.first_ref) | copy-start | bytes 786436
  91.8 4.8 %copy-start.1 = (bf16[512,256]{1,0:T(8,128)(2,1)S(1)}, bf16[512,256]{1,0:T(8,128)(2,1)}, u32[]{:S(2)}) copy-start(bf16[512,256]{1,0:T(8,128)(2,1)} %constant.18.clone.second_ref) | copy-start | bytes 786436
  91.8 4.9 %copy-start.2 = (bf16[512,256]{1,0:T(8,128)(2,1)S(1)}, bf16[512,256]{1,0:T(8,128)(2,1)}, u32[]{:S(2)}) copy-start(bf16[512,256]{1,0:T(8,128)(2,1)} %constant.19.clone.third_ref) | copy-start | bytes 786436
  91.8 4.9 %copy-start.3 = (bf16[512,256]{1,0:T(8,128)(2,1)S(1)}, bf16[512,256]{1,0:T(8,128)(2,1)}, u32[]{:S(2)}) copy-start(bf16[512,256]{1,0:T(8,128)(2,1)} %constant.20.clone.fourth_ref) | copy-start | bytes 786436
  92.3 11.2 %collective-permute-start = (bf16[64,4096]{1,0:T(8,128)(2,1)S(1)}, bf16[64,4096]{1,0:T(8,128)(2,1)S(1)}, u32[]{:S(2)}, u32[]{:S(2)}) collective-permute-start(bf16[64,4096]{1,0:T(8,128)(2,1)S(1)} %shard_map.84), channel_id=1, source_target_pairs={{32,0},{64,32},{96,64},{33,1},{65,33},{97,65},{34,2},{66,34},{98,6... | collective-permute-start | bytes 1572872 | tf_op jit(solution)/shard_map/ppermute | solution.py:561
  107.9 14.9 %all-to-all-start.1 = ((f32[128,4,128]{2,1,0:T(4,128)}), f32[128,4,128]{2,1,0:T(4,128)S(1)}, u32[]{:S(2)}, u32[]{:S(2)}) async-start(f32[128,4,128]{2,1,0:T(4,128)} %shard_map.85), calls=%async_computation.1 | async-start | bytes 524288 | tf_op jit(solution)/shard_map/all_to_all | solution.py:564

commit v5 on v4

--- a/solution.py
+++ b/solution.py
@@ -35,19 +35,15 @@
 NN = (((1,), (0,)), ((), ()))
 
 
-def real_basis(kind):
+def real_basis():
     pos = np.arange(PS)
-    rows = {}
+    rows = np.zeros((2, 32, PS))
     for k in range(32):
         angle = 2.0 * math.pi * ((k * pos) % PS) / PS
-        rows[k, 0] = np.cos(angle)
-        rows[k, 1] = np.sin(angle) if k else np.cos(math.pi * pos)
-    if kind == "forward":
-        for (k, part), row in rows.items():
-            rows[k, part] = row * (math.sqrt(2.0) if k else 1.0) / 8.0
-    x_order = np.stack([rows[k, part] for part in range(2) for k in range(32)])
-    y_order = np.stack([rows[k, part] for k in range(32) for part in range(2)])
-    return x_order, y_order
+        rows[0, k] = np.cos(angle)
+        rows[1, k] = np.sin(angle) if k else np.cos(math.pi * pos)
+        rows[:, k] *= (math.sqrt(2.0) if k else 1.0) / 8.0
+    return rows
 
 
 def split_table(table):
@@ -57,13 +53,19 @@
 
 
 def tables():
-    fwd_x, fwd_y = real_basis("forward")
-    inv_x, inv_y = real_basis("inverse")
-    eye = np.eye(4)
-    first = np.einsum("ab,ky->kaby", eye, fwd_y).reshape(256, 256)
-    second = np.einsum("ab,ktx->aktbx", eye, fwd_x.reshape(64, 16, 4)).reshape(256, 256)
-    third = np.einsum("ab,kd->dabk", eye, inv_x).reshape(256, 256)
-    fourth = np.einsum("ab,qkd->adqbk", eye, inv_y.reshape(16, 4, 64)).reshape(256, 256)
+    basis = real_basis()
+    by_x = basis.reshape(2, 8, 4, PS)
+    by_y = basis.reshape(2, 16, 2, PS)
+    two, four = np.eye(2), np.eye(4)
+    first = np.einsum("ab,pqky->qpkaby", four, by_y).reshape(256, 256)
+    second = np.einsum("pu,kv,cgitb->cgpkituvb", two, two, by_x.reshape(2, 8, 4, 16, 4))
+    second = second.reshape(256, 256)
+    shift = (np.arange(PS) + 32) % PS - 32
+    weigh = np.einsum("pkd,d,rld->pkrl", basis, shift, basis)
+    third = np.einsum("pu,kv,cgidhj->cgpkidhuvj", two, two, weigh.reshape(2, 8, 4, 2, 8, 4))
+    third = third.reshape(256, 256)
+    fourth = np.einsum("ij,pqkurv->qpkiruvj", four, weigh.reshape(2, 16, 2, 2, 16, 2))
+    fourth = fourth.reshape(256, 256)
     return [split_table(t) for t in (first, second, third, fourth)]
 
 
@@ -247,85 +249,115 @@
     return total
 
 
-def cross(a, b, first_step):
+ROOT = math.sqrt(2.0)
+
+
+def cross_rows(own, other, first_step):
+    lanes = own.shape[1]
+    a, b = (value.reshape(2, 8, 2, 8, lanes) for value in (own, other))
+    shape = (8, 8, lanes)
+    line = lax.broadcasted_iota(jnp.int32, shape, 1)
+    head = (lax.broadcasted_iota(jnp.int32, shape, 0) == 0) & ((line == 0) | (line == 4))
+    pair = line < 4
+    if first_step < lanes:
+        pair = pair & (lax.broadcasted_iota(jnp.int32, shape, 2) < first_step)
+
     def along_y(p, r):
-        b_sine, b_cosine = b[r, 1], b[r, 0]
-        if first_step is not None:
-            b_sine, b_cosine = (
-                jnp.zeros_like(b_sine) if first_step else b_sine,
-                -b_sine if first_step else b_cosine,
-            )
-        return a[p, 0] * b[r, 0] + a[p, 1] * b_sine, a[p, 0] * b_sine - a[p, 1] * b_cosine
+        b_cosine, b_sine = b[r, :, 0], b[r, :, 1]
+        if first_step:
+            mixed, b_sine = b_sine, jnp.where(pair, 0.0, b_sine)
+            turned = jnp.where(pair, -mixed, b_cosine)
+        else:
+            turned = b_cosine
+        return (
+            a[p, :, 0] * b_cosine + a[p, :, 1] * b_sine,
+            a[p, :, 0] * b_sine - a[p, :, 1] * turned,
+        )
 
     cc, cs, sc, ss = along_y(0, 0), along_y(0, 1), along_y(1, 0), along_y(1, 1)
-    head = lax.broadcasted_iota(jnp.int32, cc[0].shape, 0) == 0
-    out = {}
-    for part in range(2):
-        out[0, part] = cc[part] + jnp.where(head, 0.0, ss[part])
-        out[1, part] = jnp.where(head, ss[part], cs[part] - sc[part])
-    return out
-
-
-def cross_rows(own, other, first_step):
-    pieces = []
-    for yk in range(2):
-        a, b = (
-            {
-                (x, y): value[yk * 128 + y * 64 + x * 32 : yk * 128 + y * 64 + x * 32 + 32]
-                for x in range(2)
-                for y in range(2)
-            }
-            for value in (own, other)
-        )
-        out = cross(a, b, first_step if yk == 0 else None)
-        pieces += [out[0, 0], out[1, 0], out[0, 1], out[1, 1]]
-    return split(jnp.concatenate(pieces, axis=0))
-
-
-def signed(index):
-    return float((index + 32) % 64 - 32)
+    parts = {}
+    for y in range(2):
+        parts[0, y] = jnp.where(head, ROOT * cc[y], cc[y] + ss[y])
+        parts[1, y] = jnp.where(head, ROOT * ss[y], cs[y] - sc[y])
+        if first_step:
+            for x in range(2):
+                parts[x, y] = jnp.where(pair, ROOT * parts[x, y], parts[x, y])
+    rows = jnp.stack([jnp.stack([parts[x, y] for y in range(2)], axis=1) for x in range(2)])
+    return rows.reshape(256, lanes)
 
 
 def down(value):
     return jnp.sum(value, axis=0, keepdims=True)
 
 
-def flow_sums(operands, third_ref, fourth_ref, back_high, back_low, sums_ref):
+def weighed(table_ref, high):
+    both = mm(table_ref[...], high)
+    return both[:256] + both[256:]
+
+
+def flow_sums(operands, third_ref, fourth_ref, high_ref, twice_ref, sums_ref):
     lanes = 128
+    total = jnp.zeros((8, 2 * lanes), F32)
+    along_x = jnp.zeros((8, 2 * lanes), F32)
+    along_y = jnp.zeros((8, 2 * lanes), F32)
     for q in range(0, TILES, 2):
-        rows = [cross_rows(*operands(q + i), q + i == 0) for i in range(2)]
-        high, low = (jnp.concatenate([rows[0][i], rows[1][i]], axis=1) for i in range(2))
-        high, low = split(mm3(third_ref[...], high, low))
+        rows = jnp.concatenate(
+            [cross_rows(*operands(q + i), 0 if q + i else lanes) for i in range(2)], axis=1
+        )
+        high = rows.astype(BF16)
+        twice = 2.0 * rows - high.astype(F32)
+        total = total + sublane_sum(rows * rows)
+        along_x = along_x + sublane_sum(twice * weighed(third_ref, high))
         for i in range(2):
-            back_high[q + i] = high[:, i * lanes : (i + 1) * lanes]
-            back_low[q + i] = low[:, i * lanes : (i + 1) * lanes]
-    all_d0 = jnp.zeros((64, lanes), F32)
-    weighted = jnp.zeros((8, lanes), F32)
+            high_ref[q + i] = high[:, i * lanes : (i + 1) * lanes]
+            twice_ref[q + i] = twice[:, i * lanes : (i + 1) * lanes]
     for g in range(0, TILES, 2):
-        high, low = (
+        high, twice = (
             jnp.concatenate(
                 [ref[:, 16 * (g + i) : 16 * (g + i) + 16, :].reshape(256, lanes) for i in range(2)],
                 axis=1,
             )
-            for ref in (back_high, back_low)
-        )
-        corr = mm3(fourth_ref[...], high, low)
-        power = corr * corr
-        for i in range(2):
-            for d in range(4):
-                block = power[d * 64 : d * 64 + 64, i * lanes : (i + 1) * lanes]
-                all_d0 = all_d0 + block
-                weighted = weighted + sublane_sum(block) * signed((g + i) * 4 + d)
-    index = lax.broadcasted_iota(jnp.int32, (64, lanes), 0)
-    shift = jnp.where(index < 32, index, index - 64).astype(F32)
-    sums_ref[0:1, :] = down(all_d0)
-    sums_ref[1:2, :] = down(weighted)
-    sums_ref[2:3, :] = down(all_d0 * shift)
+            for ref in (high_ref, twice_ref)
+        )
+        along_y = along_y + sublane_sum(twice * weighed(fourth_ref, high))
+    for i, value in enumerate((total, along_x, along_y)):
+        sums_ref[i : i + 1, :] = down(value[:, :lanes] + value[:, lanes:])
+
+
+def turn(value):
+    return pltpu.roll(value, BLOCK, 1)
+
+
+def flow_sums_packed(operands, third_ref, fourth_ref, turned_ref, sums_ref):
+    total = jnp.zeros((8, 256), F32)
+    along_x = jnp.zeros((8, 256), F32)
+    along_y = jnp.zeros((8, 256), F32)
+    left = lax.broadcasted_iota(jnp.int32, (8, 16, 128), 2) < BLOCK
+    for p in range(0, TILES // 2, 2):
+        pieces = [cross_rows(*operands(p + i), 0 if p + i else BLOCK) for i in range(2)]
+        for i, piece in enumerate(pieces):
+            straight = piece.reshape(8, 2, 16, 128)
+            turned = turn(piece).reshape(8, 2, 16, 128)
+            turned_ref[:, 2 * (p + i)] = jnp.where(left, straight[:, 0], turned[:, 1])
+            turned_ref[:, 2 * (p + i) + 1] = jnp.where(left, turned[:, 0], straight[:, 1])
+        rows = jnp.concatenate(pieces, axis=1)
+        high = rows.astype(BF16)
+        total = total + sublane_sum(rows * rows)
+        twice = 2.0 * rows - high.astype(F32)
+        along_x = along_x + sublane_sum(twice * weighed(third_ref, high))
+    for g in range(0, TILES // 2, 2):
+        rows = jnp.concatenate([turned_ref[g + i].reshape(256, 128) for i in range(2)], axis=1)
+        high = rows.astype(BF16)
+        twice = 2.0 * rows - high.astype(F32)
+        along_y = along_y + sublane_sum(twice * weighed(fourth_ref, high))
+    for i, value in enumerate((total, along_x, along_y)):
+        value = down(value[:, :128] + value[:, 128:])
+        sums_ref[i : i + 1, :] = value + turn(value)
 
 
 def spectrum_kernel(
-    rows_ref, first_ref, second_ref, third_ref, fourth_ref, own_ref, square_ref, sums_ref,
-    place, high, low, own_first, back_high, back_low,
+    rows_ref, first_ref, second_ref, third_ref, fourth_ref, last_ref, square_ref, sums_ref, third_sums_ref,
+    place, high, low, own_first, own_second, high_part, twice_part, turned,
 ):
     ids = row_ids(rows_ref)
     for j in range(PARTS):
@@ -355,36 +387,46 @@
             own = jnp.where(lax.broadcasted_iota(jnp.int32, (256, 1), 0) == 0, 0.0, own)
         square = square + sublane_sum(own * own)
         own_first[q] = own[:, :128]
-        own_ref[q] = own[:, 128:]
+        own_second[q] = own[:, 128:]
     square_ref[...] = square
     left = lax.broadcasted_iota(jnp.int32, (256, 128), 1) < BLOCK
 
     def operands(q):
-        own, after = own_first[q], own_ref[q]
-        return own, jnp.where(left, pltpu.roll(own, BLOCK, 1), pltpu.roll(after, BLOCK, 1))
-
-    flow_sums(operands, third_ref, fourth_ref, back_high, back_low, sums_ref)
+        own = own_first[q]
+        return own, jnp.where(left, turn(own), turn(own_second[q]))
+
+    def packed_operands(p):
+        even, odd = own_second[2 * p], own_second[2 * p + 1]
+        last = jnp.where(left, turn(even), odd)
+        last_ref[p] = last
+        return jnp.where(left, even, turn(odd)), last
+
+    flow_sums(operands, third_ref, fourth_ref, high_part, twice_part, sums_ref)
+    flow_sums_packed(packed_operands, third_ref, fourth_ref, turned, third_sums_ref)
 
 
 def spectrum(rows, tabs):
     return pl.pallas_call(
         spectrum_kernel,
         out_shape=[
-            jax.ShapeDtypeStruct((TILES, 256, 128), F32),
+            jax.ShapeDtypeStruct((TILES // 2, 256, 128), F32),
             jax.ShapeDtypeStruct((8, PATCHES), F32),
+            jax.ShapeDtypeStruct((8, 128), F32),
             jax.ShapeDtypeStruct((8, 128), F32),
         ],
         in_specs=[VMEM_SPEC] * 5,
-        out_specs=[VMEM_SPEC] * 3,
+        out_specs=[VMEM_SPEC] * 4,
         scratch_shapes=[
             pltpu.VMEM((PARTS, 2 * BLOCK, 8 * N_XY), BF16),
             pltpu.VMEM((TILES, 256, PATCHES), BF16),
             pltpu.VMEM((TILES, 256, PATCHES), BF16),
             pltpu.VMEM((TILES, 256, 128), F32),
+            pltpu.VMEM((TILES, 256, 128), F32),
             pltpu.VMEM((TILES, 256, 128), BF16),
-            pltpu.VMEM((TILES, 256, 128), BF16),
+            pltpu.VMEM((TILES, 256, 128), F32),
+            pltpu.VMEM((TILES // 2, TILES, 16, 128), F32),
         ],
-        compiler_params=pltpu.CompilerParams(vmem_limit_bytes=20 * MIB),
+        compiler_params=pltpu.CompilerParams(vmem_limit_bytes=24 * MIB),
         cost_estimate=pl.CostEstimate(
             flops=2 * TILES * 256 * 256 * 11 * 256, bytes_accessed=12 << 20, transcendentals=0
         ),
@@ -426,21 +468,16 @@
 
 
 def flow_kernel(
-    own_ref, square_ref, early_ref, next_ref, first_ref, second_ref, third_ref, fourth_ref, out_ref,
-    next_high, next_low, follow, back_high, back_low, late,
+    last_ref, square_ref, early_ref, third_sums_ref, next_ref,
+    first_ref, second_ref, third_ref, fourth_ref, out_ref,
+    next_high, next_low, follow, turned, late,
 ):
     next_spectrum(next_ref, first_ref, second_ref, next_high, next_low, follow)
-    left = lax.broadcasted_iota(jnp.int32, (256, 128), 1) < BLOCK
-
-    def operands(q):
-        i = q % GROUP
-        own = own_ref[q]
-        after = follow[q // GROUP, :, (i // 2) * 128 : (i // 2) * 128 + 128]
-        if i % 2 == 0:
-            after = pltpu.roll(after, BLOCK, 1)
-        return own, jnp.where(left, pltpu.roll(own, BLOCK, 1), after)
-
-    flow_sums(operands, third_ref, fourth_ref, back_high, back_low, late)
+
+    def operands(p):
+        return last_ref[p], follow[p // 2, :, (p % 2) * 128 : (p % 2) * 128 + 128]
+
+    flow_sums_packed(operands, third_ref, fourth_ref, turned, late)
     after = jnp.zeros((8, 256), F32)
     for g in range(GROUPS):
         after = after + sublane_sum(follow[g] * follow[g])
@@ -452,11 +489,12 @@
     other = jnp.concatenate(
         [jnp.where(left, low_roll, high_roll), jnp.where(left, high_roll, after)], axis=1
     )
+    later = jnp.where(left, third_sums_ref[...], late[...])
     total, along_x, along_y = (
-        jnp.concatenate([early_ref[i : i + 1, :], late[i : i + 1, :]], axis=1) for i in range(3)
+        jnp.concatenate([early_ref[i : i + 1, :], later[i : i + 1, :]], axis=1) for i in range(3)
     )
     norm = (down(own) * (1.0 / FLAT) + 1e-05) * (down(other) * (1.0 / FLAT) + 1e-05)
-    factor = (1.0 / (float(FLAT) * float(FLAT))) / norm
+    factor = (1024.0 / (float(FLAT) * float(FLAT))) / norm
     total = jnp.maximum(total * factor, 0.5)
     tile_rows = []
     for value in (along_x * factor / total, along_y * factor / total):
@@ -476,25 +514,24 @@
             out_ref[j * N_XY + b] = packed
 
 
-def flow_windows(own, square, early, following, tabs):
+def flow_windows(own, following, tabs):
     return pl.pallas_call(
         flow_kernel,
         out_shape=jax.ShapeDtypeStruct((N_SEC * N_XY, 4, 128), F32),
-        in_specs=[VMEM_SPEC] * 8,
+        in_specs=[VMEM_SPEC] * 9,
         out_specs=VMEM_SPEC,
         scratch_shapes=[
             pltpu.VMEM((GROUPS, 256, 256), BF16),
             pltpu.VMEM((GROUPS, 256, 256), BF16),
             pltpu.VMEM((GROUPS, 256, 256), F32),
-            pltpu.VMEM((TILES, 256, 128), BF16),
-            pltpu.VMEM((TILES, 256, 128), BF16),
+            pltpu.VMEM((TILES // 2, TILES, 16, 128), F32),
             pltpu.VMEM((8, 128), F32),
         ],
         compiler_params=pltpu.CompilerParams(vmem_limit_bytes=24 * MIB),
         cost_estimate=pl.CostEstimate(
             flops=2 * TILES * 256 * 256 * 8 * 256, bytes_accessed=8 << 20, transcendentals=0
         ),
-    )(own, square, early, following, *tabs)
+    )(*own, following, *tabs)
 
 
 def relax_kernel(place_ref, arrived_ref, out_ref):
@@ -559,8 +596,8 @@
     first = first_section(arrived)
     back = [(i + 1, i) for i in range(N_SEC - 1)]
     following = lax.ppermute(first, "sec", back)
-    own, square, early = spectrum(arrived, tabs)
-    windows = flow_windows(own, square, early, following, tabs)
+    own = spectrum(arrived, tabs)
+    windows = flow_windows(own, following, tabs)
     got = lax.all_to_all(windows, ("sec", "xy"), split_axis=0, concat_axis=0, tiled=True)
     place = jnp.stack([lax.axis_index("sec"), lax.axis_index("xy")]).astype(jnp.int32)
     return relax(place, got).transpose(3, 0, 1, 2)

time: 125 us -> 124 us (level)
  Pallas kernels: 19.2 us -> 17.9 us
    pallas_call x1, Pallas kernels: 4.35 us -> 2.93 us  [flow_windows(): pl.pallas_call(flow_kernel, out_shape=jax.ShapeDtypeStruct((N_SEC * N_XY,...]
  transfers between devices with their start and end apart: 2 -> 2, of which waited for: 2 -> 2; matrix products, arithmetic and copies ran while one was open for 0% -> 0% of each run, Pallas kernels for 5% -> 6%
where the time goes in v5:
time: 124 us; the launch traced here: 123 us
  blocking collectives  86.3 us (70%)
  Pallas kernels  17.9 us (14%)
  waiting for transfers between devices  11.4 us (9%)
  starting transfers between devices  7.7 us (6%)
    all_to_all x1, blocking collectives, local(): lax.all_to_all(outgoing, 'xy', split_axis=0, concat_axis=0, tiled=True)  86.3 us
    all_to_all x1, waiting for transfers between devices, local(): lax.all_to_all(windows, ('sec', 'xy'), split_axis=0, concat_axis=0, tiled...  11.2 us
    pallas_call x1, Pallas kernels, spectrum(): pl.pallas_call(spectrum_kernel, out_shape=[jax.ShapeDtypeStruct((TILES //...  6.89 us
    pallas_call x1, Pallas kernels, send_rows(): pl.pallas_call(send_kernel, out_shape=jax.ShapeDtypeStruct((N_XY, TILES_O...  5.47 us
    ppermute x1, starting transfers between devices, local(): following = lax.ppermute(first, 'sec', back)  4.11 us
    all_to_all x1, starting transfers between devices, local(): lax.all_to_all(windows, ('sec', 'xy'), split_axis=0, concat_axis=0, tiled...  3.59 us
    pallas_call x1, Pallas kernels, flow_windows(): pl.pallas_call(flow_kernel, out_shape=jax.ShapeDtypeStruct((N_SEC * N_XY,...  2.93 us
  transfers between devices with their start and end apart: 2, of which 2 were waited for; matrix products, arithmetic and copies ran while one was open for 0% of the time, Pallas kernels for 6%

profile of v5, /device:TPU:1, one launch (start us, length us, event | category | flops | bytes accessed | tf_op | source)
XLA Modules:
  0.0 123.4 jit_solution(8033329456137023383)
XLA Ops:
  0.0 5.5 %shard_map.82 = bf16[32,97,8,128]{3,2,1,0:T(8,128)(2,1)} custom-call(s32[4,96]{1,0:T(4,128)} %bitcast.4, s32[4,96]{1,0:T(4,128)} %slot_hbm.1, f32[4,96]{1,0:T(4,128)} %blend_hbm.1, bf16[4,96,4096]{2,1,0:T(8,128)(2,1)} %raw_hbm.1), custom_call_target="tpu_custom_call" | custom-call | tf_op jit(solution)/shard_map/pallas_call | solution.py:182
  5.5 86.3 %all_to_all.10.rows_ref = bf16[32,97,8,128]{3,2,1,0:T(8,128)(2,1)S(1)} all-to-all(bf16[32,97,8,128]{3,2,1,0:T(8,128)(2,1)} %shard_map.82), channel_id=1, replica_groups=mesh['sec'=4,'xy'=32] {'xy'}, dimensions={0} | all-to-all | bytes 12713984 | tf_op jit(solution)/shard_map/all_to_all | solution.py:595
  91.8 0.0 copy-start
  91.8 0.0 copy-start.1
  91.8 0.0 copy-start.2
  91.8 0.0 copy-start.3
  91.8 0.5 shard_map.84
  92.3 4.1 %collective-permute-start = (bf16[64,4096]{1,0:T(8,128)(2,1)S(1)}, bf16[64,4096]{1,0:T(8,128)(2,1)S(1)}, u32[]{:S(2)}, u32[]{:S(2)}) collective-permute-start(bf16[64,4096]{1,0:T(8,128)(2,1)S(1)} %shard_map.84), channel_id=1, source_target_pairs={{32,0},{64,32},{96,64},{33,1},{65,33},{97,65},{34,2},{66,34},{98,6... | collective-permute-start | bytes 1572872 | tf_op jit(solution)/shard_map/ppermute | solution.py:598
  96.4 0.0 copy-done
  96.4 0.0 copy-done.1
  96.4 0.0 copy-done.2
  96.5 0.0 copy-done.3
  96.5 6.9 %shard_map.83 = (f32[8,256,128]{2,1,0:T(8,128)S(1)}, f32[8,256]{1,0:T(8,128)S(1)}, f32[8,128]{1,0:T(8,128)S(1)}, f32[8,128]{1,0:T(8,128)S(1)}) custom-call(bf16[32,97,8,128]{3,2,1,0:T(8,128)(2,1)S(1)} %all_to_all.10.rows_ref, bf16[512,256]{1,0:T(8,128)(2,1)S(1)} %copy-done, bf16[512,256]{1,0:T(8,128)(2,1)S(1)} %copy-done.1, bf16[512,256]{1,0:T(8,128)(2,1)S(1)} %copy-done.2, ...), custom_call_target="tpu_custom_call" | custom-call | flops 5905580032 | bytes 12582912 | tf_op jit(solution)/shard_map/pallas_call | solution.py:409
  103.4 0.2 collective-permute-done.next_ref
  103.6 2.9 %shard_map.85 = f32[128,4,128]{2,1,0:T(4,128)} custom-call(f32[8,256,128]{2,1,0:T(8,128)S(1)} %get-tuple-element.9.last_ref, f32[8,256]{1,0:T(8,128)S(1)} %get-tuple-element.10.square_ref, f32[8,128]{1,0:T(8,128)S(1)} %get-tuple-element.11.early_ref, f32[8,128]{1,0:T(8,128)S(1)} %get-tuple-element.12.third_sums_ref, ...), custom_call_target="tpu_custom_call" | custom-call | flops 4294967296 | bytes 8388608 | tf_op jit(solution)/shard_map/pallas_call | solution.py:518
  106.5 3.6 %all-to-all-start.1 = ((f32[128,4,128]{2,1,0:T(4,128)}), f32[128,4,128]{2,1,0:T(4,128)S(1)}, u32[]{:S(2)}, u32[]{:S(2)}) async-start(f32[128,4,128]{2,1,0:T(4,128)} %shard_map.85), calls=%async_computation.1 | async-start | bytes 524288 | tf_op jit(solution)/shard_map/all_to_all | solution.py:601
  110.1 0.1 pad_add_fusion.place_ref
  110.2 11.2 %all-to-all-done.1.arrived_ref = f32[128,4,128]{2,1,0:T(4,128)S(1)} async-done(((f32[128,4,128]{2,1,0:T(4,128)}), f32[128,4,128]{2,1,0:T(4,128)S(1)}, u32[]{:S(2)}, u32[]{:S(2)}) %all-to-all-start.1) | async-done | bytes 262176 | tf_op jit(solution)/shard_map/all_to_all | solution.py:601
  121.4 2.1 %shard_map.86 = f32[2,2,8,15]{3,2,1,0:T(8,128)} custom-call(s32[2]{0:T(128)S(1)} %pad_add_fusion.place_ref, f32[128,4,128]{2,1,0:T(4,128)S(1)} %all-to-all-done.1.arrived_ref), custom_call_target="tpu_custom_call" | custom-call | tf_op jit(solution)/shard_map/pallas_call | solution.py:580
Async XLA Ops:
  91.8 4.7 %copy-start = (bf16[512,256]{1,0:T(8,128)(2,1)S(1)}, bf16[512,256]{1,0:T(8,128)(2,1)}, u32[]{:S(2)}) copy-start(bf16[512,256]{1,0:T(8,128)(2,1)} %constant.17.clone.first_ref) | copy-start | bytes 786436
  91.8 4.7 %copy-start.1 = (bf16[512,256]{1,0:T(8,128)(2,1)S(1)}, bf16[512,256]{1,0:T(8,128)(2,1)}, u32[]{:S(2)}) copy-start(bf16[512,256]{1,0:T(8,128)(2,1)} %constant.18.clone.second_ref) | copy-start | bytes 786436
  91.8 4.7 %copy-start.2 = (bf16[512,256]{1,0:T(8,128)(2,1)S(1)}, bf16[512,256]{1,0:T(8,128)(2,1)}, u32[]{:S(2)}) copy-start(bf16[512,256]{1,0:T(8,128)(2,1)} %constant.19.clone.third_ref) | copy-start | bytes 786436
  91.8 4.7 %copy-start.3 = (bf16[512,256]{1,0:T(8,128)(2,1)S(1)}, bf16[512,256]{1,0:T(8,128)(2,1)}, u32[]{:S(2)}) copy-start(bf16[512,256]{1,0:T(8,128)(2,1)} %constant.20.clone.fourth_ref) | copy-start | bytes 786436
  92.3 11.3 %collective-permute-start = (bf16[64,4096]{1,0:T(8,128)(2,1)S(1)}, bf16[64,4096]{1,0:T(8,128)(2,1)S(1)}, u32[]{:S(2)}, u32[]{:S(2)}) collective-permute-start(bf16[64,4096]{1,0:T(8,128)(2,1)S(1)} %shard_map.84), channel_id=1, source_target_pairs={{32,0},{64,32},{96,64},{33,1},{65,33},{97,65},{34,2},{66,34},{98,6... | collective-permute-start | bytes 1572872 | tf_op jit(solution)/shard_map/ppermute | solution.py:598
  106.5 14.9 %all-to-all-start.1 = ((f32[128,4,128]{2,1,0:T(4,128)}), f32[128,4,128]{2,1,0:T(4,128)S(1)}, u32[]{:S(2)}, u32[]{:S(2)}) async-start(f32[128,4,128]{2,1,0:T(4,128)} %shard_map.85), calls=%async_computation.1 | async-start | bytes 524288 | tf_op jit(solution)/shard_map/all_to_all | solution.py:601

commit v6 on v5

--- a/solution.py
+++ b/solution.py
@@ -95,6 +95,11 @@
 
 SEND_LANES = 1024
 SENDS = FLAT // SEND_LANES
+SEND_TILES = SEND_LANES // 128
+
+
+def tile_of(part, lane_tile):
+    return (lane_tile // SEND_TILES * PARTS + part) * SEND_TILES + lane_tile % SEND_TILES
 
 
 def send_kernel(
@@ -116,17 +121,18 @@
         )
         for i in range(SENDS)
     ]
-    for copy in large:
-        copy.start()
+    large[0].start()
     for s in range(SEC_DEV):
         for i in range(SENDS):
             warped[i, 128 * s + PIECES : 128 * s + 128, :] = jnp.zeros((32, SEND_LANES), BF16)
     line = lax.broadcasted_iota(jnp.int32, (128, 128), 0)
     lane = lax.broadcasted_iota(jnp.int32, (128, 128), 1)
+    lane_id = lax.broadcasted_iota(jnp.int32, (8 * N_XY, 128), 1)
     rows = lax.broadcasted_iota(jnp.int32, (8 * N_XY, 128), 0)
     rows = (rows // 8) * CHUNK + rows % 8
     for copy in small:
         copy.wait()
+    large[1].start()
     owners = lane_rows(lanes, owner_ref)
     slot_rows = lane_rows(lanes, slot_ref)
     blend_rows = lane_rows(lanes, blend_ref)
@@ -144,17 +150,15 @@
         blend[at, :] = column(blend_rows[s : s + 1])
         slots[at, :] = (column(slot_rows[s : s + 1]) + float(s * BLOCK + 1)).astype(BF16)
 
+    ids = [mm(select[j], slots[128 * j : 128 * j + 256, :]) for j in range(PARTS)]
+    ids = jnp.where(lane_id == 0, ids[0], jnp.where(lane_id == 1, ids[1], ids[2]))
+    out_ref[:, TILES_OUT - 1] = ids.reshape(N_XY, 8, 128).astype(BF16)
     copies = []
-
-    def send_tiles(first, count):
-        at = pl.ds(first, count)
-        copies.append(
-            pltpu.make_async_copy(out_ref.at[:, at], out_hbm.at[:, at], out_sems.at[len(copies)])
-        )
-        copies[-1].start()
-
     for i in range(SENDS):
         large[i].wait()
+        if i == 0:
+            large[2].start()
+            large[3].start()
         for s in range(SEC_DEV):
             at = slice(128 * s, 128 * s + PIECES)
             scale = blend[at, :]
@@ -163,16 +167,12 @@
                 warped[i, at, to] = (raw_ref[i, s, :, to].astype(F32) * scale).astype(BF16)
         for j in range(PARTS):
             value = mm(select[j], warped[i, 128 * j : 128 * j + 256, :])
-            first = LANE_TILES * j + i * (SEND_LANES // 128)
-            for tile in range(SEND_LANES // 128):
+            for tile in range(SEND_TILES):
                 piece = value[:, tile * 128 : tile * 128 + 128].reshape(N_XY, 8, 128)
-                out_ref[:, first + tile] = piece.astype(BF16)
-            send_tiles(first, SEND_LANES // 128)
-    ids = [mm(select[j], slots[128 * j : 128 * j + 256, :]) for j in range(PARTS)]
-    lane = lax.broadcasted_iota(jnp.int32, (8 * N_XY, 128), 1)
-    ids = jnp.where(lane == 0, ids[0], jnp.where(lane == 1, ids[1], ids[2]))
-    out_ref[:, TILES_OUT - 1] = ids.reshape(N_XY, 8, 128).astype(BF16)
-    send_tiles(TILES_OUT - 1, 1)
+                out_ref[:, tile_of(j, i * SEND_TILES + tile)] = piece.astype(BF16)
+        at = pl.ds(i * PARTS * SEND_TILES, PARTS * SEND_TILES + (i == SENDS - 1))
+        copies.append(pltpu.make_async_copy(out_ref.at[:, at], out_hbm.at[:, at], out_sems.at[i]))
+        copies[i].start()
     for copy in copies:
         copy.wait()
 
@@ -197,7 +197,7 @@
             pltpu.VMEM((N_XY, TILES_OUT, 8, 128), BF16),
             pltpu.SemaphoreType.DMA((3,)),
             pltpu.SemaphoreType.DMA((SENDS,)),
-            pltpu.SemaphoreType.DMA((SENDS * PARTS + 1,)),
+            pltpu.SemaphoreType.DMA((SENDS,)),
         ],
         compiler_params=pltpu.CompilerParams(vmem_limit_bytes=60 * MIB),
     )(owner, slot, blend, raw)
@@ -214,9 +214,13 @@
 
 
 def row_tiles(rows_ref, part, lane, size):
-    first = LANE_TILES * part + lane // 128
+    first = lane // 128
     return jnp.concatenate(
-        [rows_ref[:, first + tile].reshape(8 * N_XY, 128) for tile in range(size // 128)], axis=1
+        [
+            rows_ref[:, tile_of(part, first + tile)].reshape(8 * N_XY, 128)
+            for tile in range(size // 128)
+        ],
+        axis=1,
     )
 
 
@@ -534,8 +538,8 @@
     )(*own, following, *tabs)
 
 
-def relax_kernel(place_ref, arrived_ref, out_ref):
-    column, block = place_ref[0], place_ref[1]
+def relax_kernel(arrived_ref, out_ref):
+    column, block = lax.axis_index("sec"), lax.axis_index("xy")
     lane = lax.broadcasted_iota(jnp.int32, (8, 128), 1)
     lane = jnp.where(lane < 64, lane, lane - 64)
     top = lane < GYW
@@ -576,17 +580,14 @@
             out_ref[c, i] = turned[at : at + 8, :15]
 
 
-def relax(place, arrived):
+def relax(arrived):
     return pl.pallas_call(
         relax_kernel,
         out_shape=jax.ShapeDtypeStruct((2, 2, 8, 15), F32),
-        in_specs=[
-            pl.BlockSpec(memory_space=pltpu.SMEM),
-            pl.BlockSpec(memory_space=pltpu.VMEM),
-        ],
+        in_specs=[VMEM_SPEC],
         out_specs=pl.BlockSpec(memory_space=pltpu.VMEM),
         compiler_params=pltpu.CompilerParams(vmem_limit_bytes=8 * MIB),
-    )(place, arrived)
+    )(arrived)
 
 
 def local(raw_pieces, piece_owner, piece_slot, blend):
@@ -599,8 +600,7 @@
     own = spectrum(arrived, tabs)
     windows = flow_windows(own, following, tabs)
     got = lax.all_to_all(windows, ("sec", "xy"), split_axis=0, concat_axis=0, tiled=True)
-    place = jnp.stack([lax.axis_index("sec"), lax.axis_index("xy")]).astype(jnp.int32)
-    return relax(place, got).transpose(3, 0, 1, 2)
+    return relax(got).transpose(3, 0, 1, 2)
 
 
 def solution(mesh):

time: 124 us -> 122 us (0.984)
  blocking collectives: 86.3 us -> 101 us
  waiting for transfers between devices: 11.4 us -> 0.2 us
  starting transfers between devices: 7.7 us -> 4.11 us
  Pallas kernels: 17.9 us -> 16.3 us
    all_to_all x0 -> x1, blocking collectives: none -> 14.7 us  [local(): lax.all_to_all(windows, ('sec', 'xy'), split_axis=0, concat_axis=0, tiled...]
    all_to_all x1 -> x0, waiting for transfers between devices: 11.2 us -> none  [local(): lax.all_to_all(windows, ('sec', 'xy'), split_axis=0, concat_axis=0, tiled...]
    all_to_all x1 -> x0, starting transfers between devices: 3.59 us -> none  [local(): lax.all_to_all(windows, ('sec', 'xy'), split_axis=0, concat_axis=0, tiled...]
  transfers between devices with their start and end apart: 2 -> 1, of which waited for: 2 -> 1; matrix products, arithmetic and copies ran while one was open for 0% -> 0% of each run, Pallas kernels for 6% -> 6%
where the time goes in v6:
time: 122 us
  blocking collectives  101 us (83%)
  Pallas kernels  16.3 us (13%)
  starting transfers between devices  4.11 us (3%)
    all_to_all x1, blocking collectives, local(): lax.all_to_all(outgoing, 'xy', split_axis=0, concat_axis=0, tiled=True)  86.3 us
    all_to_all x1, blocking collectives, local(): lax.all_to_all(windows, ('sec', 'xy'), split_axis=0, concat_axis=0, tiled...  14.7 us
    pallas_call x1, Pallas kernels, spectrum(): pl.pallas_call(spectrum_kernel, out_shape=[jax.ShapeDtypeStruct((TILES //...  6.89 us
    pallas_call x1, Pallas kernels, send_rows(): pl.pallas_call(send_kernel, out_shape=jax.ShapeDtypeStruct((N_XY, TILES_O...  5.12 us
    ppermute x1, starting transfers between devices, local(): following = lax.ppermute(first, 'sec', back)  4.11 us
  transfers between devices with their start and end apart: 1, of which 1 were waited for; matrix products, arithmetic and copies ran while one was open for 0% of the time, Pallas kernels for 6%

profile of v6, /device:TPU:1, one launch (start us, length us, event | category | flops | bytes accessed | tf_op | source)
XLA Modules:
  0.0 121.6 jit_solution(13274093857165341942)
XLA Ops:
  0.0 5.1 %shard_map.82 = bf16[32,97,8,128]{3,2,1,0:T(8,128)(2,1)} custom-call(s32[4,96]{1,0:T(4,128)} %bitcast.2, s32[4,96]{1,0:T(4,128)} %slot_hbm.1, f32[4,96]{1,0:T(4,128)} %blend_hbm.1, bf16[4,96,4096]{2,1,0:T(8,128)(2,1)} %raw_hbm.1), custom_call_target="tpu_custom_call" | custom-call | tf_op jit(solution)/shard_map/pallas_call | solution.py:182
  5.1 86.3 %all_to_all.10.rows_ref = bf16[32,97,8,128]{3,2,1,0:T(8,128)(2,1)S(1)} all-to-all(bf16[32,97,8,128]{3,2,1,0:T(8,128)(2,1)} %shard_map.82), channel_id=1, replica_groups=mesh['sec'=4,'xy'=32] {'xy'}, dimensions={0} | all-to-all | bytes 12713984 | tf_op jit(solution)/shard_map/all_to_all | solution.py:596
  91.4 0.0 copy-start
  91.4 0.0 copy-start.1
  91.4 0.0 copy-start.2
  91.4 0.0 copy-start.3
  91.4 0.5 shard_map.84
  92.0 4.1 %collective-permute-start = (bf16[64,4096]{1,0:T(8,128)(2,1)S(1)}, bf16[64,4096]{1,0:T(8,128)(2,1)S(1)}, u32[]{:S(2)}, u32[]{:S(2)}) collective-permute-start(bf16[64,4096]{1,0:T(8,128)(2,1)S(1)} %shard_map.84), channel_id=1, source_target_pairs={{32,0},{64,32},{96,64},{33,1},{65,33},{97,65},{34,2},{66,34},{98,6... | collective-permute-start | bytes 1572872 | tf_op jit(solution)/shard_map/ppermute | solution.py:599
  96.1 0.0 copy-done
  96.1 0.0 copy-done.1
  96.1 0.0 copy-done.2
  96.1 0.0 copy-done.3
  96.1 6.9 %shard_map.83 = (f32[8,256,128]{2,1,0:T(8,128)S(1)}, f32[8,256]{1,0:T(8,128)S(1)}, f32[8,128]{1,0:T(8,128)S(1)}, f32[8,128]{1,0:T(8,128)S(1)}) custom-call(bf16[32,97,8,128]{3,2,1,0:T(8,128)(2,1)S(1)} %all_to_all.10.rows_ref, bf16[512,256]{1,0:T(8,128)(2,1)S(1)} %copy-done.3, bf16[512,256]{1,0:T(8,128)(2,1)S(1)} %copy-done.2, ...), custom_call_target="tpu_custom_call" | custom-call | flops 5905580032 | bytes 12582912 | tf_op jit(solution)/shard_map/pallas_call | solution.py:413
  103.0 0.2 collective-permute-done.next_ref
  103.2 2.2 %shard_map.85 = f32[128,4,128]{2,1,0:T(4,128)S(1)} custom-call(f32[8,256,128]{2,1,0:T(8,128)S(1)} %get-tuple-element.9.last_ref, f32[8,256]{1,0:T(8,128)S(1)} %get-tuple-element.10.square_ref, f32[8,128]{1,0:T(8,128)S(1)} %get-tuple-element.11.early_ref, f32[8,128]{1,0:T(8,128)S(1)} %get-tuple-element.12.third_sums_ref, ...), custom_call_target="tpu_custom_call" | custom-call | flops 4294967296 | bytes 8388608 | tf_op jit(solution)/shard_map/pallas_call | solution.py:522
  105.5 14.7 %all_to_all.11.arrived_ref = f32[128,4,128]{2,1,0:T(4,128)S(1)} all-to-all(f32[128,4,128]{2,1,0:T(4,128)S(1)} %shard_map.85), channel_id=1, replica_groups=mesh['sec'=4,'xy'=32] {'sec','xy'}, dimensions={0} | all-to-all | bytes 524288 | tf_op jit(solution)/shard_map/all_to_all | solution.py:602
  120.1 1.5 %shard_map.86 = f32[2,2,8,15]{3,2,1,0:T(8,128)} custom-call(f32[128,4,128]{2,1,0:T(4,128)S(1)} %all_to_all.11.arrived_ref), custom_call_target="tpu_custom_call" | custom-call | tf_op jit(solution)/shard_map/pallas_call | solution.py:584
Async XLA Ops:
  91.4 4.7 %copy-start = (bf16[512,256]{1,0:T(8,128)(2,1)S(1)}, bf16[512,256]{1,0:T(8,128)(2,1)}, u32[]{:S(2)}) copy-start(bf16[512,256]{1,0:T(8,128)(2,1)} %constant.11.clone.fourth_ref) | copy-start | bytes 786436
  91.4 4.7 %copy-start.1 = (bf16[512,256]{1,0:T(8,128)(2,1)S(1)}, bf16[512,256]{1,0:T(8,128)(2,1)}, u32[]{:S(2)}) copy-start(bf16[512,256]{1,0:T(8,128)(2,1)} %constant.10.clone.third_ref) | copy-start | bytes 786436
  91.4 4.7 %copy-start.2 = (bf16[512,256]{1,0:T(8,128)(2,1)S(1)}, bf16[512,256]{1,0:T(8,128)(2,1)}, u32[]{:S(2)}) copy-start(bf16[512,256]{1,0:T(8,128)(2,1)} %constant.9.clone.second_ref) | copy-start | bytes 786436
  91.4 4.7 %copy-start.3 = (bf16[512,256]{1,0:T(8,128)(2,1)S(1)}, bf16[512,256]{1,0:T(8,128)(2,1)}, u32[]{:S(2)}) copy-start(bf16[512,256]{1,0:T(8,128)(2,1)} %constant.8.clone.first_ref) | copy-start | bytes 786436
  92.0 11.3 %collective-permute-start = (bf16[64,4096]{1,0:T(8,128)(2,1)S(1)}, bf16[64,4096]{1,0:T(8,128)(2,1)S(1)}, u32[]{:S(2)}, u32[]{:S(2)}) collective-permute-start(bf16[64,4096]{1,0:T(8,128)(2,1)S(1)} %shard_map.84), channel_id=1, source_target_pairs={{32,0},{64,32},{96,64},{33,1},{65,33},{97,65},{34,2},{66,34},{98,6... | collective-permute-start | bytes 1572872 | tf_op jit(solution)/shard_map/ppermute | solution.py:599

commit v7 on v6

--- a/solution.py
+++ b/solution.py
@@ -366,7 +366,7 @@
     ids = row_ids(rows_ref)
     for j in range(PARTS):
         place[j] = places(ids, j, 2 * BLOCK)
-    wide = 2 * TILE
+    wide = 8 * TILE
     for at in range(0, FLAT, wide):
         pieces, before = [], None
         for j in range(PARTS):
@@ -374,7 +374,7 @@
             pieces.append(value[:BLOCK] if before is None else before + value[:BLOCK])
             before = value[BLOCK:]
         patches = jnp.concatenate(pieces + [before], axis=0).astype(BF16)
-        for i in range(2):
+        for i in range(wide // TILE):
             both = mm(first_ref[...], patches[:, i * TILE : (i + 1) * TILE], NT)
             t = at // TILE + i
             high[t], low[t] = split(both[:256] + both[256:])

time: 122 us -> 122 us (level)
  transfers between devices with their start and end apart: 1 -> 1, of which waited for: 1 -> 1; matrix products, arithmetic and copies ran while one was open for 0% -> 0% of each run, Pallas kernels for 6% -> 5%
where the time goes in v7:
time: 122 us
  blocking collectives  101 us (83%)
  Pallas kernels  15.4 us (13%)
  starting transfers between devices  4.11 us (3%)
    all_to_all x1, blocking collectives, local(): lax.all_to_all(outgoing, 'xy', split_axis=0, concat_axis=0, tiled=True)  86.3 us
    all_to_all x1, blocking collectives, local(): lax.all_to_all(windows, ('sec', 'xy'), split_axis=0, concat_axis=0, tiled...  14.7 us
    pallas_call x1, Pallas kernels, spectrum(): pl.pallas_call(spectrum_kernel, out_shape=[jax.ShapeDtypeStruct((TILES //...  5.96 us
    pallas_call x1, Pallas kernels, send_rows(): pl.pallas_call(send_kernel, out_shape=jax.ShapeDtypeStruct((N_XY, TILES_O...  5.12 us
    ppermute x1, starting transfers between devices, local(): following = lax.ppermute(first, 'sec', back)  4.11 us
  transfers between devices with their start and end apart: 1, of which 1 were waited for; matrix products, arithmetic and copies ran while one was open for 0% of the time, Pallas kernels for 5%

profile of v7, /device:TPU:1, one launch (start us, length us, event | category | flops | bytes accessed | tf_op | source)
XLA Modules:
  0.0 121.6 jit_solution(13127990573471825571)
XLA Ops:
  0.0 5.1 %shard_map.82 = bf16[32,97,8,128]{3,2,1,0:T(8,128)(2,1)} custom-call(s32[4,96]{1,0:T(4,128)} %bitcast.2, s32[4,96]{1,0:T(4,128)} %slot_hbm.1, f32[4,96]{1,0:T(4,128)} %blend_hbm.1, bf16[4,96,4096]{2,1,0:T(8,128)(2,1)} %raw_hbm.1), custom_call_target="tpu_custom_call" | custom-call | tf_op jit(solution)/shard_map/pallas_call | solution.py:182
  5.1 86.3 %all_to_all.10.rows_ref = bf16[32,97,8,128]{3,2,1,0:T(8,128)(2,1)S(1)} all-to-all(bf16[32,97,8,128]{3,2,1,0:T(8,128)(2,1)} %shard_map.82), channel_id=1, replica_groups=mesh['sec'=4,'xy'=32] {'xy'}, dimensions={0} | all-to-all | bytes 12713984 | tf_op jit(solution)/shard_map/all_to_all | solution.py:596
  91.4 0.0 copy-start
  91.4 0.0 copy-start.1
  91.4 0.0 copy-start.2
  91.4 0.0 copy-start.3
  91.4 0.5 shard_map.84
  92.0 4.1 %collective-permute-start = (bf16[64,4096]{1,0:T(8,128)(2,1)S(1)}, bf16[64,4096]{1,0:T(8,128)(2,1)S(1)}, u32[]{:S(2)}, u32[]{:S(2)}) collective-permute-start(bf16[64,4096]{1,0:T(8,128)(2,1)S(1)} %shard_map.84), channel_id=1, source_target_pairs={{32,0},{64,32},{96,64},{33,1},{65,33},{97,65},{34,2},{66,34},{98,6... | collective-permute-start | bytes 1572872 | tf_op jit(solution)/shard_map/ppermute | solution.py:599
  96.1 0.0 copy-done
  96.1 0.0 copy-done.1
  96.1 0.0 copy-done.2
  96.1 0.0 copy-done.3
  96.1 6.0 %shard_map.83 = (f32[8,256,128]{2,1,0:T(8,128)S(1)}, f32[8,256]{1,0:T(8,128)S(1)}, f32[8,128]{1,0:T(8,128)S(1)}, f32[8,128]{1,0:T(8,128)S(1)}) custom-call(bf16[32,97,8,128]{3,2,1,0:T(8,128)(2,1)S(1)} %all_to_all.10.rows_ref, bf16[512,256]{1,0:T(8,128)(2,1)S(1)} %copy-done.3, bf16[512,256]{1,0:T(8,128)(2,1)S(1)} %copy-done.2, ...), custom_call_target="tpu_custom_call" | custom-call | flops 5905580032 | bytes 12582912 | tf_op jit(solution)/shard_map/pallas_call | solution.py:413
  102.1 1.1 collective-permute-done.next_ref
  103.2 2.2 %shard_map.85 = f32[128,4,128]{2,1,0:T(4,128)S(1)} custom-call(f32[8,256,128]{2,1,0:T(8,128)S(1)} %get-tuple-element.9.last_ref, f32[8,256]{1,0:T(8,128)S(1)} %get-tuple-element.10.square_ref, f32[8,128]{1,0:T(8,128)S(1)} %get-tuple-element.11.early_ref, f32[8,128]{1,0:T(8,128)S(1)} %get-tuple-element.12.third_sums_ref, ...), custom_call_target="tpu_custom_call" | custom-call | flops 4294967296 | bytes 8388608 | tf_op jit(solution)/shard_map/pallas_call | solution.py:522
  105.5 14.7 %all_to_all.11.arrived_ref = f32[128,4,128]{2,1,0:T(4,128)S(1)} all-to-all(f32[128,4,128]{2,1,0:T(4,128)S(1)} %shard_map.85), channel_id=1, replica_groups=mesh['sec'=4,'xy'=32] {'sec','xy'}, dimensions={0} | all-to-all | bytes 524288 | tf_op jit(solution)/shard_map/all_to_all | solution.py:602
  120.1 1.5 %shard_map.86 = f32[2,2,8,15]{3,2,1,0:T(8,128)} custom-call(f32[128,4,128]{2,1,0:T(4,128)S(1)} %all_to_all.11.arrived_ref), custom_call_target="tpu_custom_call" | custom-call | tf_op jit(solution)/shard_map/pallas_call | solution.py:584
Async XLA Ops:
  91.4 4.7 %copy-start = (bf16[512,256]{1,0:T(8,128)(2,1)S(1)}, bf16[512,256]{1,0:T(8,128)(2,1)}, u32[]{:S(2)}) copy-start(bf16[512,256]{1,0:T(8,128)(2,1)} %constant.11.clone.fourth_ref) | copy-start | bytes 786436
  91.4 4.7 %copy-start.1 = (bf16[512,256]{1,0:T(8,128)(2,1)S(1)}, bf16[512,256]{1,0:T(8,128)(2,1)}, u32[]{:S(2)}) copy-start(bf16[512,256]{1,0:T(8,128)(2,1)} %constant.10.clone.third_ref) | copy-start | bytes 786436
  91.4 4.7 %copy-start.2 = (bf16[512,256]{1,0:T(8,128)(2,1)S(1)}, bf16[512,256]{1,0:T(8,128)(2,1)}, u32[]{:S(2)}) copy-start(bf16[512,256]{1,0:T(8,128)(2,1)} %constant.9.clone.second_ref) | copy-start | bytes 786436
  91.4 4.7 %copy-start.3 = (bf16[512,256]{1,0:T(8,128)(2,1)S(1)}, bf16[512,256]{1,0:T(8,128)(2,1)}, u32[]{:S(2)}) copy-start(bf16[512,256]{1,0:T(8,128)(2,1)} %constant.8.clone.first_ref) | copy-start | bytes 786436
  92.0 11.3 %collective-permute-start = (bf16[64,4096]{1,0:T(8,128)(2,1)S(1)}, bf16[64,4096]{1,0:T(8,128)(2,1)S(1)}, u32[]{:S(2)}, u32[]{:S(2)}) collective-permute-start(bf16[64,4096]{1,0:T(8,128)(2,1)S(1)} %shard_map.84), channel_id=1, source_target_pairs={{32,0},{64,32},{96,64},{33,1},{65,33},{97,65},{34,2},{66,34},{98,6... | collective-permute-start | bytes 1572872 | tf_op jit(solution)/shard_map/ppermute | solution.py:599

commit v8 on v7

--- a/solution.py
+++ b/solution.py
@@ -154,6 +154,14 @@
     ids = jnp.where(lane_id == 0, ids[0], jnp.where(lane_id == 1, ids[1], ids[2]))
     out_ref[:, TILES_OUT - 1] = ids.reshape(N_XY, 8, 128).astype(BF16)
     copies = []
+
+    def leave(first, count):
+        at = pl.ds(first, count)
+        copies.append(
+            pltpu.make_async_copy(out_ref.at[:, at], out_hbm.at[:, at], out_sems.at[len(copies)])
+        )
+        copies[-1].start()
+
     for i in range(SENDS):
         large[i].wait()
         if i == 0:
@@ -170,9 +178,10 @@
             for tile in range(SEND_TILES):
                 piece = value[:, tile * 128 : tile * 128 + 128].reshape(N_XY, 8, 128)
                 out_ref[:, tile_of(j, i * SEND_TILES + tile)] = piece.astype(BF16)
-        at = pl.ds(i * PARTS * SEND_TILES, PARTS * SEND_TILES + (i == SENDS - 1))
-        copies.append(pltpu.make_async_copy(out_ref.at[:, at], out_hbm.at[:, at], out_sems.at[i]))
-        copies[i].start()
+            if i == SENDS - 1:
+                leave((i * PARTS + j) * SEND_TILES, SEND_TILES + (j == PARTS - 1))
+        if i < SENDS - 1:
+            leave(i * PARTS * SEND_TILES, PARTS * SEND_TILES)
     for copy in copies:
         copy.wait()
 
@@ -197,7 +206,7 @@
             pltpu.VMEM((N_XY, TILES_OUT, 8, 128), BF16),
             pltpu.SemaphoreType.DMA((3,)),
             pltpu.SemaphoreType.DMA((SENDS,)),
-            pltpu.SemaphoreType.DMA((SENDS,)),
+            pltpu.SemaphoreType.DMA((SENDS + PARTS - 1,)),
         ],
         compiler_params=pltpu.CompilerParams(vmem_limit_bytes=60 * MIB),
     )(owner, slot, blend, raw)

time: 122 us -> 122 us (level)
  no operation moved by 1% of the time
where the time goes in v8:
time: 122 us; the launch traced here: 121 us
  blocking collectives  101 us (83%)
  Pallas kernels  15.2 us (12%)
  starting transfers between devices  4.11 us (3%)
    all_to_all x1, blocking collectives, local(): lax.all_to_all(outgoing, 'xy', split_axis=0, concat_axis=0, tiled=True)  86.3 us
    all_to_all x1, blocking collectives, local(): lax.all_to_all(windows, ('sec', 'xy'), split_axis=0, concat_axis=0, tiled...  14.7 us
    pallas_call x1, Pallas kernels, spectrum(): pl.pallas_call(spectrum_kernel, out_shape=[jax.ShapeDtypeStruct((TILES //...  5.96 us
    pallas_call x1, Pallas kernels, send_rows(): pl.pallas_call(send_kernel, out_shape=jax.ShapeDtypeStruct((N_XY, TILES_O...  4.96 us
    ppermute x1, starting transfers between devices, local(): following = lax.ppermute(first, 'sec', back)  4.11 us
  transfers between devices with their start and end apart: 1, of which 1 were waited for; matrix products, arithmetic and copies ran while one was open for 0% of the time, Pallas kernels for 5%

profile of v8, /device:TPU:1, one launch (start us, length us, event | category | flops | bytes accessed | tf_op | source)
XLA Modules:
  0.0 121.5 jit_solution(15937016831740005474)
XLA Ops:
  0.0 5.0 %shard_map.82 = bf16[32,97,8,128]{3,2,1,0:T(8,128)(2,1)} custom-call(s32[4,96]{1,0:T(4,128)} %bitcast.2, s32[4,96]{1,0:T(4,128)} %slot_hbm.1, f32[4,96]{1,0:T(4,128)} %blend_hbm.1, bf16[4,96,4096]{2,1,0:T(8,128)(2,1)} %raw_hbm.1), custom_call_target="tpu_custom_call" | custom-call | tf_op jit(solution)/shard_map/pallas_call | solution.py:191
  5.0 86.3 %all_to_all.10.rows_ref = bf16[32,97,8,128]{3,2,1,0:T(8,128)(2,1)S(1)} all-to-all(bf16[32,97,8,128]{3,2,1,0:T(8,128)(2,1)} %shard_map.82), channel_id=1, replica_groups=mesh['sec'=4,'xy'=32] {'xy'}, dimensions={0} | all-to-all | bytes 12713984 | tf_op jit(solution)/shard_map/all_to_all | solution.py:605
  91.3 0.0 copy-start
  91.3 0.0 copy-start.1
  91.3 0.0 copy-start.2
  91.3 0.0 copy-start.3
  91.3 0.5 shard_map.84
  91.8 4.1 %collective-permute-start = (bf16[64,4096]{1,0:T(8,128)(2,1)S(1)}, bf16[64,4096]{1,0:T(8,128)(2,1)S(1)}, u32[]{:S(2)}, u32[]{:S(2)}) collective-permute-start(bf16[64,4096]{1,0:T(8,128)(2,1)S(1)} %shard_map.84), channel_id=1, source_target_pairs={{32,0},{64,32},{96,64},{33,1},{65,33},{97,65},{34,2},{66,34},{98,6... | collective-permute-start | bytes 1572872 | tf_op jit(solution)/shard_map/ppermute | solution.py:608
  95.9 0.0 copy-done
  95.9 0.0 copy-done.1
  95.9 0.0 copy-done.2
  95.9 0.0 copy-done.3
  96.0 6.0 %shard_map.83 = (f32[8,256,128]{2,1,0:T(8,128)S(1)}, f32[8,256]{1,0:T(8,128)S(1)}, f32[8,128]{1,0:T(8,128)S(1)}, f32[8,128]{1,0:T(8,128)S(1)}) custom-call(bf16[32,97,8,128]{3,2,1,0:T(8,128)(2,1)S(1)} %all_to_all.10.rows_ref, bf16[512,256]{1,0:T(8,128)(2,1)S(1)} %copy-done.3, bf16[512,256]{1,0:T(8,128)(2,1)S(1)} %copy-done.2, ...), custom_call_target="tpu_custom_call" | custom-call | flops 5905580032 | bytes 12582912 | tf_op jit(solution)/shard_map/pallas_call | solution.py:422
  101.9 1.1 collective-permute-done.next_ref
  103.0 2.2 %shard_map.85 = f32[128,4,128]{2,1,0:T(4,128)S(1)} custom-call(f32[8,256,128]{2,1,0:T(8,128)S(1)} %get-tuple-element.9.last_ref, f32[8,256]{1,0:T(8,128)S(1)} %get-tuple-element.10.square_ref, f32[8,128]{1,0:T(8,128)S(1)} %get-tuple-element.11.early_ref, f32[8,128]{1,0:T(8,128)S(1)} %get-tuple-element.12.third_sums_ref, ...), custom_call_target="tpu_custom_call" | custom-call | flops 4294967296 | bytes 8388608 | tf_op jit(solution)/shard_map/pallas_call | solution.py:531
  105.3 14.7 %all_to_all.11.arrived_ref = f32[128,4,128]{2,1,0:T(4,128)S(1)} all-to-all(f32[128,4,128]{2,1,0:T(4,128)S(1)} %shard_map.85), channel_id=1, replica_groups=mesh['sec'=4,'xy'=32] {'sec','xy'}, dimensions={0} | all-to-all | bytes 524288 | tf_op jit(solution)/shard_map/all_to_all | solution.py:611
  119.9 1.5 %shard_map.86 = f32[2,2,8,15]{3,2,1,0:T(8,128)} custom-call(f32[128,4,128]{2,1,0:T(4,128)S(1)} %all_to_all.11.arrived_ref), custom_call_target="tpu_custom_call" | custom-call | tf_op jit(solution)/shard_map/pallas_call | solution.py:593
Async XLA Ops:
  91.3 4.7 %copy-start = (bf16[512,256]{1,0:T(8,128)(2,1)S(1)}, bf16[512,256]{1,0:T(8,128)(2,1)}, u32[]{:S(2)}) copy-start(bf16[512,256]{1,0:T(8,128)(2,1)} %constant.11.clone.fourth_ref) | copy-start | bytes 786436
  91.3 4.7 %copy-start.1 = (bf16[512,256]{1,0:T(8,128)(2,1)S(1)}, bf16[512,256]{1,0:T(8,128)(2,1)}, u32[]{:S(2)}) copy-start(bf16[512,256]{1,0:T(8,128)(2,1)} %constant.10.clone.third_ref) | copy-start | bytes 786436
  91.3 4.7 %copy-start.2 = (bf16[512,256]{1,0:T(8,128)(2,1)S(1)}, bf16[512,256]{1,0:T(8,128)(2,1)}, u32[]{:S(2)}) copy-start(bf16[512,256]{1,0:T(8,128)(2,1)} %constant.9.clone.second_ref) | copy-start | bytes 786436
  91.3 4.7 %copy-start.3 = (bf16[512,256]{1,0:T(8,128)(2,1)S(1)}, bf16[512,256]{1,0:T(8,128)(2,1)}, u32[]{:S(2)}) copy-start(bf16[512,256]{1,0:T(8,128)(2,1)} %constant.8.clone.first_ref) | copy-start | bytes 786436
  91.8 11.3 %collective-permute-start = (bf16[64,4096]{1,0:T(8,128)(2,1)S(1)}, bf16[64,4096]{1,0:T(8,128)(2,1)S(1)}, u32[]{:S(2)}, u32[]{:S(2)}) collective-permute-start(bf16[64,4096]{1,0:T(8,128)(2,1)S(1)} %shard_map.84), channel_id=1, source_target_pairs={{32,0},{64,32},{96,64},{33,1},{65,33},{97,65},{34,2},{66,34},{98,6... | collective-permute-start | bytes 1572872 | tf_op jit(solution)/shard_map/ppermute | solution.py:608

commit v9 on v8

--- a/solution.py
+++ b/solution.py
@@ -569,18 +569,22 @@
             )
             flow[o] = value * mask[o]
             mesh[o] = jnp.where(mask[o] > 0.0, value, 0.0)
+        def swap(value):
+            return jnp.where(top, pltpu.roll(value, 128 - GYW, 1), pltpu.roll(value, GYW, 1))
+
+        other, other_flow = ({o: swap(v) for o, v in part.items()} for part in (mesh, flow))
         for step in range(ITERS):
             reach = (ITERS - step) // 2
-            up = {o: pltpu.roll(mesh[o], 128 - GYW, 1) for o in mesh}
-            down = {o: pltpu.roll(mesh[o], GYW, 1) for o in mesh}
-            new = {}
+            new, new_other = {}, {}
             for o in range(-reach, reach + 1):
-                near = jnp.where(
-                    top, up[o] + up.get(o - 1, zero), down[o] + down.get(o + 1, zero)
-                )
-                near = near + pltpu.roll(mesh[o], 1, 1) + pltpu.roll(mesh[o], 127, 1)
-                new[o] = flow[o] + mask[o] * near
-            mesh = new
+                near = other[o] + jnp.where(top, other.get(o - 1, zero), other.get(o + 1, zero))
+                sides = pltpu.roll(mesh[o], 1, 1) + pltpu.roll(mesh[o], 127, 1)
+                new[o] = flow[o] + mask[o] * (near + sides)
+                if step < ITERS - 1:
+                    near = mesh[o] + jnp.where(top, mesh.get(o + 1, zero), mesh.get(o - 1, zero))
+                    sides = pltpu.roll(other[o], 1, 1) + pltpu.roll(other[o], 127, 1)
+                    new_other[o] = other_flow[o] + mask[o] * (near + sides)
+            mesh, other = new, new_other
         result.append(mesh[0])
     turned = jnp.concatenate(result + [jnp.zeros((112, 128), F32)], axis=0).T
     for c in range(2):

time: 122 us -> 122 us (level)
  no operation moved by 1% of the time
where the time goes in v9:
time: 122 us; the launch traced here: 121 us
  blocking collectives  101 us (83%)
  Pallas kernels  15.1 us (12%)
  starting transfers between devices  4.11 us (3%)
    all_to_all x1, blocking collectives, local(): lax.all_to_all(outgoing, 'xy', split_axis=0, concat_axis=0, tiled=True)  86.3 us
    all_to_all x1, blocking collectives, local(): lax.all_to_all(windows, ('sec', 'xy'), split_axis=0, concat_axis=0, tiled...  14.7 us
    pallas_call x1, Pallas kernels, spectrum(): pl.pallas_call(spectrum_kernel, out_shape=[jax.ShapeDtypeStruct((TILES //...  5.96 us
    pallas_call x1, Pallas kernels, send_rows(): pl.pallas_call(send_kernel, out_shape=jax.ShapeDtypeStruct((N_XY, TILES_O...  4.96 us
    ppermute x1, starting transfers between devices, local(): following = lax.ppermute(first, 'sec', back)  4.11 us
  transfers between devices with their start and end apart: 1, of which 1 were waited for; matrix products, arithmetic and copies ran while one was open for 0% of the time, Pallas kernels for 5%

profile of v9, /device:TPU:1, one launch (start us, length us, event | category | flops | bytes accessed | tf_op | source)
XLA Modules:
  0.0 121.3 jit_solution(1821109771113752193)
XLA Ops:
  0.0 5.0 %shard_map.82 = bf16[32,97,8,128]{3,2,1,0:T(8,128)(2,1)} custom-call(s32[4,96]{1,0:T(4,128)} %bitcast.2, s32[4,96]{1,0:T(4,128)} %slot_hbm.1, f32[4,96]{1,0:T(4,128)} %blend_hbm.1, bf16[4,96,4096]{2,1,0:T(8,128)(2,1)} %raw_hbm.1), custom_call_target="tpu_custom_call" | custom-call | tf_op jit(solution)/shard_map/pallas_call | solution.py:191
  5.0 86.3 %all_to_all.10.rows_ref = bf16[32,97,8,128]{3,2,1,0:T(8,128)(2,1)S(1)} all-to-all(bf16[32,97,8,128]{3,2,1,0:T(8,128)(2,1)} %shard_map.82), channel_id=1, replica_groups=mesh['sec'=4,'xy'=32] {'xy'}, dimensions={0} | all-to-all | bytes 12713984 | tf_op jit(solution)/shard_map/all_to_all | solution.py:609
  91.3 0.0 copy-start
  91.3 0.0 copy-start.1
  91.3 0.0 copy-start.2
  91.3 0.0 copy-start.3
  91.3 0.5 shard_map.84
  91.8 4.1 %collective-permute-start = (bf16[64,4096]{1,0:T(8,128)(2,1)S(1)}, bf16[64,4096]{1,0:T(8,128)(2,1)S(1)}, u32[]{:S(2)}, u32[]{:S(2)}) collective-permute-start(bf16[64,4096]{1,0:T(8,128)(2,1)S(1)} %shard_map.84), channel_id=1, source_target_pairs={{32,0},{64,32},{96,64},{33,1},{65,33},{97,65},{34,2},{66,34},{98,6... | collective-permute-start | bytes 1572872 | tf_op jit(solution)/shard_map/ppermute | solution.py:612
  95.9 0.0 copy-done
  95.9 0.0 copy-done.1
  95.9 0.0 copy-done.2
  95.9 0.0 copy-done.3
  96.0 6.0 %shard_map.83 = (f32[8,256,128]{2,1,0:T(8,128)S(1)}, f32[8,256]{1,0:T(8,128)S(1)}, f32[8,128]{1,0:T(8,128)S(1)}, f32[8,128]{1,0:T(8,128)S(1)}) custom-call(bf16[32,97,8,128]{3,2,1,0:T(8,128)(2,1)S(1)} %all_to_all.10.rows_ref, bf16[512,256]{1,0:T(8,128)(2,1)S(1)} %copy-done.3, bf16[512,256]{1,0:T(8,128)(2,1)S(1)} %copy-done.2, ...), custom_call_target="tpu_custom_call" | custom-call | flops 5905580032 | bytes 12582912 | tf_op jit(solution)/shard_map/pallas_call | solution.py:422
  101.9 1.1 collective-permute-done.next_ref
  103.0 2.2 %shard_map.85 = f32[128,4,128]{2,1,0:T(4,128)S(1)} custom-call(f32[8,256,128]{2,1,0:T(8,128)S(1)} %get-tuple-element.9.last_ref, f32[8,256]{1,0:T(8,128)S(1)} %get-tuple-element.10.square_ref, f32[8,128]{1,0:T(8,128)S(1)} %get-tuple-element.11.early_ref, f32[8,128]{1,0:T(8,128)S(1)} %get-tuple-element.12.third_sums_ref, ...), custom_call_target="tpu_custom_call" | custom-call | flops 4294967296 | bytes 8388608 | tf_op jit(solution)/shard_map/pallas_call | solution.py:531
  105.3 14.7 %all_to_all.11.arrived_ref = f32[128,4,128]{2,1,0:T(4,128)S(1)} all-to-all(f32[128,4,128]{2,1,0:T(4,128)S(1)} %shard_map.85), channel_id=1, replica_groups=mesh['sec'=4,'xy'=32] {'sec','xy'}, dimensions={0} | all-to-all | bytes 524288 | tf_op jit(solution)/shard_map/all_to_all | solution.py:615
  119.9 1.4 %shard_map.86 = f32[2,2,8,15]{3,2,1,0:T(8,128)} custom-call(f32[128,4,128]{2,1,0:T(4,128)S(1)} %all_to_all.11.arrived_ref), custom_call_target="tpu_custom_call" | custom-call | tf_op jit(solution)/shard_map/pallas_call | solution.py:597
Async XLA Ops:
  91.3 4.7 %copy-start = (bf16[512,256]{1,0:T(8,128)(2,1)S(1)}, bf16[512,256]{1,0:T(8,128)(2,1)}, u32[]{:S(2)}) copy-start(bf16[512,256]{1,0:T(8,128)(2,1)} %constant.11.clone.fourth_ref) | copy-start | bytes 786436
  91.3 4.7 %copy-start.1 = (bf16[512,256]{1,0:T(8,128)(2,1)S(1)}, bf16[512,256]{1,0:T(8,128)(2,1)}, u32[]{:S(2)}) copy-start(bf16[512,256]{1,0:T(8,128)(2,1)} %constant.10.clone.third_ref) | copy-start | bytes 786436
  91.3 4.7 %copy-start.2 = (bf16[512,256]{1,0:T(8,128)(2,1)S(1)}, bf16[512,256]{1,0:T(8,128)(2,1)}, u32[]{:S(2)}) copy-start(bf16[512,256]{1,0:T(8,128)(2,1)} %constant.9.clone.second_ref) | copy-start | bytes 786436
  91.3 4.7 %copy-start.3 = (bf16[512,256]{1,0:T(8,128)(2,1)S(1)}, bf16[512,256]{1,0:T(8,128)(2,1)}, u32[]{:S(2)}) copy-start(bf16[512,256]{1,0:T(8,128)(2,1)} %constant.8.clone.first_ref) | copy-start | bytes 786436
  91.8 11.3 %collective-permute-start = (bf16[64,4096]{1,0:T(8,128)(2,1)S(1)}, bf16[64,4096]{1,0:T(8,128)(2,1)S(1)}, u32[]{:S(2)}, u32[]{:S(2)}) collective-permute-start(bf16[64,4096]{1,0:T(8,128)(2,1)S(1)} %shard_map.84), channel_id=1, source_target_pairs={{32,0},{64,32},{96,64},{33,1},{65,33},{97,65},{34,2},{66,34},{98,6... | collective-permute-start | bytes 1572872 | tf_op jit(solution)/shard_map/ppermute | solution.py:612

commit v10 on v9

--- a/solution.py
+++ b/solution.py
@@ -310,30 +310,31 @@
 
 def flow_sums(operands, third_ref, fourth_ref, high_ref, twice_ref, sums_ref):
     lanes = 128
-    total = jnp.zeros((8, 2 * lanes), F32)
-    along_x = jnp.zeros((8, 2 * lanes), F32)
-    along_y = jnp.zeros((8, 2 * lanes), F32)
-    for q in range(0, TILES, 2):
+    total = jnp.zeros((8, 4 * lanes), F32)
+    along_x = jnp.zeros((8, 4 * lanes), F32)
+    along_y = jnp.zeros((8, 4 * lanes), F32)
+    for q in range(0, TILES, 4):
         rows = jnp.concatenate(
-            [cross_rows(*operands(q + i), 0 if q + i else lanes) for i in range(2)], axis=1
+            [cross_rows(*operands(q + i), 0 if q + i else lanes) for i in range(4)], axis=1
         )
         high = rows.astype(BF16)
         twice = 2.0 * rows - high.astype(F32)
         total = total + sublane_sum(rows * rows)
         along_x = along_x + sublane_sum(twice * weighed(third_ref, high))
-        for i in range(2):
+        for i in range(4):
             high_ref[q + i] = high[:, i * lanes : (i + 1) * lanes]
             twice_ref[q + i] = twice[:, i * lanes : (i + 1) * lanes]
-    for g in range(0, TILES, 2):
+    for g in range(0, TILES, 4):
         high, twice = (
             jnp.concatenate(
-                [ref[:, 16 * (g + i) : 16 * (g + i) + 16, :].reshape(256, lanes) for i in range(2)],
+                [ref[:, 16 * (g + i) : 16 * (g + i) + 16, :].reshape(256, lanes) for i in range(4)],
                 axis=1,
             )
             for ref in (high_ref, twice_ref)
         )
         along_y = along_y + sublane_sum(twice * weighed(fourth_ref, high))
     for i, value in enumerate((total, along_x, along_y)):
+        value = value[:, : 2 * lanes] + value[:, 2 * lanes :]
         sums_ref[i : i + 1, :] = down(value[:, :lanes] + value[:, lanes:])
 
 
@@ -390,12 +391,16 @@
 
     square = jnp.zeros((8, PATCHES), F32)
     for q in range(TILES):
-        at = slice(16 * q, 16 * q + 16)
-        own = mm3(
-            second_ref[...],
-            high[:, at, :].reshape(256, PATCHES),
-            low[:, at, :].reshape(256, PATCHES),
-        )
+        if q % 2 == 0:
+            pairs = [
+                jnp.concatenate(
+                    [ref[:, 16 * i : 16 * i + 16, :].reshape(256, PATCHES) for i in (q, q + 1)],
+                    axis=1,
+                )
+                for ref in (high, low)
+            ]
+            both_q = mm3(second_ref[...], *pairs)
+        own = both_q[:, (q % 2) * PATCHES : (q % 2 + 1) * PATCHES]
         if q == 0:
             own = jnp.where(lax.broadcasted_iota(jnp.int32, (256, 1), 0) == 0, 0.0, own)
         square = square + sublane_sum(own * own)

time: 122 us -> 122 us (level)
  no operation moved by 1% of the time
where the time goes in v10:
time: 122 us; the launch traced here: 121 us
  blocking collectives  101 us (83%)
  Pallas kernels  15.1 us (12%)
  starting transfers between devices  4.11 us (3%)
    all_to_all x1, blocking collectives, local(): lax.all_to_all(outgoing, 'xy', split_axis=0, concat_axis=0, tiled=True)  86.3 us
    all_to_all x1, blocking collectives, local(): lax.all_to_all(windows, ('sec', 'xy'), split_axis=0, concat_axis=0, tiled...  14.7 us
    pallas_call x1, Pallas kernels, spectrum(): pl.pallas_call(spectrum_kernel, out_shape=[jax.ShapeDtypeStruct((TILES //...  5.96 us
    pallas_call x1, Pallas kernels, send_rows(): pl.pallas_call(send_kernel, out_shape=jax.ShapeDtypeStruct((N_XY, TILES_O...  4.96 us
    ppermute x1, starting transfers between devices, local(): following = lax.ppermute(first, 'sec', back)  4.11 us
  transfers between devices with their start and end apart: 1, of which 1 were waited for; matrix products, arithmetic and copies ran while one was open for 0% of the time, Pallas kernels for 5%

profile of v10, /device:TPU:1, one launch (start us, length us, event | category | flops | bytes accessed | tf_op | source)
XLA Modules:
  0.0 121.3 jit_solution(5250836608929387113)
XLA Ops:
  0.0 5.0 %shard_map.82 = bf16[32,97,8,128]{3,2,1,0:T(8,128)(2,1)} custom-call(s32[4,96]{1,0:T(4,128)} %bitcast.2, s32[4,96]{1,0:T(4,128)} %slot_hbm.1, f32[4,96]{1,0:T(4,128)} %blend_hbm.1, bf16[4,96,4096]{2,1,0:T(8,128)(2,1)} %raw_hbm.1), custom_call_target="tpu_custom_call" | custom-call | tf_op jit(solution)/shard_map/pallas_call | solution.py:191
  5.0 86.3 %all_to_all.10.rows_ref = bf16[32,97,8,128]{3,2,1,0:T(8,128)(2,1)S(1)} all-to-all(bf16[32,97,8,128]{3,2,1,0:T(8,128)(2,1)} %shard_map.82), channel_id=1, replica_groups=mesh['sec'=4,'xy'=32] {'xy'}, dimensions={0} | all-to-all | bytes 12713984 | tf_op jit(solution)/shard_map/all_to_all | solution.py:614
  91.3 0.0 copy-start
  91.3 0.0 copy-start.1
  91.3 0.0 copy-start.2
  91.3 0.0 copy-start.3
  91.3 0.5 shard_map.84
  91.8 4.1 %collective-permute-start = (bf16[64,4096]{1,0:T(8,128)(2,1)S(1)}, bf16[64,4096]{1,0:T(8,128)(2,1)S(1)}, u32[]{:S(2)}, u32[]{:S(2)}) collective-permute-start(bf16[64,4096]{1,0:T(8,128)(2,1)S(1)} %shard_map.84), channel_id=1, source_target_pairs={{32,0},{64,32},{96,64},{33,1},{65,33},{97,65},{34,2},{66,34},{98,6... | collective-permute-start | bytes 1572872 | tf_op jit(solution)/shard_map/ppermute | solution.py:617
  95.9 0.0 copy-done
  95.9 0.0 copy-done.1
  95.9 0.0 copy-done.2
  95.9 0.0 copy-done.3
  96.0 6.0 %shard_map.83 = (f32[8,256,128]{2,1,0:T(8,128)S(1)}, f32[8,256]{1,0:T(8,128)S(1)}, f32[8,128]{1,0:T(8,128)S(1)}, f32[8,128]{1,0:T(8,128)S(1)}) custom-call(bf16[32,97,8,128]{3,2,1,0:T(8,128)(2,1)S(1)} %all_to_all.10.rows_ref, bf16[512,256]{1,0:T(8,128)(2,1)S(1)} %copy-done.3, bf16[512,256]{1,0:T(8,128)(2,1)S(1)} %copy-done.2, ...), custom_call_target="tpu_custom_call" | custom-call | flops 5905580032 | bytes 12582912 | tf_op jit(solution)/shard_map/pallas_call | solution.py:427
  101.9 1.1 collective-permute-done.next_ref
  103.0 2.2 %shard_map.85 = f32[128,4,128]{2,1,0:T(4,128)S(1)} custom-call(f32[8,256,128]{2,1,0:T(8,128)S(1)} %get-tuple-element.9.last_ref, f32[8,256]{1,0:T(8,128)S(1)} %get-tuple-element.10.square_ref, f32[8,128]{1,0:T(8,128)S(1)} %get-tuple-element.11.early_ref, f32[8,128]{1,0:T(8,128)S(1)} %get-tuple-element.12.third_sums_ref, ...), custom_call_target="tpu_custom_call" | custom-call | flops 4294967296 | bytes 8388608 | tf_op jit(solution)/shard_map/pallas_call | solution.py:536
  105.3 14.7 %all_to_all.11.arrived_ref = f32[128,4,128]{2,1,0:T(4,128)S(1)} all-to-all(f32[128,4,128]{2,1,0:T(4,128)S(1)} %shard_map.85), channel_id=1, replica_groups=mesh['sec'=4,'xy'=32] {'sec','xy'}, dimensions={0} | all-to-all | bytes 524288 | tf_op jit(solution)/shard_map/all_to_all | solution.py:620
  119.9 1.4 %shard_map.86 = f32[2,2,8,15]{3,2,1,0:T(8,128)} custom-call(f32[128,4,128]{2,1,0:T(4,128)S(1)} %all_to_all.11.arrived_ref), custom_call_target="tpu_custom_call" | custom-call | tf_op jit(solution)/shard_map/pallas_call | solution.py:602
Async XLA Ops:
  91.3 4.7 %copy-start = (bf16[512,256]{1,0:T(8,128)(2,1)S(1)}, bf16[512,256]{1,0:T(8,128)(2,1)}, u32[]{:S(2)}) copy-start(bf16[512,256]{1,0:T(8,128)(2,1)} %constant.11.clone.fourth_ref) | copy-start | bytes 786436
  91.3 4.7 %copy-start.1 = (bf16[512,256]{1,0:T(8,128)(2,1)S(1)}, bf16[512,256]{1,0:T(8,128)(2,1)}, u32[]{:S(2)}) copy-start(bf16[512,256]{1,0:T(8,128)(2,1)} %constant.10.clone.third_ref) | copy-start | bytes 786436
  91.3 4.7 %copy-start.2 = (bf16[512,256]{1,0:T(8,128)(2,1)S(1)}, bf16[512,256]{1,0:T(8,128)(2,1)}, u32[]{:S(2)}) copy-start(bf16[512,256]{1,0:T(8,128)(2,1)} %constant.9.clone.second_ref) | copy-start | bytes 786436
  91.3 4.7 %copy-start.3 = (bf16[512,256]{1,0:T(8,128)(2,1)S(1)}, bf16[512,256]{1,0:T(8,128)(2,1)}, u32[]{:S(2)}) copy-start(bf16[512,256]{1,0:T(8,128)(2,1)} %constant.8.clone.first_ref) | copy-start | bytes 786436
  91.8 11.3 %collective-permute-start = (bf16[64,4096]{1,0:T(8,128)(2,1)S(1)}, bf16[64,4096]{1,0:T(8,128)(2,1)S(1)}, u32[]{:S(2)}, u32[]{:S(2)}) collective-permute-start(bf16[64,4096]{1,0:T(8,128)(2,1)S(1)} %shard_map.84), channel_id=1, source_target_pairs={{32,0},{64,32},{96,64},{33,1},{65,33},{97,65},{34,2},{66,34},{98,6... | collective-permute-start | bytes 1572872 | tf_op jit(solution)/shard_map/ppermute | solution.py:617
